TPU v7x, 256 devices: a whole 4x4x8 slice. The times are simulated.
256 devices in a mesh: slab: 128 (over x, z, y), lvl: 2 (over core).
Axes of the slice: x: 4, y: 4, z: 8, core: 2. Of those that a mesh axis runs over, the one named last changes fastest.
Arguments:
- adjoint_final: float32 [2, 256, 19, 16, 256], P('lvl', 'slab'), may hold values from -6 to 6
- populations: bfloat16 [4, 2, 256, 19, 16, 256], P(None, 'lvl', 'slab'), as said below
- relaxation: float32 [2, 256, 16, 256], P('lvl', 'slab'), may hold values from 0.8 to 1.9
- blend: float32 [2, 256, 16, 256], P('lvl', 'slab'), may hold values from 0.1 to 0.9
- solid: int32 [2, 256, 16, 256], P('lvl', 'slab'), may hold values from 0 to 1, as said below
- chain: int32 [2, 256, 2], P('lvl', 'slab'), may hold values from -1 to 255, as said below
- parent: int32 [256, 2], P('slab'), may hold values from -1 to 255, as said below
- children: int32 [256, 8], P('slab'), may hold values from -1 to 255, as said below
Outputs:
- adjoint_initial: float32 [2, 256, 19, 16, 256], P('lvl', 'slab')
Inputs may be any that keep to these rules, and one draw needn't show every extreme that they name: `solid`: fluid cells fill the layers x = 0 and x = 15 of every block. chain[l, g, 1] is g + 1 or -1 and chain[l, g, 0] is g - 1 or -1; chain[l, g, 1] = g + 1 exactly when chain[l, g + 1, 0] = g; chain[l, 0, 0] = chain[l, 255, 1] = -1. parent[f, 0] is -1 (then parent[f, 1] = -1) or a coarse block p with |p // 2 - f // 2| <= 1, and parent[f, 1] its octant 0 to 7; no pair (p, octant) is named twice. For any a and b, at most one fine block f with f // 2 = a has a parent p with p // 2 = b, and for every a some b reaches 1. children[p, o] = f exactly when parent[f] = (p, o); -1 where no fine block names (p, o). Every entry is positive, and the sum over the 19 populations of a cell is positive.
All inputs are finite; a program needn't handle non-finite values.
Results may differ from a plain program's by a relative error of at most 0.0003.
Values sent between devices are 32-bit elements; how exact they have to be, the bound alone decides.
No kernel may reach another device: no remote copies, remote signals or barrier semaphores. Data moves between devices by JAX's collectives and lax.ppermute only.
A program may use at most 64 MiB of HBM per device.

v0:
```python
import functools

import jax
import jax.numpy as jnp
from jax import lax
from jax.experimental import pallas as pl
from jax.experimental.pallas import tpu as pltpu
from jax.sharding import PartitionSpec as P

velocities = [
    (0, 0, 0),
    (1, 0, 0),
    (-1, 0, 0),
    (0, 1, 0),
    (0, -1, 0),
    (0, 0, 1),
    (0, 0, -1),
    (1, 1, 0),
    (-1, -1, 0),
    (1, -1, 0),
    (-1, 1, 0),
    (1, 0, 1),
    (-1, 0, -1),
    (1, 0, -1),
    (-1, 0, 1),
    (0, 1, 1),
    (0, -1, -1),
    (0, 1, -1),
    (0, -1, 1),
]
east_pops = [1, 7, 9, 11, 13]
west_pops = [2, 8, 10, 12, 14]
opposite = [velocities.index((-c[0], -c[1], -c[2])) for c in velocities]
axes = ("slab", "lvl")
pops, edge, plane = 19, 16, 256
f32, bf16 = jnp.float32, jnp.bfloat16

item_row = (0, 0, 56)
mate_d = 40
own_f, far_f, own_d, mate_f, far_d = 40, 48, 96, 104, 112
mate_rows, level_rows = 48, 120
at_level, at_odd, at_prev, at_inner, at_next = 12, 13, 14, 15, 16
table_size = 17


def level_swap(value, slabs):
    pairs = [(2 * s + v, 2 * s + 1 - v) for s in range(slabs) for v in (0, 1)]
    return lax.ppermute(value, axes, pairs)


def mate_swap(value, slabs, cross):
    pairs = [(2 * s + v, 2 * (s ^ 1) + (v ^ cross)) for s in range(slabs) for v in (0, 1)]
    return lax.ppermute(value, axes, pairs)


def far_swap(value, slabs):
    pairs = []
    for s in range(slabs):
        other = s - 1 if s % 2 == 0 else s + 1
        for v in (0, 1):
            if 0 <= other < slabs:
                pairs.append((2 * s + v, 2 * other + v))
            else:
                pairs.append((2 * s + v, 2 * s + 1 - v))
    return lax.ppermute(value, axes, pairs)


def cell_key(index, level, octant):
    y, z = index >> 4, index & 15
    fine = (y >> 1) * 8 + (z >> 1)
    inside = ((y >> 3) == ((octant >> 1) & 1)) & ((z >> 3) == (octant & 1))
    coarse = jnp.where(inside, (y & 7) * 8 + (z & 7), -1)
    return jnp.where(level == 1, fine, coarse)


def select(values, matrix):
    high = values.astype(bf16)
    low = (values - high.astype(f32)).astype(bf16)
    return jnp.dot(high, matrix, preferred_element_type=f32) + jnp.dot(
        low, matrix, preferred_element_type=f32
    )


def ones_where(mask):
    return jnp.where(mask, 1.0, 0.0).astype(bf16)


def iota(shape, dim):
    return lax.broadcasted_iota(jnp.int32, shape, dim)


def pick_matrices(d_ref, j):
    level, octant = d_ref[at_level], d_ref[6 + j]
    source = cell_key(iota((plane, 128), 0), level, octant)
    pick = ones_where(source == (iota((1, 128), 1) & 63))
    target = cell_key(iota((1, plane), 1), 1 - level, octant)
    place = jnp.concatenate(
        [ones_where(source == target[:, :128]), ones_where(source == target[:, 128:])], axis=1
    )
    return pick, place


def plane_scale(d_ref):
    return jnp.where(d_ref[at_level] == 0, 0.125, 1.0)


def pack(d_ref, alpha_ref, w_ref, k_ref, near_ref, lvl_ref, loc_ref, scratch, matrices):
    item_scr, rim_scr, half_scr = scratch
    level = d_ref[at_level]
    odd = d_ref[at_odd]
    near_ref[...] = jnp.zeros_like(near_ref)
    lvl_ref[...] = jnp.zeros_like(lvl_ref)
    item_scr[152:160, :] = jnp.zeros((8, plane), f32)
    rim_scr[...] = jnp.zeros_like(rim_scr)
    loc_ref[...] = jnp.zeros_like(loc_ref)
    for i in range(5):
        e, w = east_pops[i], west_pops[i]
        low = alpha_ref[0, e, 0:1, :] * k_ref[0, 0:1, :]
        high = alpha_ref[1, w, edge - 1 : edge, :] * k_ref[1, edge - 1 : edge, :]
        loc_ref[i : i + 1, :] = jnp.where(odd == 1, low, high)
        loc_ref[8 + i : 9 + i, :] = jnp.where(odd == 1, high, low)
    for j in range(3):
        base = item_row[j]
        out_ref = near_ref if j == 0 else lvl_ref

        @pl.when(d_ref[j] == 1)
        def _(j=j, base=base, out_ref=out_ref):
            g, octant, other = d_ref[3 + j], d_ref[6 + j], d_ref[9 + j]
            ox = octant >> 2
            pick, place = matrices(j)

            @pl.when(level == 0)
            def _():
                rows = pl.ds(pl.multiple_of(ox * 8, 8), 8)
                part = alpha_ref[g, :, rows, :] * w_ref[g, rows, :][None]
                item_scr[0:152, :] = part.reshape(152, plane)

            @pl.when(level == 1)
            def _():
                part = (alpha_ref[g] * w_ref[g][None]).reshape(304, plane)
                for n in range(2):
                    lanes = slice(128 * n, 128 * n + 128)
                    half_scr[n, 0:304, :] = part[:, lanes]
                    item_scr[0:152, lanes] = (
                        half_scr[n, pl.ds(0, 152, stride=2), :]
                        + half_scr[n, pl.ds(1, 152, stride=2), :]
                    )

            picked = select(item_scr[...], pick)
            left = iota((40, 128), 1) < 64
            out_ref[base : base + 40, 0:128] = jnp.where(left, picked[0:40], picked[40:80])
            out_ref[base : base + 40, 128:256] = jnp.where(left, picked[80:120], picked[120:160])

            @pl.when((level == 0) | (ox == other))
            def _():
                for i in range(5):
                    e, w = east_pops[i] * 8, west_pops[i] * 8 + 7
                    rim_scr[i : i + 1, :] = jnp.where(
                        other == 1, item_scr[w : w + 1, :], item_scr[e : e + 1, :]
                    )
                spread = select(rim_scr[...], place) * plane_scale(d_ref)
                towards_d = other != odd
                if j == 0:

                    @pl.when(towards_d)
                    def _():
                        near_ref[mate_d : mate_d + 8, :] = spread

                    @pl.when(jnp.logical_not(towards_d))
                    def _():
                        lvl_ref[mate_f : mate_f + 8, :] = spread

                else:
                    if j == 1:
                        row = jnp.where(towards_d, far_d, far_f)
                    else:
                        row = jnp.where(towards_d, own_d, own_f)
                    lvl_ref[pl.ds(pl.multiple_of(row, 8), 8), :] = spread


def describe(slab, level, chain_ref, parent_ref, children_ref, d_ref):
    odd = slab & 1
    for n in range(at_level):
        d_ref[n] = 0

    def note(valid, offset, g, octant, other):
        slot = jnp.where(offset == 0, 2, jnp.where(offset == 1 - 2 * odd, 0, 1))

        @pl.when(valid)
        def _():
            d_ref[slot] = 1
            d_ref[3 + slot] = g
            d_ref[6 + slot] = octant
            d_ref[9 + slot] = other & 1

    @pl.when(level == 0)
    def _():
        for g in range(2):
            for octant in range(8):
                fine = children_ref[g, octant]
                note(fine >= 0, (fine >> 1) - slab, g, octant, fine)

    @pl.when(level == 1)
    def _():
        for g in range(2):
            coarse = parent_ref[g, 0]
            note(coarse >= 0, (coarse >> 1) - slab, g, parent_ref[g, 1], coarse)

    def flag(entry):
        return jnp.where(entry >= 0, 1, 0)

    d_ref[at_level] = level
    d_ref[at_odd] = odd
    d_ref[at_prev] = flag(chain_ref[0, 0])
    d_ref[at_inner] = flag(chain_ref[0, 1])
    d_ref[at_next] = flag(chain_ref[1, 1])


def first_pack_kernel(*refs):
    tables_in, (alpha_in, w_in) = refs[:3], refs[3:5]
    d_ref, near_ref, lvl_ref, loc_ref, k_ref, alpha_ref, w_ref = refs[5:12]
    scratch, tables, sems = refs[12:15], refs[15:18], refs[18]
    small = [pltpu.make_async_copy(tables_in[n], tables[n], sems.at[n]) for n in range(3)]
    large = [
        pltpu.make_async_copy(w_in, w_ref, sems.at[3]),
        pltpu.make_async_copy(alpha_in, alpha_ref, sems.at[4]),
    ]
    for copy in small + large:
        copy.start()
    for copy in small:
        copy.wait()
    level = lax.axis_index("lvl")
    describe(lax.axis_index("slab"), level, *tables, d_ref)
    x = iota((edge, plane), 0)
    cell = iota((edge, plane), 1)
    covers = []
    for g in range(2):
        covered = jnp.zeros((edge, plane), jnp.bool_)
        for j in range(3):
            octant = d_ref[6 + j]
            inside = (
                ((x >> 3) == (octant >> 2))
                & ((cell >> 7) == ((octant >> 1) & 1))
                & (((cell >> 3) & 1) == (octant & 1))
            ) | (level == 1)
            covered = covered | (inside & (d_ref[j] == 1) & (d_ref[3 + j] == g))
        covers.append(covered)
    for copy in large:
        copy.wait()
    for g in range(2):
        k_ref[g] = jnp.where(covers[g], 1.0 - w_ref[g], 1.0)
    matrices = functools.partial(pick_matrices, d_ref)
    pack(d_ref, alpha_ref, w_ref, k_ref, near_ref, lvl_ref, loc_ref, scratch, matrices)


def moved_cells(values, c, z):
    if c[1] == 0 and c[2] == 0:
        return values
    base = -16 * c[1]
    axis = values.ndim - 1
    if c[2] == 0:
        return pltpu.roll(values, base % plane, axis)
    inner = pltpu.roll(values, (base - c[2]) % plane, axis)
    around = pltpu.roll(values, (base + 15 * c[2]) % plane, axis)
    return jnp.where(z == (15 if c[2] == 1 else 0), around, inner)


def fields_kernel(*refs):
    d_ref, pop_ref, relax_ref, solid_ref = refs[:4]
    u_ref, keep_ref, gain_ref, bits_ref, pick_ref, place_ref, pad_scr = refs[4:]
    for j in range(3):
        pick_ref[j], place_ref[j] = pick_matrices(d_ref, j)
    z = iota((edge, plane), 1) & 15
    for g in range(2):
        solid = solid_ref[g] > 0
        omega = relax_ref[g]
        keep_ref[g] = jnp.where(solid, 0.0, 1.0 - omega)
        gain_ref[g] = jnp.where(solid, 0.0, omega)
        pad_scr[0:8, :] = jnp.zeros((8, plane), f32)
        pad_scr[24:32, :] = jnp.zeros((8, plane), f32)
        pad_scr[8:24, :] = jnp.where(solid, 1.0, 0.0)
        bits = jnp.zeros((edge, plane), jnp.int32)
        for i in range(pops):
            c = velocities[i]
            blocked = moved_cells(pad_scr[8 + c[0] : 24 + c[0], :], c, z) > 0.5
            bits = bits | jnp.where(blocked, 1 << i, 0)
        bits_ref[g] = bits
    steps = pop_ref.shape[0]
    for t in range(steps):
        for g in range(2):
            total = jnp.zeros((edge, plane), f32)
            flow = [jnp.zeros((edge, plane), f32) for _ in range(3)]
            for i in range(pops):
                f = pop_ref[t, g, i].astype(f32)
                total = total + f
                for a in range(3):
                    if velocities[i][a] == 1:
                        flow[a] = flow[a] + f
                    elif velocities[i][a] == -1:
                        flow[a] = flow[a] - f
            for a in range(3):
                u_ref[t, g, a] = flow[a] / total


def collide(pulled, u, keep, gain):
    g = pulled
    plus = {i: g[i] + g[i + 1] for i in range(1, pops, 2)}
    minus = {i: g[i] - g[i + 1] for i in range(1, pops, 2)}
    xy, xz, yz = plus[7] + plus[9], plus[11] + plus[13], plus[15] + plus[17]
    px, py, pz = 2.0 * plus[1], 2.0 * plus[3], 2.0 * plus[5]
    weight = 12.0 * g[0] + (px + py + pz) + (xy + xz + yz)
    qxx, qyy, qzz = px + xy + xz, py + xy + yz, pz + xz + yz
    qxy, qxz, qyz = plus[7] - plus[9], plus[11] - plus[13], plus[15] - plus[17]
    jx = 2.0 * minus[1] + (minus[7] + minus[9]) + (minus[11] + minus[13])
    jy = 2.0 * minus[3] + (minus[7] - minus[9]) + (minus[15] + minus[17])
    jz = 2.0 * minus[5] + (minus[11] - minus[13]) + (minus[15] - minus[17])
    ux, uy, uz = u
    qux = qxx * ux + qxy * uy + qxz * uz
    quy = qxy * ux + qyy * uy + qyz * uz
    quz = qxz * ux + qyz * uy + qzz * uz
    speed = ux * ux + uy * uy + uz * uz
    along = ux * qux + uy * quy + uz * quz
    scale = gain * (1.0 / 36.0)
    rest = scale * (weight * (1.0 + 1.5 * speed) - 4.5 * along)
    scale = gain * (1.0 / 12.0)
    mx = scale * (jx + 3.0 * qux - ux * weight)
    my = scale * (jy + 3.0 * quy - uy * weight)
    mz = scale * (jz + 3.0 * quz - uz * weight)
    out = [None] * pops
    out[0] = keep * g[0] + rest
    pairs = [mx, my, mz, mx + my, mx - my, mx + mz, mx - mz, my + mz, my - mz]
    for n, i in enumerate(range(1, pops, 2)):
        out[i] = keep * g[i] + (rest + pairs[n])
        out[i + 1] = keep * g[i + 1] + (rest - pairs[n])
    return out


def step_kernel(*refs, first, last):
    (d_ref, alpha_ref, k_ref, u_ref, keep_ref, gain_ref, bits_ref) = refs[:7]
    (mate_ref, lvl_ref, far_ref) = refs[7:10]
    refs = refs[10:]
    if not first:
        added_ref, refs = refs[0], refs[1:]
    if not last:
        (w_ref, pick_ref, place_ref), refs = refs[:3], refs[3:]
        out_ref, near_out, lvl_out, loc_out, beta_scr, item_scr, rim_scr, half_scr = refs
    else:
        out_ref, beta_scr, half_scr = refs
    level = d_ref[at_level]
    odd = d_ref[at_odd]
    for g in range(2):
        beta_scr[g, :, 8:24, :] = alpha_ref[g] * k_ref[g][None]
    if not first:
        for is_odd, (g, x) in enumerate(late_layer):

            @pl.when(odd == is_odd)
            def _(g=g, x=x):
                kept = k_ref[g, x : x + 1, :]
                for i in range(pops):
                    beta_scr[g, i, 8 + x : 9 + x, :] += added_ref[i : i + 1, :] * kept

    sources = (mate_ref, far_ref, lvl_ref)
    for j in range(3):
        first = item_row[j]

        @pl.when(d_ref[j] == 1)
        def _(j=j, first=first):
            g, octant = d_ref[3 + j], d_ref[6 + j]
            left = iota((40, 128), 1) < 64
            a = sources[j][first : first + 40, 0:128]
            b = sources[j][first : first + 40, 128:256]
            stacked = jnp.concatenate(
                [
                    jnp.where(left, a, 0.0),
                    jnp.where(left, 0.0, a),
                    jnp.where(left, b, 0.0),
                    jnp.where(left, 0.0, b),
                ],
                axis=0,
            )
            target = cell_key(iota((1, plane), 1), level, octant)
            spread = select(stacked, ones_where((iota((128, plane), 0) & 63) == target))

            @pl.when(level == 0)
            def _():
                rows = pl.ds(pl.multiple_of(8 + (octant >> 2) * 8, 8), 8)
                beta_scr[g, :, rows, :] += spread[0:152].reshape(pops, 8, plane)

            @pl.when(level == 1)
            def _():
                for n in range(2):
                    lanes = slice(128 * n, 128 * n + 128)
                    half = spread[:, lanes] * 0.125
                    half_scr[n, pl.ds(0, 160, stride=2), :] = half
                    half_scr[n, pl.ds(1, 160, stride=2), :] = half
                    both = half_scr[n, 0:304, :].reshape(pops, edge, 128)
                    beta_scr[g, :, 8:24, lanes] += both

    from_d = lvl_ref[mate_f : mate_f + 8, :]
    from_f = far_ref[own_f : own_f + 8, :] + lvl_ref[far_d : far_d + 8, :]
    above = jnp.where(odd == 1, from_f, from_d)
    below = jnp.where(odd == 1, from_d, from_f)
    above = jnp.where(d_ref[at_next] == 1, above, 0.0)
    below = jnp.where(d_ref[at_prev] == 1, below, 0.0)
    inner = d_ref[at_inner] == 1
    for i in range(5):
        e, w = east_pops[i], west_pops[i]
        beta_scr[1, e, 24:25, :] = above[i : i + 1]
        beta_scr[0, w, 7:8, :] = below[i : i + 1]
        beta_scr[0, e, 24:25, :] = jnp.where(inner, beta_scr[1, e, 8:9, :], 0.0)
        beta_scr[1, w, 7:8, :] = jnp.where(inner, beta_scr[0, w, 23:24, :], 0.0)
    z = iota((8, plane), 1) & 15
    for g in range(2):
        for h in range(2):
            rows = slice(8 * h, 8 * h + 8)
            first = 8 + 8 * h
            bits = bits_ref[g, rows, :]
            pulled = []
            for i in range(pops):
                c = velocities[i]
                v = beta_scr[g, i, first + c[0] : first + c[0] + 8, :]
                v = moved_cells(v, c, z)
                back = beta_scr[g, opposite[i], first : first + 8, :]
                pulled.append(jnp.where((bits & (1 << i)) != 0, back, v))
            u = [u_ref[g, a, rows, :] for a in range(3)]
            done = collide(pulled, u, keep_ref[g, rows, :], gain_ref[g, rows, :])
            for i in range(pops):
                out_ref[g, i, rows, :] = done[i]
    if not last:
        scratch = (item_scr, rim_scr, half_scr)
        matrices = lambda j: (pick_ref[j], place_ref[j])
        pack(d_ref, out_ref, w_ref, k_ref, near_out, lvl_out, loc_out, scratch, matrices)


late_layer = ((1, edge - 1), (0, 0))


def late_values(is_odd, late_ref, u_ref, keep_ref, gain_ref):
    g, x = late_layer[is_odd]
    z = iota((8, plane), 1) & 15
    late = late_ref[...]
    pulled = [0.0] * pops
    for n, i in enumerate((east_pops, west_pops)[is_odd]):
        pulled[i] = moved_cells(late, velocities[i], z)[n : n + 1]
    rows = slice(x, x + 1)
    u = [u_ref[g, a, rows, :] for a in range(3)]
    return collide(pulled, u, keep_ref[g, rows, :], gain_ref[g, rows, :])


def finish_kernel(*refs):
    (d_ref, late_ref, u_ref, keep_ref, gain_ref, w_ref, k_ref, pick_ref, place_ref) = refs[:9]
    (near_in, lvl_in, loc_in, added_ref, near_ref, lvl_ref, loc_ref, rim_scr) = refs[9:]
    level = d_ref[at_level]
    near_ref[...] = near_in[...]
    lvl_ref[...] = lvl_in[...]
    loc_ref[...] = loc_in[...]
    added_ref[...] = jnp.zeros_like(added_ref)
    rim_scr[...] = jnp.zeros_like(rim_scr)

    def side(is_odd):
        g, x = late_layer[is_odd]
        leaving = (west_pops, east_pops)[is_odd]
        values = late_values(is_odd, late_ref, u_ref, keep_ref, gain_ref)
        for i in range(pops):
            added_ref[i : i + 1, :] = values[i]
        kept, weight = k_ref[g, x : x + 1, :], w_ref[g, x : x + 1, :]
        for n, i in enumerate(leaving):
            loc_ref[n : n + 1, :] += values[i] * kept
            rim_scr[n : n + 1, :] = values[i] * weight
        weighted = added_ref[...] * weight
        left = iota((1, 128), 1) < 64
        at_row = iota((8, plane), 0) == (0 if is_odd else 7)
        for j in range(3):
            base = item_row[j]
            out_ref = near_ref if j == 0 else lvl_ref
            octant, other = d_ref[6 + j], d_ref[9 + j]
            ox = octant >> 2
            inside = (level == 1) | (ox == 1 - is_odd)

            @pl.when((d_ref[j] == 1) & (d_ref[3 + j] == g) & inside)
            def _(j=j, base=base, out_ref=out_ref, ox=ox, other=other):
                picked = select(weighted, pick_ref[j])
                for n in range(5):
                    a, b, c, d = (picked[m : m + 1] for m in (n, 5 + n, 10 + n, 15 + n))
                    row = jnp.concatenate([jnp.where(left, a, b), jnp.where(left, c, d)], axis=1)
                    tile = slice(base + 8 * n, base + 8 * n + 8)
                    out_ref[tile, :] += jnp.where(at_row, row, 0.0)

                @pl.when((other == 1 - is_odd) & ((level == 0) | (ox == other)))
                def _():
                    first = (mate_d, far_d, own_d)[j]
                    spread = select(rim_scr[...], place_ref[j]) * plane_scale(d_ref)
                    out_ref[first : first + 8, :] += spread

    @pl.when((d_ref[at_odd] == 0) & (d_ref[at_next] == 1))
    def _():
        side(0)

    @pl.when((d_ref[at_odd] == 1) & (d_ref[at_prev] == 1))
    def _():
        side(1)


def last_kernel(d_ref, alpha_in, late_ref, u_ref, keep_ref, gain_ref, alpha_ref):
    alpha_ref[...] = alpha_in[...]

    def side(is_odd):
        g, x = late_layer[is_odd]
        values = late_values(is_odd, late_ref, u_ref, keep_ref, gain_ref)
        for i in range(pops):
            alpha_ref[g, i, x : x + 1, :] += values[i]

    @pl.when((d_ref[at_odd] == 0) & (d_ref[at_next] == 1))
    def _():
        side(0)

    @pl.when((d_ref[at_odd] == 1) & (d_ref[at_prev] == 1))
    def _():
        side(1)


def smem():
    return pl.BlockSpec(memory_space=pltpu.SMEM)


def vmem():
    return pl.BlockSpec(memory_space=pltpu.VMEM)


def shape(*dims, dtype=f32):
    return jax.ShapeDtypeStruct(dims, dtype)


params = pltpu.CompilerParams(vmem_limit_bytes=24 * 1024 * 1024)
half_scratch = [pltpu.VMEM((2, 320, 128), f32)]
pack_scratch = [pltpu.VMEM((160, plane), f32), pltpu.VMEM((8, plane), f32)] + half_scratch
near_shape = shape(mate_rows, plane)
level_shape = shape(level_rows, plane)
ends_shape = shape(16, plane)
field = shape(2, edge, plane)
state = shape(2, pops, edge, plane)


def hbm():
    return pl.BlockSpec(memory_space=pltpu.HBM)


def cost(flops, bytes_accessed):
    return pl.CostEstimate(flops=flops, bytes_accessed=bytes_accessed, transcendentals=0)


def call(kernel, outs, ins, scratch, name, in_specs=None, out_specs=None, estimate=None):
    with jax.named_scope(name):
        return pl.pallas_call(
            kernel,
            out_shape=outs,
            in_specs=in_specs or [smem()] + [vmem()] * (len(ins) - 1),
            out_specs=out_specs or [vmem()] * len(outs),
            scratch_shapes=scratch,
            compiler_params=params,
            cost_estimate=estimate,
        )(*ins)


def local(
    adjoint_final, populations, relaxation, blend, solid, chain, parent, children, *, slabs
):
    steps = populations.shape[0]
    messages = [near_shape, level_shape, ends_shape]
    table, near, lvl, ends, kept, alpha, weights = call(
        first_pack_kernel,
        [shape(table_size, dtype=jnp.int32)] + messages + [field, state, field],
        (chain[0], parent, children, adjoint_final[0], blend[0]),
        pack_scratch
        + [pltpu.SMEM(v.shape, jnp.int32) for v in (chain[0], parent, children)]
        + [pltpu.SemaphoreType.DMA((5,))],
        "pack_first",
        in_specs=[hbm()] * 5,
        out_specs=[smem()] + [vmem()] * 6,
    )
    flows, keep, gain, bits, pick, place = call(
        fields_kernel,
        [
            shape(steps, 2, 3, edge, plane),
            field,
            field,
            shape(2, edge, plane, dtype=jnp.int32),
            shape(3, plane, 128, dtype=bf16),
            shape(3, plane, plane, dtype=bf16),
        ],
        (table, populations[:, 0], relaxation[0], solid[0]),
        [pltpu.VMEM((32, plane), f32)],
        "flow_fields",
        estimate=cost(4_000_000, 2_000_000),
    )
    added = None
    for t in range(steps - 1, -1, -1):
        first, last = t == steps - 1, t == 0
        u = flows[t]
        with jax.named_scope("exchange"):
            lvl = level_swap(lvl, slabs)
            mate = mate_swap(near, slabs, 1)
            extra = ends[8:16] + mate[mate_d : mate_d + 8]
            far = far_swap(lvl[0:56] + jnp.pad(extra, ((own_f, 8), (0, 0))), slabs)
            late = mate_swap(ends[0:8] + lvl[own_d : own_d + 8] + far[far_f : far_f + 8], slabs, 0)
        ins = [table, alpha, kept, u, keep, gain, bits, mate, lvl, far]
        if not first:
            ins += [added]
        if not last:
            ins += [weights, pick, place]
        got = call(
            functools.partial(step_kernel, first=first, last=last),
            [state] + ([] if last else messages),
            ins,
            [pltpu.VMEM((2, pops, 32, plane), f32)] + (half_scratch if last else pack_scratch),
            "step",
            estimate=cost(8_000_000, 2_000_000),
        )
        alpha = got[0]
        if last:
            alpha = call(
                last_kernel, [state], (table, alpha, late, u, keep, gain), (), "finish"
            )[0]
        else:
            added, near, lvl, ends = call(
                finish_kernel,
                [shape(24, plane)] + messages,
                (table, late, u, keep, gain, weights, kept, pick, place, *got[1:]),
                [pltpu.VMEM((8, plane), f32)],
                "finish",
            )
    return alpha[None]


def solution(mesh):
    return jax.shard_map(
        functools.partial(local, slabs=mesh.shape["slab"]),
        mesh=mesh,
        in_specs=(
            P("lvl", "slab", None, None, None),
            P(None, "lvl", "slab", None, None, None),
            P("lvl", "slab", None, None),
            P("lvl", "slab", None, None),
            P("lvl", "slab", None, None),
            P("lvl", "slab", None),
            P("slab", None),
            P("slab", None),
        ),
        out_specs=P("lvl", "slab", None, None, None),
        check_vma=False,
    )
```

profile of v0, /device:TPU:6, one launch (start us, length us, event | category | flops | bytes accessed | tf_op | source)
XLA Modules:
  0.0 78.0 jit_solution(6110876454328296691)
XLA Ops:
  3.9 2.3 %pack_first.1 = (s32[17]{0:T(128)S(1)}, f32[48,256]{1,0:T(8,128)S(1)}, f32[120,256]{1,0:T(8,128)S(1)}, f32[16,256]{1,0:T(8,128)S(1)}, f32[2,16,256]{2,1,0:T(8,12...) custom-call(s32[2,2]{1,0:T(2,128)S(1)} %bitcast.20, s32[2,2]{1,0:T(2,128)S(1)} %copy-done.6, ...), custom_call_target="tpu_custom_call" | custom-call | tf_op jit(solution)/shard_map/pack_first/pallas_call | solution.py:554
  6.2 1.1 %collective-permute-start = (f32[48,256]{1,0:T(8,128)S(1)}, f32[48,256]{1,0:T(8,128)S(1)}, u32[]{:S(2)}, u32[]{:S(2)}) collective-permute-start(f32[48,256]{1,0:T(8,128)S(1)} %get-tuple-element.49), channel_id=1, source_target_pairs={{0,3},{1,2},{2,1},{3,0},{4,7},{5,6},{6,5},{7,4},{8,11},{9,10},{10,... | collective-permute-start | bytes 147464 | tf_op jit(solution)/shard_map/exchange/ppermute | solution.py:53
  7.5 2.5 %collective-permute-done.refs_7_ = f32[48,256]{1,0:T(8,128)S(1)} collective-permute-done((f32[48,256]{1,0:T(8,128)S(1)}, f32[48,256]{1,0:T(8,128)S(1)}, u32[]{:S(2)}, u32[]{:S(2)}) %collective-permute-start) | collective-permute-done | bytes 49184 | tf_op jit(solution)/shard_map/exchange/ppermute | solution.py:53
  10.0 8.7 %collective-permute-start.2 = (f32[56,256]{1,0:T(8,128)S(1)}, f32[56,256]{1,0:T(8,128)S(1)}, u32[]{:S(2)}, u32[]{:S(2)}) collective-permute-start(f32[56,256]{1,0:T(8,128)S(1)} %slice_add_fusion.3), channel_id=1, source_target_pairs={{0,1},{1,0},{2,4},{3,5},{4,2},{5,3},{6,8},{7,9},{8,6},{9,7},{10,12... | collective-permute-start | bytes 172040 | tf_op jit(solution)/shard_map/exchange/ppermute | solution.py:65
  18.7 1.3 %copy-done = bf16[4,1,2,19,16,256]{5,4,3,2,1,0:T(8,128)(2,1)S(1)} copy-done((bf16[4,1,2,19,16,256]{5,4,3,2,1,0:T(8,128)(2,1)S(1)}, bf16[4,1,2,19,16,256]{5,4,3,2,1,0:T(8,128)(2,1)}, u32[]{:S(2)}) %copy-start) | copy-done | bytes 1245208
  21.5 1.3 %flow_fields.1 = (f32[4,2,3,16,256]{4,3,2,1,0:T(8,128)S(1)}, f32[2,16,256]{2,1,0:T(8,128)S(1)}, f32[2,16,256]{2,1,0:T(8,128)S(1)}, s32[2,16,256]{2,1,0:T(8,128)S...) custom-call(s32[17]{0:T(128)S(1)} %get-tuple-element.42.refs_0_.d_ref, ...), custom_call_target="tpu_custom_call" | custom-call | flops 4000000 | bytes 2000000 | tf_op jit(solution)/shard_map/flow_fields/pallas_call | solution.py:554
  23.0 2.1 %step.4 = (f32[2,19,16,256]{3,2,1,0:T(8,128)S(1)}, f32[48,256]{1,0:T(8,128)S(1)}, f32[120,256]{1,0:T(8,128)S(1)}, f32[16,256]{1,0:T(8,128)S(1)}) custom-call(s32[17]{0:T(128)S(1)} %get-tuple-element.42.refs_0_.d_ref, f32[2,19,16,256]{3,2,1,0:T(8,128)S(1)} %get-tuple-element.43.refs_1_, f32[2,16,256]{2,1,0:T(8,128)S(1)} %get-tuple-element.44.refs_2_.refs_6_, ...), custom_call_target="tpu_custom_call" | custom-call | flops 8000000 | bytes 2000000 | tf_op jit(solution)/shard_map/step/pallas_call | solution.py:554
  25.1 1.5 %collective-permute-done.3.refs_1_ = f32[8,256]{1,0:T(8,128)S(1)} collective-permute-done((f32[8,256]{1,0:T(8,128)S(1)}, f32[8,256]{1,0:T(8,128)S(1)}, u32[]{:S(2)}, u32[]{:S(2)}) %collective-permute-start.3) | collective-permute-done | bytes 8224 | tf_op jit(solution)/shard_map/exchange/ppermute | solution.py:53
  27.7 3.4 %collective-permute-done.4.refs_7_ = f32[48,256]{1,0:T(8,128)S(1)} collective-permute-done((f32[48,256]{1,0:T(8,128)S(1)}, f32[48,256]{1,0:T(8,128)S(1)}, u32[]{:S(2)}, u32[]{:S(2)}) %collective-permute-start.4) | collective-permute-done | bytes 49184 | tf_op jit(solution)/shard_map/exchange/ppermute | solution.py:53
  31.1 4.1 %collective-permute-start.6 = (f32[56,256]{1,0:T(8,128)S(1)}, f32[56,256]{1,0:T(8,128)S(1)}, u32[]{:S(2)}, u32[]{:S(2)}) collective-permute-start(f32[56,256]{1,0:T(8,128)S(1)} %slice_add_fusion.2), channel_id=1, source_target_pairs={{0,1},{1,0},{2,4},{3,5},{4,2},{5,3},{6,8},{7,9},{8,6},{9,7},{10,12... | collective-permute-start | bytes 172040 | tf_op jit(solution)/shard_map/exchange/ppermute | solution.py:65
  35.2 4.4 %collective-permute-done.6.refs_9_ = f32[56,256]{1,0:T(8,128)S(1)} collective-permute-done((f32[56,256]{1,0:T(8,128)S(1)}, f32[56,256]{1,0:T(8,128)S(1)}, u32[]{:S(2)}, u32[]{:S(2)}) %collective-permute-start.6) | collective-permute-done | bytes 57376 | tf_op jit(solution)/shard_map/exchange/ppermute | solution.py:65
  39.6 2.2 %step.5 = (f32[2,19,16,256]{3,2,1,0:T(8,128)S(1)}, f32[48,256]{1,0:T(8,128)S(1)}, f32[120,256]{1,0:T(8,128)S(1)}, f32[16,256]{1,0:T(8,128)S(1)}) custom-call(s32[17]{0:T(128)S(1)} %get-tuple-element.42.refs_0_.d_ref, f32[2,19,16,256]{3,2,1,0:T(8,128)S(1)} %get-tuple-element.55.refs_1_, f32[2,16,256]{2,1,0:T(8,128)S(1)} %get-tuple-element.44.refs_2_.refs_6_, ...), custom_call_target="tpu_custom_call" | custom-call | flops 8000000 | bytes 2000000 | tf_op jit(solution)/shard_map/step/pallas_call | solution.py:554
  41.7 1.5 %collective-permute-done.7.refs_1_ = f32[8,256]{1,0:T(8,128)S(1)} collective-permute-done((f32[8,256]{1,0:T(8,128)S(1)}, f32[8,256]{1,0:T(8,128)S(1)}, u32[]{:S(2)}, u32[]{:S(2)}) %collective-permute-start.7) | collective-permute-done | bytes 8224 | tf_op jit(solution)/shard_map/exchange/ppermute | solution.py:53
  44.3 3.4 %collective-permute-done.8.refs_7_ = f32[48,256]{1,0:T(8,128)S(1)} collective-permute-done((f32[48,256]{1,0:T(8,128)S(1)}, f32[48,256]{1,0:T(8,128)S(1)}, u32[]{:S(2)}, u32[]{:S(2)}) %collective-permute-start.8) | collective-permute-done | bytes 49184 | tf_op jit(solution)/shard_map/exchange/ppermute | solution.py:53
  47.7 3.9 %collective-permute-start.10 = (f32[56,256]{1,0:T(8,128)S(1)}, f32[56,256]{1,0:T(8,128)S(1)}, u32[]{:S(2)}, u32[]{:S(2)}) collective-permute-start(f32[56,256]{1,0:T(8,128)S(1)} %slice_add_fusion.1), channel_id=1, source_target_pairs={{0,1},{1,0},{2,4},{3,5},{4,2},{5,3},{6,8},{7,9},{8,6},{9,7},{10,12... | collective-permute-start | bytes 172040 | tf_op jit(solution)/shard_map/exchange/ppermute | solution.py:65
  51.6 4.5 %collective-permute-done.10.refs_9_ = f32[56,256]{1,0:T(8,128)S(1)} collective-permute-done((f32[56,256]{1,0:T(8,128)S(1)}, f32[56,256]{1,0:T(8,128)S(1)}, u32[]{:S(2)}, u32[]{:S(2)}) %collective-permute-start.10) | collective-permute-done | bytes 57376 | tf_op jit(solution)/shard_map/exchange/ppermute | solution.py:65
  56.2 2.2 %step.6 = (f32[2,19,16,256]{3,2,1,0:T(8,128)S(1)}, f32[48,256]{1,0:T(8,128)S(1)}, f32[120,256]{1,0:T(8,128)S(1)}, f32[16,256]{1,0:T(8,128)S(1)}) custom-call(s32[17]{0:T(128)S(1)} %get-tuple-element.42.refs_0_.d_ref, f32[2,19,16,256]{3,2,1,0:T(8,128)S(1)} %get-tuple-element.63.refs_1_, f32[2,16,256]{2,1,0:T(8,128)S(1)} %get-tuple-element.44.refs_2_.refs_6_, ...), custom_call_target="tpu_custom_call" | custom-call | flops 8000000 | bytes 2000000 | tf_op jit(solution)/shard_map/step/pallas_call | solution.py:554
  58.4 1.5 %collective-permute-done.11.refs_1_ = f32[8,256]{1,0:T(8,128)S(1)} collective-permute-done((f32[8,256]{1,0:T(8,128)S(1)}, f32[8,256]{1,0:T(8,128)S(1)}, u32[]{:S(2)}, u32[]{:S(2)}) %collective-permute-start.11) | collective-permute-done | bytes 8224 | tf_op jit(solution)/shard_map/exchange/ppermute | solution.py:53
  60.9 3.4 %collective-permute-done.12.refs_7_ = f32[48,256]{1,0:T(8,128)S(1)} collective-permute-done((f32[48,256]{1,0:T(8,128)S(1)}, f32[48,256]{1,0:T(8,128)S(1)}, u32[]{:S(2)}, u32[]{:S(2)}) %collective-permute-start.12) | collective-permute-done | bytes 49184 | tf_op jit(solution)/shard_map/exchange/ppermute | solution.py:53
  64.3 3.8 %collective-permute-start.14 = (f32[56,256]{1,0:T(8,128)S(1)}, f32[56,256]{1,0:T(8,128)S(1)}, u32[]{:S(2)}, u32[]{:S(2)}) collective-permute-start(f32[56,256]{1,0:T(8,128)S(1)} %slice_add_fusion), channel_id=1, source_target_pairs={{0,1},{1,0},{2,4},{3,5},{4,2},{5,3},{6,8},{7,9},{8,6},{9,7},{10,12... | collective-permute-start | bytes 172040 | tf_op jit(solution)/shard_map/exchange/ppermute | solution.py:65
  68.1 4.7 %collective-permute-done.14.refs_9_ = f32[56,256]{1,0:T(8,128)S(1)} collective-permute-done((f32[56,256]{1,0:T(8,128)S(1)}, f32[56,256]{1,0:T(8,128)S(1)}, u32[]{:S(2)}, u32[]{:S(2)}) %collective-permute-start.14) | collective-permute-done | bytes 57376 | tf_op jit(solution)/shard_map/exchange/ppermute | solution.py:65
  72.8 1.4 %step.7.alpha_in = f32[2,19,16,256]{3,2,1,0:T(8,128)S(1)} custom-call(s32[17]{0:T(128)S(1)} %get-tuple-element.42.refs_0_.d_ref, f32[2,19,16,256]{3,2,1,0:T(8,128)S(1)} %get-tuple-element.71.refs_1_, f32[2,16,256]{2,1,0:T(8,128)S(1)} %get-tuple-element.44.refs_2_.refs_6_, f32[2,3,16,256]{3,2,1,0:T(8,128)S(1)} %get-tuple-element.79.refs_3_.u_ref, ...), custom_call_target="tpu_custom_call" | custom-call | flops 8000000 | bytes 2000000 | tf_op jit(solution)/shard_map/step/pallas_call | solution.py:554
  74.2 2.2 %collective-permute-done.15.late_ref = f32[8,256]{1,0:T(8,128)S(1)} collective-permute-done((f32[8,256]{1,0:T(8,128)S(1)}, f32[8,256]{1,0:T(8,128)S(1)}, u32[]{:S(2)}, u32[]{:S(2)}) %collective-permute-start.15) | collective-permute-done | bytes 8224 | tf_op jit(solution)/shard_map/exchange/ppermute | solution.py:53
  76.5 1.5 %finish.7 = f32[2,19,16,256]{3,2,1,0:T(8,128)} custom-call(s32[17]{0:T(128)S(1)} %get-tuple-element.42.refs_0_.d_ref, f32[2,19,16,256]{3,2,1,0:T(8,128)S(1)} %step.7.alpha_in, f32[8,256]{1,0:T(8,128)S(1)} %collective-permute-done.15.late_ref, f32[2,3,16,256]{3,2,1,0:T(8,128)S(1)} %get-tuple-element.79.refs_3_.u_ref, ...), custom_call_target="tpu_custom_call" | custom-call | tf_op jit(solution)/shard_map/finish/pallas_call | solution.py:554
  (47 shorter events, 9.0 us)
Async XLA Ops:
  0.0 1.1 %copy-start.1 = (f32[1,2,19,16,256]{4,3,2,1,0:T(8,128)S(1)}, f32[1,2,19,16,256]{4,3,2,1,0:T(8,128)}, u32[]{:S(2)}) copy-start(f32[1,2,19,16,256]{4,3,2,1,0:T(8,128)} %param.8) | copy-start | bytes 1867780
  1.1 0.8 copy-start.2
  1.8 0.7 copy-start.5
  2.5 0.7 copy-start.6
  3.2 0.7 copy-start.7
  6.2 3.8 %collective-permute-start = (f32[48,256]{1,0:T(8,128)S(1)}, f32[48,256]{1,0:T(8,128)S(1)}, u32[]{:S(2)}, u32[]{:S(2)}) collective-permute-start(f32[48,256]{1,0:T(8,128)S(1)} %get-tuple-element.49), channel_id=1, source_target_pairs={{0,3},{1,2},{2,1},{3,0},{4,7},{5,6},{6,5},{7,4},{8,11},{9,10},{10,... | collective-permute-start | bytes 147464 | tf_op jit(solution)/shard_map/exchange/ppermute | solution.py:53
  7.3 2.7 %collective-permute-start.1 = (f32[120,256]{1,0:T(8,128)S(1)}, f32[120,256]{1,0:T(8,128)S(1)}, u32[]{:S(2)}, u32[]{:S(2)}) collective-permute-start(f32[120,256]{1,0:T(8,128)S(1)} %get-tuple-element.50), channel_id=1, source_target_pairs={{0,1},{1,0},{2,3},{3,2},{4,5},{5,4},{6,7},{7,6},{8,9},{9,8},{10,11... | collective-permute-start | bytes 368648 | tf_op jit(solution)/shard_map/exchange/ppermute | solution.py:48
  10.0 12.8 %collective-permute-start.2 = (f32[56,256]{1,0:T(8,128)S(1)}, f32[56,256]{1,0:T(8,128)S(1)}, u32[]{:S(2)}, u32[]{:S(2)}) collective-permute-start(f32[56,256]{1,0:T(8,128)S(1)} %slice_add_fusion.3), channel_id=1, source_target_pairs={{0,1},{1,0},{2,4},{3,5},{4,2},{5,3},{6,8},{7,9},{8,6},{9,7},{10,12... | collective-permute-start | bytes 172040 | tf_op jit(solution)/shard_map/exchange/ppermute | solution.py:65
  18.7 1.3 %copy-start = (bf16[4,1,2,19,16,256]{5,4,3,2,1,0:T(8,128)(2,1)S(1)}, bf16[4,1,2,19,16,256]{5,4,3,2,1,0:T(8,128)(2,1)}, u32[]{:S(2)}) copy-start(bf16[4,1,2,19,16,256]{5,4,3,2,1,0:T(8,128)(2,1)} %param.9) | copy-start | bytes 3735556
  20.0 0.8 copy-start.3
  20.8 0.8 copy-start.4
  22.8 3.7 %collective-permute-start.3 = (f32[8,256]{1,0:T(8,128)S(1)}, f32[8,256]{1,0:T(8,128)S(1)}, u32[]{:S(2)}, u32[]{:S(2)}) collective-permute-start(f32[8,256]{1,0:T(8,128)S(1)} %slice_add_fusion.13), channel_id=1, source_target_pairs={{0,2},{1,3},{2,0},{3,1},{4,6},{5,7},{6,4},{7,5},{8,10},{9,11},{10,... | collective-permute-start | bytes 24584 | tf_op jit(solution)/shard_map/exchange/ppermute | solution.py:53
  27.5 3.5 %collective-permute-start.4 = (f32[48,256]{1,0:T(8,128)S(1)}, f32[48,256]{1,0:T(8,128)S(1)}, u32[]{:S(2)}, u32[]{:S(2)}) collective-permute-start(f32[48,256]{1,0:T(8,128)S(1)} %get-tuple-element.59), channel_id=1, source_target_pairs={{0,3},{1,2},{2,1},{3,0},{4,7},{5,6},{6,5},{7,4},{8,11},{9,10},{10,... | collective-permute-start | bytes 147464 | tf_op jit(solution)/shard_map/exchange/ppermute | solution.py:53
  27.6 3.5 %collective-permute-start.5 = (f32[120,256]{1,0:T(8,128)S(1)}, f32[120,256]{1,0:T(8,128)S(1)}, u32[]{:S(2)}, u32[]{:S(2)}) collective-permute-start(f32[120,256]{1,0:T(8,128)S(1)} %get-tuple-element.60), channel_id=1, source_target_pairs={{0,1},{1,0},{2,3},{3,2},{4,5},{5,4},{6,7},{7,6},{8,9},{9,8},{10,11... | collective-permute-start | bytes 368648 | tf_op jit(solution)/shard_map/exchange/ppermute | solution.py:48
  31.1 8.5 %collective-permute-start.6 = (f32[56,256]{1,0:T(8,128)S(1)}, f32[56,256]{1,0:T(8,128)S(1)}, u32[]{:S(2)}, u32[]{:S(2)}) collective-permute-start(f32[56,256]{1,0:T(8,128)S(1)} %slice_add_fusion.2), channel_id=1, source_target_pairs={{0,1},{1,0},{2,4},{3,5},{4,2},{5,3},{6,8},{7,9},{8,6},{9,7},{10,12... | collective-permute-start | bytes 172040 | tf_op jit(solution)/shard_map/exchange/ppermute | solution.py:65
  39.6 3.7 %collective-permute-start.7 = (f32[8,256]{1,0:T(8,128)S(1)}, f32[8,256]{1,0:T(8,128)S(1)}, u32[]{:S(2)}, u32[]{:S(2)}) collective-permute-start(f32[8,256]{1,0:T(8,128)S(1)} %slice_add_fusion.10), channel_id=1, source_target_pairs={{0,2},{1,3},{2,0},{3,1},{4,6},{5,7},{6,4},{7,5},{8,10},{9,11},{10,... | collective-permute-start | bytes 24584 | tf_op jit(solution)/shard_map/exchange/ppermute | solution.py:53
  44.2 3.5 %collective-permute-start.8 = (f32[48,256]{1,0:T(8,128)S(1)}, f32[48,256]{1,0:T(8,128)S(1)}, u32[]{:S(2)}, u32[]{:S(2)}) collective-permute-start(f32[48,256]{1,0:T(8,128)S(1)} %get-tuple-element.67), channel_id=1, source_target_pairs={{0,3},{1,2},{2,1},{3,0},{4,7},{5,6},{6,5},{7,4},{8,11},{9,10},{10,... | collective-permute-start | bytes 147464 | tf_op jit(solution)/shard_map/exchange/ppermute | solution.py:53
  44.2 3.5 %collective-permute-start.9 = (f32[120,256]{1,0:T(8,128)S(1)}, f32[120,256]{1,0:T(8,128)S(1)}, u32[]{:S(2)}, u32[]{:S(2)}) collective-permute-start(f32[120,256]{1,0:T(8,128)S(1)} %get-tuple-element.68), channel_id=1, source_target_pairs={{0,1},{1,0},{2,3},{3,2},{4,5},{5,4},{6,7},{7,6},{8,9},{9,8},{10,11... | collective-permute-start | bytes 368648 | tf_op jit(solution)/shard_map/exchange/ppermute | solution.py:48
  47.7 8.5 %collective-permute-start.10 = (f32[56,256]{1,0:T(8,128)S(1)}, f32[56,256]{1,0:T(8,128)S(1)}, u32[]{:S(2)}, u32[]{:S(2)}) collective-permute-start(f32[56,256]{1,0:T(8,128)S(1)} %slice_add_fusion.1), channel_id=1, source_target_pairs={{0,1},{1,0},{2,4},{3,5},{4,2},{5,3},{6,8},{7,9},{8,6},{9,7},{10,12... | collective-permute-start | bytes 172040 | tf_op jit(solution)/shard_map/exchange/ppermute | solution.py:65
  56.2 3.7 %collective-permute-start.11 = (f32[8,256]{1,0:T(8,128)S(1)}, f32[8,256]{1,0:T(8,128)S(1)}, u32[]{:S(2)}, u32[]{:S(2)}) collective-permute-start(f32[8,256]{1,0:T(8,128)S(1)} %slice_add_fusion.7), channel_id=1, source_target_pairs={{0,2},{1,3},{2,0},{3,1},{4,6},{5,7},{6,4},{7,5},{8,10},{9,11},{10,... | collective-permute-start | bytes 24584 | tf_op jit(solution)/shard_map/exchange/ppermute | solution.py:53
  60.8 3.5 %collective-permute-start.12 = (f32[48,256]{1,0:T(8,128)S(1)}, f32[48,256]{1,0:T(8,128)S(1)}, u32[]{:S(2)}, u32[]{:S(2)}) collective-permute-start(f32[48,256]{1,0:T(8,128)S(1)} %get-tuple-element.75), channel_id=1, source_target_pairs={{0,3},{1,2},{2,1},{3,0},{4,7},{5,6},{6,5},{7,4},{8,11},{9,10},{10,... | collective-permute-start | bytes 147464 | tf_op jit(solution)/shard_map/exchange/ppermute | solution.py:53
  60.8 3.5 %collective-permute-start.13 = (f32[120,256]{1,0:T(8,128)S(1)}, f32[120,256]{1,0:T(8,128)S(1)}, u32[]{:S(2)}, u32[]{:S(2)}) collective-permute-start(f32[120,256]{1,0:T(8,128)S(1)} %get-tuple-element.76), channel_id=1, source_target_pairs={{0,1},{1,0},{2,3},{3,2},{4,5},{5,4},{6,7},{7,6},{8,9},{9,8},{10,11... | collective-permute-start | bytes 368648 | tf_op jit(solution)/shard_map/exchange/ppermute | solution.py:48
  64.3 8.5 %collective-permute-start.14 = (f32[56,256]{1,0:T(8,128)S(1)}, f32[56,256]{1,0:T(8,128)S(1)}, u32[]{:S(2)}, u32[]{:S(2)}) collective-permute-start(f32[56,256]{1,0:T(8,128)S(1)} %slice_add_fusion), channel_id=1, source_target_pairs={{0,1},{1,0},{2,4},{3,5},{4,2},{5,3},{6,8},{7,9},{8,6},{9,7},{10,12... | collective-permute-start | bytes 172040 | tf_op jit(solution)/shard_map/exchange/ppermute | solution.py:65
  72.8 3.7 %collective-permute-start.15 = (f32[8,256]{1,0:T(8,128)S(1)}, f32[8,256]{1,0:T(8,128)S(1)}, u32[]{:S(2)}, u32[]{:S(2)}) collective-permute-start(f32[8,256]{1,0:T(8,128)S(1)} %slice_add_fusion.4), channel_id=1, source_target_pairs={{0,2},{1,3},{2,0},{3,1},{4,6},{5,7},{6,4},{7,5},{8,10},{9,11},{10,... | collective-permute-start | bytes 24584 | tf_op jit(solution)/shard_map/exchange/ppermute | solution.py:53
where the time goes:
time: 78.5 us; the launch traced here: 78 us
  waiting for transfers between devices  33 us (42%)
  starting transfers between devices  22.3 us (28%)
  Pallas kernels  15.8 us (20%)
  local copies, waits for them, and re-layouts  6.7 us (9%)
    ppermute x4, starting transfers between devices, far_swap(): return lax.ppermute(value, axes, pairs)  20.5 us
    ppermute x8, waiting for transfers between devices, mate_swap(): return lax.ppermute(value, axes, pairs)  19.3 us
    pallas_call x10, Pallas kernels, call(): pl.pallas_call(kernel, out_shape=outs, in_specs=in_specs or [smem()] + [v...  15.8 us
    ppermute x4, waiting for transfers between devices, far_swap(): return lax.ppermute(value, axes, pairs)  13.6 us
    unnamed x16, local copies, waits for them, and re-layouts  6.68 us
  transfers between devices with their start and end apart: 16, of which 11 were waited for; matrix products, arithmetic and copies ran while one was open for 0% of the time, Pallas kernels for 12%

commit v1 on v0

--- a/solution.py
+++ b/solution.py
@@ -35,12 +35,10 @@
 pops, edge, plane = 19, 16, 256
 f32, bf16 = jnp.float32, jnp.bfloat16
 
-item_row = (0, 0, 56)
-mate_d = 40
-own_f, far_f, own_d, mate_f, far_d = 40, 48, 96, 104, 112
-mate_rows, level_rows = 48, 120
-at_level, at_odd, at_prev, at_inner, at_next = 12, 13, 14, 15, 16
-table_size = 17
+item_row = (0, 0, 48)
+own_f, mate_f, far_d, loc_d, level_rows = 40, 88, 96, 104, 112
+loc_f, far_f, own_d, kept_rows = 0, 8, 16, 24
+at_parent, at_octant, at_prev, at_next = 8, 9, 10, 11
 
 
 def level_swap(value, slabs):
@@ -74,11 +72,11 @@
 
 
 def select(values, matrix):
-    high = values.astype(bf16)
-    low = (values - high.astype(f32)).astype(bf16)
-    return jnp.dot(high, matrix, preferred_element_type=f32) + jnp.dot(
-        low, matrix, preferred_element_type=f32
-    )
+    rows = values.shape[0]
+    high = values.astype(bf16).astype(f32)
+    halves = jnp.concatenate([high, values - high], axis=0).astype(bf16)
+    both = jnp.dot(halves, matrix, preferred_element_type=f32)
+    return both[:rows] + both[rows:]
 
 
 def ones_where(mask):
@@ -89,8 +87,36 @@
     return lax.broadcasted_iota(jnp.int32, shape, dim)
 
 
-def pick_matrices(d_ref, j):
-    level, octant = d_ref[at_level], d_ref[6 + j]
+class Table:
+    def __init__(self, row):
+        codes = [row[0, j] for j in range(3)]
+        self.valid = [code >= 0 for code in codes]
+        self.block = [(code >> 4) & 1 for code in codes]
+        self.octant = [(code >> 1) & 7 for code in codes]
+        self.other = [code & 1 for code in codes]
+        self.level, self.odd, prev, inner, next_ = (row[0, j] for j in range(3, 8))
+        self.prev, self.inner, self.next = prev >= 0, inner >= 0, next_ >= 0
+
+
+def make_table(tables, slab, level):
+    odd = slab & 1
+    row, lane = iota(tables.shape, 0), iota(tables.shape, 1)
+    octant = jnp.where(level == 0, lane, pltpu.roll(tables, 127, 1))
+    here = jnp.where(level == 0, jnp.where(lane < at_parent, 1, 0), jnp.where(lane == at_parent, 1, 0))
+    code = row * 16 + octant * 2 + (tables & 1)
+    code = jnp.where((here == 1) & (row < 2) & (tables >= 0), code, -1)
+    offset = (tables >> 1) - slab
+    towards = 1 - 2 * odd
+    values = [jnp.max(jnp.where(offset == d, code, -1)) for d in (towards, -towards, 0)]
+    values += [level, odd, tables[0, at_prev], tables[0, at_next], tables[1, at_next]]
+    out = jnp.zeros(tables.shape, jnp.int32)
+    for n, value in enumerate(values):
+        out = jnp.where(lane == n, value, out)
+    return out
+
+
+def pick_matrices(t, j):
+    level, octant = t.level, t.octant[j]
     source = cell_key(iota((plane, 128), 0), level, octant)
     pick = ones_where(source == (iota((1, 128), 1) & 63))
     target = cell_key(iota((1, plane), 1), 1 - level, octant)
@@ -100,44 +126,42 @@
     return pick, place
 
 
-def plane_scale(d_ref):
-    return jnp.where(d_ref[at_level] == 0, 0.125, 1.0)
-
-
-def pack(d_ref, alpha_ref, w_ref, k_ref, near_ref, lvl_ref, loc_ref, scratch, matrices):
+def plane_scale(t):
+    return jnp.where(t.level == 0, 0.125, 1.0)
+
+
+def pack(t, alpha_ref, w_ref, k_ref, item_ref, side_ref, lvl_ref, ends_ref, scratch, matrices):
     item_scr, rim_scr, half_scr = scratch
-    level = d_ref[at_level]
-    odd = d_ref[at_odd]
-    near_ref[...] = jnp.zeros_like(near_ref)
-    lvl_ref[...] = jnp.zeros_like(lvl_ref)
+    level, odd = t.level, t.odd
+    for ref in (item_ref, side_ref, lvl_ref, ends_ref):
+        ref[...] = jnp.zeros_like(ref)
     item_scr[152:160, :] = jnp.zeros((8, plane), f32)
     rim_scr[...] = jnp.zeros_like(rim_scr)
-    loc_ref[...] = jnp.zeros_like(loc_ref)
     for i in range(5):
         e, w = east_pops[i], west_pops[i]
-        low = alpha_ref[0, e, 0:1, :] * k_ref[0, 0:1, :]
-        high = alpha_ref[1, w, edge - 1 : edge, :] * k_ref[1, edge - 1 : edge, :]
-        loc_ref[i : i + 1, :] = jnp.where(odd == 1, low, high)
-        loc_ref[8 + i : 9 + i, :] = jnp.where(odd == 1, high, low)
+        low = alpha_ref[e, 0:1, :] * k_ref[0, 0:1, :]
+        high = alpha_ref[pops + w, edge - 1 : edge, :] * k_ref[1, edge - 1 : edge, :]
+        lvl_ref[loc_d + i : loc_d + i + 1, :] = jnp.where(odd == 1, low, high)
+        ends_ref[loc_f + i : loc_f + i + 1, :] = jnp.where(odd == 1, high, low)
     for j in range(3):
         base = item_row[j]
-        out_ref = near_ref if j == 0 else lvl_ref
-
-        @pl.when(d_ref[j] == 1)
+        out_ref = item_ref if j == 0 else lvl_ref
+
+        @pl.when(t.valid[j])
         def _(j=j, base=base, out_ref=out_ref):
-            g, octant, other = d_ref[3 + j], d_ref[6 + j], d_ref[9 + j]
+            g, octant, other = t.block[j], t.octant[j], t.other[j]
             ox = octant >> 2
             pick, place = matrices(j)
 
             @pl.when(level == 0)
             def _():
                 rows = pl.ds(pl.multiple_of(ox * 8, 8), 8)
-                part = alpha_ref[g, :, rows, :] * w_ref[g, rows, :][None]
+                part = alpha_ref[pl.ds(g * pops, pops), rows, :] * w_ref[g, rows, :][None]
                 item_scr[0:152, :] = part.reshape(152, plane)
 
             @pl.when(level == 1)
             def _():
-                part = (alpha_ref[g] * w_ref[g][None]).reshape(304, plane)
+                part = (alpha_ref[pl.ds(g * pops, pops)] * w_ref[g][None]).reshape(304, plane)
                 for n in range(2):
                     lanes = slice(128 * n, 128 * n + 128)
                     half_scr[n, 0:304, :] = part[:, lanes]
@@ -158,99 +182,43 @@
                     rim_scr[i : i + 1, :] = jnp.where(
                         other == 1, item_scr[w : w + 1, :], item_scr[e : e + 1, :]
                     )
-                spread = select(rim_scr[...], place) * plane_scale(d_ref)
+                spread = select(rim_scr[...], place) * plane_scale(t)
                 towards_d = other != odd
-                if j == 0:
-
-                    @pl.when(towards_d)
-                    def _():
-                        near_ref[mate_d : mate_d + 8, :] = spread
-
-                    @pl.when(jnp.logical_not(towards_d))
-                    def _():
-                        lvl_ref[mate_f : mate_f + 8, :] = spread
-
-                else:
-                    if j == 1:
-                        row = jnp.where(towards_d, far_d, far_f)
-                    else:
-                        row = jnp.where(towards_d, own_d, own_f)
-                    lvl_ref[pl.ds(pl.multiple_of(row, 8), 8), :] = spread
-
-
-def describe(slab, level, chain_ref, parent_ref, children_ref, d_ref):
-    odd = slab & 1
-    for n in range(at_level):
-        d_ref[n] = 0
-
-    def note(valid, offset, g, octant, other):
-        slot = jnp.where(offset == 0, 2, jnp.where(offset == 1 - 2 * odd, 0, 1))
-
-        @pl.when(valid)
-        def _():
-            d_ref[slot] = 1
-            d_ref[3 + slot] = g
-            d_ref[6 + slot] = octant
-            d_ref[9 + slot] = other & 1
-
-    @pl.when(level == 0)
-    def _():
-        for g in range(2):
-            for octant in range(8):
-                fine = children_ref[g, octant]
-                note(fine >= 0, (fine >> 1) - slab, g, octant, fine)
-
-    @pl.when(level == 1)
-    def _():
-        for g in range(2):
-            coarse = parent_ref[g, 0]
-            note(coarse >= 0, (coarse >> 1) - slab, g, parent_ref[g, 1], coarse)
-
-    def flag(entry):
-        return jnp.where(entry >= 0, 1, 0)
-
-    d_ref[at_level] = level
-    d_ref[at_odd] = odd
-    d_ref[at_prev] = flag(chain_ref[0, 0])
-    d_ref[at_inner] = flag(chain_ref[0, 1])
-    d_ref[at_next] = flag(chain_ref[1, 1])
+                to_d = ((side_ref, 0), (lvl_ref, far_d), (ends_ref, own_d))[j]
+                to_f = ((lvl_ref, mate_f), (ends_ref, far_f), (lvl_ref, own_f))[j]
+                for wanted, (ref, row) in ((towards_d, to_d), (other == odd, to_f)):
+
+                    @pl.when(wanted)
+                    def _(ref=ref, row=row):
+                        ref[row : row + 8, :] = spread
 
 
 def first_pack_kernel(*refs):
-    tables_in, (alpha_in, w_in) = refs[:3], refs[3:5]
-    d_ref, near_ref, lvl_ref, loc_ref, k_ref, alpha_ref, w_ref = refs[5:12]
-    scratch, tables, sems = refs[12:15], refs[15:18], refs[18]
-    small = [pltpu.make_async_copy(tables_in[n], tables[n], sems.at[n]) for n in range(3)]
-    large = [
-        pltpu.make_async_copy(w_in, w_ref, sems.at[3]),
-        pltpu.make_async_copy(alpha_in, alpha_ref, sems.at[4]),
-    ]
-    for copy in small + large:
-        copy.start()
-    for copy in small:
-        copy.wait()
-    level = lax.axis_index("lvl")
-    describe(lax.axis_index("slab"), level, *tables, d_ref)
+    tables_ref, alpha_ref, d_ref, item_ref, side_ref, lvl_ref, ends_ref, k_ref = refs[:8]
+    scratch = refs[8:]
+    w_ref = alpha_ref.at[blend_at : blend_at + 2]
+    row = make_table(tables_ref[...], lax.axis_index("slab"), lax.axis_index("lvl"))
+    d_ref[...] = row
+    t = Table(row)
+    level = t.level
     x = iota((edge, plane), 0)
     cell = iota((edge, plane), 1)
     covers = []
     for g in range(2):
         covered = jnp.zeros((edge, plane), jnp.bool_)
         for j in range(3):
-            octant = d_ref[6 + j]
+            octant = t.octant[j]
             inside = (
                 ((x >> 3) == (octant >> 2))
                 & ((cell >> 7) == ((octant >> 1) & 1))
                 & (((cell >> 3) & 1) == (octant & 1))
             ) | (level == 1)
-            covered = covered | (inside & (d_ref[j] == 1) & (d_ref[3 + j] == g))
+            covered = covered | (inside & t.valid[j] & (t.block[j] == g))
         covers.append(covered)
-    for copy in large:
-        copy.wait()
     for g in range(2):
         k_ref[g] = jnp.where(covers[g], 1.0 - w_ref[g], 1.0)
-    matrices = functools.partial(pick_matrices, d_ref)
-    pack(d_ref, alpha_ref, w_ref, k_ref, near_ref, lvl_ref, loc_ref, scratch, matrices)
+    matrices = functools.partial(pick_matrices, t)
+    pack(t, alpha_ref, w_ref, k_ref, item_ref, side_ref, lvl_ref, ends_ref, scratch, matrices)
 
 
 def moved_cells(values, c, z):
@@ -268,8 +236,9 @@
 def fields_kernel(*refs):
     d_ref, pop_ref, relax_ref, solid_ref = refs[:4]
     u_ref, keep_ref, gain_ref, bits_ref, pick_ref, place_ref, pad_scr = refs[4:]
+    t = Table(d_ref[...])
     for j in range(3):
-        pick_ref[j], place_ref[j] = pick_matrices(d_ref, j)
+        pick_ref[j], place_ref[j] = pick_matrices(t, j)
     z = iota((edge, plane), 1) & 15
     for g in range(2):
         solid = solid_ref[g] > 0
@@ -343,13 +312,13 @@
         added_ref, refs = refs[0], refs[1:]
     if not last:
         (w_ref, pick_ref, place_ref), refs = refs[:3], refs[3:]
-        out_ref, near_out, lvl_out, loc_out, beta_scr, item_scr, rim_scr, half_scr = refs
+        out_ref, *sent, beta_scr, item_scr, rim_scr, half_scr = refs
     else:
         out_ref, beta_scr, half_scr = refs
-    level = d_ref[at_level]
-    odd = d_ref[at_odd]
+    t = Table(d_ref[...])
+    level, odd = t.level, t.odd
     for g in range(2):
-        beta_scr[g, :, 8:24, :] = alpha_ref[g] * k_ref[g][None]
+        beta_scr[g, :, 8:24, :] = alpha_ref[g * pops : (g + 1) * pops] * k_ref[g][None]
     if not first:
         for is_odd, (g, x) in enumerate(late_layer):
 
@@ -363,9 +332,9 @@
     for j in range(3):
         first = item_row[j]
 
-        @pl.when(d_ref[j] == 1)
+        @pl.when(t.valid[j])
         def _(j=j, first=first):
-            g, octant = d_ref[3 + j], d_ref[6 + j]
+            g, octant = t.block[j], t.octant[j]
             left = iota((40, 128), 1) < 64
             a = sources[j][first : first + 40, 0:128]
             b = sources[j][first : first + 40, 128:256]
@@ -397,12 +366,12 @@
                     beta_scr[g, :, 8:24, lanes] += both
 
     from_d = lvl_ref[mate_f : mate_f + 8, :]
-    from_f = far_ref[own_f : own_f + 8, :] + lvl_ref[far_d : far_d + 8, :]
+    from_f = far_ref[40:48, :] + lvl_ref[far_d : far_d + 8, :]
     above = jnp.where(odd == 1, from_f, from_d)
     below = jnp.where(odd == 1, from_d, from_f)
-    above = jnp.where(d_ref[at_next] == 1, above, 0.0)
-    below = jnp.where(d_ref[at_prev] == 1, below, 0.0)
-    inner = d_ref[at_inner] == 1
+    above = jnp.where(t.next, above, 0.0)
+    below = jnp.where(t.prev, below, 0.0)
+    inner = t.inner
     for i in range(5):
         e, w = east_pops[i], west_pops[i]
         beta_scr[1, e, 24:25, :] = above[i : i + 1]
@@ -425,11 +394,11 @@
             u = [u_ref[g, a, rows, :] for a in range(3)]
             done = collide(pulled, u, keep_ref[g, rows, :], gain_ref[g, rows, :])
             for i in range(pops):
-                out_ref[g, i, rows, :] = done[i]
+                out_ref[g * pops + i, rows, :] = done[i]
     if not last:
         scratch = (item_scr, rim_scr, half_scr)
         matrices = lambda j: (pick_ref[j], place_ref[j])
-        pack(d_ref, out_ref, w_ref, k_ref, near_out, lvl_out, loc_out, scratch, matrices)
+        pack(t, out_ref, w_ref, k_ref, *sent, scratch, matrices)
 
 
 late_layer = ((1, edge - 1), (0, 0))
@@ -449,11 +418,11 @@
 
 def finish_kernel(*refs):
     (d_ref, late_ref, u_ref, keep_ref, gain_ref, w_ref, k_ref, pick_ref, place_ref) = refs[:9]
-    (near_in, lvl_in, loc_in, added_ref, near_ref, lvl_ref, loc_ref, rim_scr) = refs[9:]
-    level = d_ref[at_level]
-    near_ref[...] = near_in[...]
-    lvl_ref[...] = lvl_in[...]
-    loc_ref[...] = loc_in[...]
+    given, added_ref, sent, rim_scr = refs[9:13], refs[13], refs[14:18], refs[18]
+    item_ref, side_ref, lvl_ref, ends_ref = sent
+    t = Table(d_ref[...])
+    for source, ref in zip(given, sent):
+        ref[...] = source[...]
     added_ref[...] = jnp.zeros_like(added_ref)
     rim_scr[...] = jnp.zeros_like(rim_scr)
 
@@ -465,19 +434,18 @@
             added_ref[i : i + 1, :] = values[i]
         kept, weight = k_ref[g, x : x + 1, :], w_ref[g, x : x + 1, :]
         for n, i in enumerate(leaving):
-            loc_ref[n : n + 1, :] += values[i] * kept
+            lvl_ref[loc_d + n : loc_d + n + 1, :] += values[i] * kept
             rim_scr[n : n + 1, :] = values[i] * weight
         weighted = added_ref[...] * weight
         left = iota((1, 128), 1) < 64
         at_row = iota((8, plane), 0) == (0 if is_odd else 7)
         for j in range(3):
             base = item_row[j]
-            out_ref = near_ref if j == 0 else lvl_ref
-            octant, other = d_ref[6 + j], d_ref[9 + j]
-            ox = octant >> 2
-            inside = (level == 1) | (ox == 1 - is_odd)
-
-            @pl.when((d_ref[j] == 1) & (d_ref[3 + j] == g) & inside)
+            out_ref = item_ref if j == 0 else lvl_ref
+            other, ox = t.other[j], t.octant[j] >> 2
+            inside = (t.level == 1) | (ox == 1 - is_odd)
+
+            @pl.when(t.valid[j] & (t.block[j] == g) & inside)
             def _(j=j, base=base, out_ref=out_ref, ox=ox, other=other):
                 picked = select(weighted, pick_ref[j])
                 for n in range(5):
@@ -486,41 +454,55 @@
                     tile = slice(base + 8 * n, base + 8 * n + 8)
                     out_ref[tile, :] += jnp.where(at_row, row, 0.0)
 
-                @pl.when((other == 1 - is_odd) & ((level == 0) | (ox == other)))
+                @pl.when((other == 1 - is_odd) & ((t.level == 0) | (ox == other)))
                 def _():
-                    first = (mate_d, far_d, own_d)[j]
-                    spread = select(rim_scr[...], place_ref[j]) * plane_scale(d_ref)
-                    out_ref[first : first + 8, :] += spread
-
-    @pl.when((d_ref[at_odd] == 0) & (d_ref[at_next] == 1))
+                    spread = select(rim_scr[...], place_ref[j]) * plane_scale(t)
+                    ref, row = ((side_ref, 0), (lvl_ref, far_d), (ends_ref, own_d))[j]
+                    ref[row : row + 8, :] += spread
+
+    @pl.when((t.odd == 0) & t.next)
     def _():
         side(0)
 
-    @pl.when((d_ref[at_odd] == 1) & (d_ref[at_prev] == 1))
+    @pl.when((t.odd == 1) & t.prev)
     def _():
         side(1)
 
 
-def last_kernel(d_ref, alpha_in, late_ref, u_ref, keep_ref, gain_ref, alpha_ref):
-    alpha_ref[...] = alpha_in[...]
+def last_kernel(d_ref, alpha_ref, late_ref, u_ref, keep_ref, gain_ref, out_ref, tile_scr, sems):
+    def tile(source, g, x, sem):
+        block, rows = pl.ds(g * pops, pops), pl.ds(x, 8)
+        source = source.at[block, rows] if source is alpha_ref else source
+        return pltpu.make_async_copy(source, out_ref.at[block, rows], sems.at[sem])
+
+    copies = [tile(alpha_ref, 0, 8, 0), tile(alpha_ref, 1, 0, 1)]
+    for copy in copies:
+        copy.start()
+    t = Table(d_ref[...])
+    odd = t.odd
+    copies.append(tile(alpha_ref, odd, pl.multiple_of(8 * odd, 8), 2))
+    copies[2].start()
+    reached = pl.multiple_of(8 - 8 * odd, 8)
+    tile_scr[...] = alpha_ref[pl.ds((1 - odd) * pops, pops), pl.ds(reached, 8), :]
 
     def side(is_odd):
-        g, x = late_layer[is_odd]
         values = late_values(is_odd, late_ref, u_ref, keep_ref, gain_ref)
+        x = late_layer[is_odd][1] % 8
         for i in range(pops):
-            alpha_ref[g, i, x : x + 1, :] += values[i]
-
-    @pl.when((d_ref[at_odd] == 0) & (d_ref[at_next] == 1))
+            tile_scr[i, x : x + 1, :] += values[i]
+
+    @pl.when((odd == 0) & t.next)
     def _():
         side(0)
 
-    @pl.when((d_ref[at_odd] == 1) & (d_ref[at_prev] == 1))
+    @pl.when((odd == 1) & t.prev)
     def _():
         side(1)
 
-
-def smem():
-    return pl.BlockSpec(memory_space=pltpu.SMEM)
+    copies.append(tile(tile_scr, 1 - odd, reached, 3))
+    copies[3].start()
+    for copy in copies:
+        copy.wait()
 
 
 def vmem():
@@ -534,11 +516,10 @@
 params = pltpu.CompilerParams(vmem_limit_bytes=24 * 1024 * 1024)
 half_scratch = [pltpu.VMEM((2, 320, 128), f32)]
 pack_scratch = [pltpu.VMEM((160, plane), f32), pltpu.VMEM((8, plane), f32)] + half_scratch
-near_shape = shape(mate_rows, plane)
-level_shape = shape(level_rows, plane)
-ends_shape = shape(16, plane)
+messages = [shape(rows, plane) for rows in (40, 8, level_rows, kept_rows)]
 field = shape(2, edge, plane)
-state = shape(2, pops, edge, plane)
+state = shape(2 * pops, edge, plane)
+blend_at = 2 * pops
 
 
 def hbm():
@@ -549,12 +530,12 @@
     return pl.CostEstimate(flops=flops, bytes_accessed=bytes_accessed, transcendentals=0)
 
 
-def call(kernel, outs, ins, scratch, name, in_specs=None, out_specs=None, estimate=None):
+def call(kernel, outs, ins, scratch, name, out_specs=None, estimate=None):
     with jax.named_scope(name):
         return pl.pallas_call(
             kernel,
             out_shape=outs,
-            in_specs=in_specs or [smem()] + [vmem()] * (len(ins) - 1),
+            in_specs=[vmem()] * len(ins),
             out_specs=out_specs or [vmem()] * len(outs),
             scratch_shapes=scratch,
             compiler_params=params,
@@ -566,18 +547,17 @@
     adjoint_final, populations, relaxation, blend, solid, chain, parent, children, *, slabs
 ):
     steps = populations.shape[0]
-    messages = [near_shape, level_shape, ends_shape]
-    table, near, lvl, ends, kept, alpha, weights = call(
+    alpha = jnp.concatenate([adjoint_final.reshape(2 * pops, edge, plane), blend[0]], axis=0)
+    tables = jnp.concatenate([children, parent, chain[0]], axis=1)
+    tables = jnp.pad(tables, ((0, 6), (0, 116)), constant_values=-1)
+    table, *sent, kept = call(
         first_pack_kernel,
-        [shape(table_size, dtype=jnp.int32)] + messages + [field, state, field],
-        (chain[0], parent, children, adjoint_final[0], blend[0]),
-        pack_scratch
-        + [pltpu.SMEM(v.shape, jnp.int32) for v in (chain[0], parent, children)]
-        + [pltpu.SemaphoreType.DMA((5,))],
+        [shape(8, 128, dtype=jnp.int32)] + messages + [field],
+        (tables, alpha),
+        pack_scratch,
         "pack_first",
-        in_specs=[hbm()] * 5,
-        out_specs=[smem()] + [vmem()] * 6,
     )
+    weights = alpha[blend_at:]
     flows, keep, gain, bits, pick, place = call(
         fields_kernel,
         [
@@ -597,12 +577,16 @@
     for t in range(steps - 1, -1, -1):
         first, last = t == steps - 1, t == 0
         u = flows[t]
+        near, side, lvl, ends = sent
         with jax.named_scope("exchange"):
             lvl = level_swap(lvl, slabs)
+            side = mate_swap(side, slabs, 1)
+            end = lvl[own_f : own_f + 8] + ends[loc_f : loc_f + 8] + side
+            far = jnp.concatenate([lvl[0:40], end, ends[far_f : far_f + 8]], axis=0)
+            far = far_swap(far, slabs)
             mate = mate_swap(near, slabs, 1)
-            extra = ends[8:16] + mate[mate_d : mate_d + 8]
-            far = far_swap(lvl[0:56] + jnp.pad(extra, ((own_f, 8), (0, 0))), slabs)
-            late = mate_swap(ends[0:8] + lvl[own_d : own_d + 8] + far[far_f : far_f + 8], slabs, 0)
+            end = lvl[loc_d : loc_d + 8] + ends[own_d : own_d + 8] + far[48:56]
+            late = mate_swap(end, slabs, 1)
         ins = [table, alpha, kept, u, keep, gain, bits, mate, lvl, far]
         if not first:
             ins += [added]
@@ -619,17 +603,22 @@
         alpha = got[0]
         if last:
             alpha = call(
-                last_kernel, [state], (table, alpha, late, u, keep, gain), (), "finish"
+                last_kernel,
+                [state],
+                (table, alpha, late, u, keep, gain),
+                [pltpu.VMEM((pops, 8, plane), f32), pltpu.SemaphoreType.DMA((4,))],
+                "finish",
+                out_specs=[hbm()],
             )[0]
         else:
-            added, near, lvl, ends = call(
+            added, *sent = call(
                 finish_kernel,
                 [shape(24, plane)] + messages,
                 (table, late, u, keep, gain, weights, kept, pick, place, *got[1:]),
                 [pltpu.VMEM((8, plane), f32)],
                 "finish",
             )
-    return alpha[None]
+    return alpha.reshape(1, 2, pops, edge, plane)
 
 
 def solution(mesh):

time: 78.5 us -> 68.5 us (0.87); the launches traced: 78 us -> 67.2 us
  starting transfers between devices: 22.3 us -> 29.6 us
  waiting for transfers between devices: 33 us -> 25.7 us
  local copies, waits for them, and re-layouts: 6.7 us -> 0.06 us
  Pallas kernels: 15.8 us -> 9.44 us
  other arithmetic: 0.06 us -> 2.1 us
    unnamed x16 -> x8, local copies, waits for them, and re-layouts: 6.68 us -> 0.01 us
    pallas_call x10, Pallas kernels: 15.8 us -> 9.44 us  [call(): pl.pallas_call(kernel, out_shape=outs, in_specs=[vmem()] * len(ins), out_...]
    ppermute x4, starting transfers between devices: 20.5 us -> 26.4 us  [far_swap(): return lax.ppermute(value, axes, pairs)]
    ppermute x8 -> x12, waiting for transfers between devices: 19.3 us -> 14.1 us  [mate_swap(): return lax.ppermute(value, axes, pairs)]
    ppermute x4, waiting for transfers between devices: 13.6 us -> 8.97 us  [far_swap(): return lax.ppermute(value, axes, pairs)]
    ppermute x4, waiting for transfers between devices: 0.01 us -> 2.6 us  [level_swap(): return lax.ppermute(value, axes, pairs)]
    concatenate x0 -> x6, other arithmetic: none -> 2.06 us  [the longest x1 1.14 us: local(): jnp.concatenate([adjoint_final.reshape(2 * pops, edge, plane), blend[0]],...]
    ppermute x8 -> x12, starting transfers between devices: 1.27 us -> 2.19 us  [mate_swap(): return lax.ppermute(value, axes, pairs)]
  transfers between devices with their start and end apart: 16 -> 20, of which waited for: 11 -> 19; matrix products, arithmetic and copies ran while one was open for 0% -> 0% of each run, Pallas kernels for 12% -> 10%
where the time goes in v1:
time: 68.5 us; the launch traced here: 67.2 us
  starting transfers between devices  29.6 us (43%)
  waiting for transfers between devices  25.7 us (38%)
  Pallas kernels  9.44 us (14%)
  other arithmetic  2.1 us (3%)
    ppermute x4, starting transfers between devices, far_swap(): return lax.ppermute(value, axes, pairs)  26.4 us
    ppermute x12, waiting for transfers between devices, mate_swap(): return lax.ppermute(value, axes, pairs)  14.1 us
    pallas_call x10, Pallas kernels, call(): pl.pallas_call(kernel, out_shape=outs, in_specs=[vmem()] * len(ins), out_...  9.44 us
    ppermute x4, waiting for transfers between devices, far_swap(): return lax.ppermute(value, axes, pairs)  8.97 us
    ppermute x4, waiting for transfers between devices, level_swap(): return lax.ppermute(value, axes, pairs)  2.6 us
    ppermute x12, starting transfers between devices, mate_swap(): return lax.ppermute(value, axes, pairs)  2.19 us
  transfers between devices with their start and end apart: 20, of which 19 were waited for; matrix products, arithmetic and copies ran while one was open for 0% of the time, Pallas kernels for 10%

profile of v1, /device:TPU:6, one launch (start us, length us, event | category | flops | bytes accessed | tf_op | source)
XLA Modules:
  0.0 67.2 jit_solution(2030180315502035974)
XLA Ops:
  0.9 1.1 %pad_maximum_fusion.refs_1_ = f32[40,16,256]{2,1,0:T(8,128)S(1)} fusion(f32[2,16,256]{2,1,0:T(8,128)} %bitcast.15, f32[38,16,256]{2,1,0:T(8,128)} %bitcast.25), kind=kLoop, calls=%fused_computation | loop fusion | flops 163840 | bytes 1310720 | tf_op jit(solution)/shard_map/concatenate | solution.py:550
  2.0 1.4 %pack_first.1 = (s32[8,128]{1,0:T(8,128)S(1)}, f32[40,256]{1,0:T(8,128)S(1)}, f32[8,256]{1,0:T(8,128)S(1)}, f32[112,256]{1,0:T(8,128)S(1)}, f32[24,256]{1,0:T(8,128)S(1)}, /*index=5*/f32[2,16,256]{2,1,0:T(8,128)S(1)}) custom-call(s32[8,128]{1,0:T(8,128)S(1)} %pad.4.refs_0_, f32[40,16,256]{2,1,0:T(8,128)S(1)} %pad_maximum_fusion.refs_1_), custom_call_target="tpu_custom_call" | custom-call | tf_op jit(solution)/shard_map/pack_first/pallas_call | solution.py:535
  3.5 1.2 %collective-permute-start.2 = (f32[8,256]{1,0:T(8,128)S(1)}, f32[8,256]{1,0:T(8,128)S(1)}, u32[]{:S(2)}, u32[]{:S(2)}) collective-permute-start(f32[8,256]{1,0:T(8,128)S(1)} %get-tuple-element.56), channel_id=1, source_target_pairs={{0,3},{1,2},{2,1},{3,0},{4,7},{5,6},{6,5},{7,4},{8,11},{9,10},{10,... | collective-permute-start | bytes 24584 | tf_op jit(solution)/shard_map/exchange/ppermute | solution.py:51
  4.8 1.8 %collective-permute-done.2 = f32[8,256]{1,0:T(8,128)S(1)} collective-permute-done((f32[8,256]{1,0:T(8,128)S(1)}, f32[8,256]{1,0:T(8,128)S(1)}, u32[]{:S(2)}, u32[]{:S(2)}) %collective-permute-start.2) | collective-permute-done | bytes 8224 | tf_op jit(solution)/shard_map/exchange/ppermute | solution.py:51
  6.6 8.3 %collective-permute-start.3 = (f32[56,256]{1,0:T(8,128)S(1)}, f32[56,256]{1,0:T(8,128)S(1)}, u32[]{:S(2)}, u32[]{:S(2)}) collective-permute-start(f32[56,256]{1,0:T(8,128)S(1)} %pad_maximum_fusion.1), channel_id=1, source_target_pairs={{0,1},{1,0},{2,4},{3,5},{4,2},{5,3},{6,8},{7,9},{8,6},{9,7},{10,12... | collective-permute-start | bytes 172040 | tf_op jit(solution)/shard_map/exchange/ppermute | solution.py:63
  15.7 1.6 %collective-permute-done.3.refs_9_ = f32[56,256]{1,0:T(8,128)S(1)} collective-permute-done((f32[56,256]{1,0:T(8,128)S(1)}, f32[56,256]{1,0:T(8,128)S(1)}, u32[]{:S(2)}, u32[]{:S(2)}) %collective-permute-start.3) | collective-permute-done | bytes 57376 | tf_op jit(solution)/shard_map/exchange/ppermute | solution.py:63
  17.6 1.0 %collective-permute-done.refs_7_ = f32[40,256]{1,0:T(8,128)S(1)} collective-permute-done((f32[40,256]{1,0:T(8,128)S(1)}, f32[40,256]{1,0:T(8,128)S(1)}, u32[]{:S(2)}, u32[]{:S(2)}) %collective-permute-start) | collective-permute-done | bytes 40992 | tf_op jit(solution)/shard_map/exchange/ppermute | solution.py:51
  18.6 1.7 %step.4 = (f32[38,16,256]{2,1,0:T(8,128)S(1)}, f32[40,256]{1,0:T(8,128)S(1)}, f32[8,256]{1,0:T(8,128)S(1)}, f32[112,256]{1,0:T(8,128)S(1)}, f32[24,256]{1,0:T(8,128)S(1)}) custom-call(s32[8,128]{1,0:T(8,128)S(1)} %get-tuple-element.47.refs_0_.d_ref, f32[40,16,256]{2,1,0:T(8,128)S(1)} %pad_maximum_fusion.refs_1_, ...), custom_call_target="tpu_custom_call" | custom-call | flops 8000000 | bytes 2000000 | tf_op jit(solution)/shard_map/step/pallas_call | solution.py:535
  22.0 2.1 %collective-permute-done.7 = f32[8,256]{1,0:T(8,128)S(1)} collective-permute-done((f32[8,256]{1,0:T(8,128)S(1)}, f32[8,256]{1,0:T(8,128)S(1)}, u32[]{:S(2)}, u32[]{:S(2)}) %collective-permute-start.7) | collective-permute-done | bytes 8224 | tf_op jit(solution)/shard_map/exchange/ppermute | solution.py:51
  24.1 6.0 %collective-permute-start.8 = (f32[56,256]{1,0:T(8,128)S(1)}, f32[56,256]{1,0:T(8,128)S(1)}, u32[]{:S(2)}, u32[]{:S(2)}) collective-permute-start(f32[56,256]{1,0:T(8,128)S(1)} %pad_maximum_fusion.2), channel_id=1, source_target_pairs={{0,1},{1,0},{2,4},{3,5},{4,2},{5,3},{6,8},{7,9},{8,6},{9,7},{10,12... | collective-permute-start | bytes 172040 | tf_op jit(solution)/shard_map/exchange/ppermute | solution.py:63
  30.1 2.5 %collective-permute-done.8.refs_9_ = f32[56,256]{1,0:T(8,128)S(1)} collective-permute-done((f32[56,256]{1,0:T(8,128)S(1)}, f32[56,256]{1,0:T(8,128)S(1)}, u32[]{:S(2)}, u32[]{:S(2)}) %collective-permute-start.8) | collective-permute-done | bytes 57376 | tf_op jit(solution)/shard_map/exchange/ppermute | solution.py:63
  32.6 1.0 %collective-permute-done.5.refs_7_ = f32[40,256]{1,0:T(8,128)S(1)} collective-permute-done((f32[40,256]{1,0:T(8,128)S(1)}, f32[40,256]{1,0:T(8,128)S(1)}, u32[]{:S(2)}, u32[]{:S(2)}) %collective-permute-start.5) | collective-permute-done | bytes 40992 | tf_op jit(solution)/shard_map/exchange/ppermute | solution.py:51
  33.6 1.7 %step.5 = (f32[38,16,256]{2,1,0:T(8,128)S(1)}, f32[40,256]{1,0:T(8,128)S(1)}, f32[8,256]{1,0:T(8,128)S(1)}, f32[112,256]{1,0:T(8,128)S(1)}, f32[24,256]{1,0:T(8,128)S(1)}) custom-call(s32[8,128]{1,0:T(8,128)S(1)} %get-tuple-element.47.refs_0_.d_ref, f32[38,16,256]{2,1,0:T(8,128)S(1)} %get-tuple-element.59.refs_1_, ...), custom_call_target="tpu_custom_call" | custom-call | flops 8000000 | bytes 2000000 | tf_op jit(solution)/shard_map/step/pallas_call | solution.py:535
  37.2 2.0 %collective-permute-done.12 = f32[8,256]{1,0:T(8,128)S(1)} collective-permute-done((f32[8,256]{1,0:T(8,128)S(1)}, f32[8,256]{1,0:T(8,128)S(1)}, u32[]{:S(2)}, u32[]{:S(2)}) %collective-permute-start.12) | collective-permute-done | bytes 8224 | tf_op jit(solution)/shard_map/exchange/ppermute | solution.py:51
  39.3 6.2 %collective-permute-start.13 = (f32[56,256]{1,0:T(8,128)S(1)}, f32[56,256]{1,0:T(8,128)S(1)}, u32[]{:S(2)}, u32[]{:S(2)}) collective-permute-start(f32[56,256]{1,0:T(8,128)S(1)} %pad_maximum_fusion.3), channel_id=1, source_target_pairs={{0,1},{1,0},{2,4},{3,5},{4,2},{5,3},{6,8},{7,9},{8,6},{9,7},{10,12... | collective-permute-start | bytes 172040 | tf_op jit(solution)/shard_map/exchange/ppermute | solution.py:63
  45.4 2.3 %collective-permute-done.13.refs_9_ = f32[56,256]{1,0:T(8,128)S(1)} collective-permute-done((f32[56,256]{1,0:T(8,128)S(1)}, f32[56,256]{1,0:T(8,128)S(1)}, u32[]{:S(2)}, u32[]{:S(2)}) %collective-permute-start.13) | collective-permute-done | bytes 57376 | tf_op jit(solution)/shard_map/exchange/ppermute | solution.py:63
  47.8 1.4 %collective-permute-done.10.refs_7_ = f32[40,256]{1,0:T(8,128)S(1)} collective-permute-done((f32[40,256]{1,0:T(8,128)S(1)}, f32[40,256]{1,0:T(8,128)S(1)}, u32[]{:S(2)}, u32[]{:S(2)}) %collective-permute-start.10) | collective-permute-done | bytes 40992 | tf_op jit(solution)/shard_map/exchange/ppermute | solution.py:51
  49.2 1.7 %step.6 = (f32[38,16,256]{2,1,0:T(8,128)S(1)}, f32[40,256]{1,0:T(8,128)S(1)}, f32[8,256]{1,0:T(8,128)S(1)}, f32[112,256]{1,0:T(8,128)S(1)}, f32[24,256]{1,0:T(8,128)S(1)}) custom-call(s32[8,128]{1,0:T(8,128)S(1)} %get-tuple-element.47.refs_0_.d_ref, f32[38,16,256]{2,1,0:T(8,128)S(1)} %get-tuple-element.69.refs_1_, ...), custom_call_target="tpu_custom_call" | custom-call | flops 8000000 | bytes 2000000 | tf_op jit(solution)/shard_map/step/pallas_call | solution.py:535
  51.5 1.0 %collective-permute-done.16.refs_8_ = f32[112,256]{1,0:T(8,128)S(1)} collective-permute-done((f32[112,256]{1,0:T(8,128)S(1)}, f32[112,256]{1,0:T(8,128)S(1)}, u32[]{:S(2)}, u32[]{:S(2)}) %collective-permute-start.16) | collective-permute-done | bytes 114720 | tf_op jit(solution)/shard_map/exchange/ppermute | solution.py:46
  52.5 2.1 %collective-permute-done.17 = f32[8,256]{1,0:T(8,128)S(1)} collective-permute-done((f32[8,256]{1,0:T(8,128)S(1)}, f32[8,256]{1,0:T(8,128)S(1)}, u32[]{:S(2)}, u32[]{:S(2)}) %collective-permute-start.17) | collective-permute-done | bytes 8224 | tf_op jit(solution)/shard_map/exchange/ppermute | solution.py:51
  54.6 5.9 %collective-permute-start.18 = (f32[56,256]{1,0:T(8,128)S(1)}, f32[56,256]{1,0:T(8,128)S(1)}, u32[]{:S(2)}, u32[]{:S(2)}) collective-permute-start(f32[56,256]{1,0:T(8,128)S(1)} %pad_maximum_fusion.4), channel_id=1, source_target_pairs={{0,1},{1,0},{2,4},{3,5},{4,2},{5,3},{6,8},{7,9},{8,6},{9,7},{10,12... | collective-permute-start | bytes 172040 | tf_op jit(solution)/shard_map/exchange/ppermute | solution.py:63
  60.5 2.5 %collective-permute-done.18.refs_9_ = f32[56,256]{1,0:T(8,128)S(1)} collective-permute-done((f32[56,256]{1,0:T(8,128)S(1)}, f32[56,256]{1,0:T(8,128)S(1)}, u32[]{:S(2)}, u32[]{:S(2)}) %collective-permute-start.18) | collective-permute-done | bytes 57376 | tf_op jit(solution)/shard_map/exchange/ppermute | solution.py:63
  63.1 1.0 %collective-permute-done.15.refs_7_ = f32[40,256]{1,0:T(8,128)S(1)} collective-permute-done((f32[40,256]{1,0:T(8,128)S(1)}, f32[40,256]{1,0:T(8,128)S(1)}, u32[]{:S(2)}, u32[]{:S(2)}) %collective-permute-start.15) | collective-permute-done | bytes 40992 | tf_op jit(solution)/shard_map/exchange/ppermute | solution.py:51
  65.0 1.2 %collective-permute-done.19.late_ref = f32[8,256]{1,0:T(8,128)S(1)} collective-permute-done((f32[8,256]{1,0:T(8,128)S(1)}, f32[8,256]{1,0:T(8,128)S(1)}, u32[]{:S(2)}, u32[]{:S(2)}) %collective-permute-start.19) | collective-permute-done | bytes 8224 | tf_op jit(solution)/shard_map/exchange/ppermute | solution.py:51
  (54 shorter events, 8.1 us)
Async XLA Ops:
  0.0 15.0 %copy-start.3 = (s32[1,2,16,256]{3,2,1,0:T(8,128)S(1)}, s32[1,2,16,256]{3,2,1,0:T(8,128)}, u32[]{:S(2)}) copy-start(s32[1,2,16,256]{3,2,1,0:T(8,128)} %param.12) | copy-start | bytes 98308
  0.0 15.0 %copy-start.2 = (f32[1,2,16,256]{3,2,1,0:T(8,128)S(1)}, f32[1,2,16,256]{3,2,1,0:T(8,128)}, u32[]{:S(2)}) copy-start(f32[1,2,16,256]{3,2,1,0:T(8,128)} %param.10) | copy-start | bytes 98308
  0.0 15.0 %copy-start.1 = (bf16[4,1,2,19,16,256]{5,4,3,2,1,0:T(8,128)(2,1)S(1)}, bf16[4,1,2,19,16,256]{5,4,3,2,1,0:T(8,128)(2,1)}, u32[]{:S(2)}) copy-start(bf16[4,1,2,19,16,256]{5,4,3,2,1,0:T(8,128)(2,1)} %param.9) | copy-start | bytes 3735556
  3.4 15.2 %copy-start = (f32[1,2,16,256]{3,2,1,0:T(8,128)S(1)}, f32[1,2,16,256]{3,2,1,0:T(8,128)}, u32[]{:S(2)}) copy-start(f32[1,2,16,256]{3,2,1,0:T(8,128)} %param.11) | copy-start | bytes 98308
  3.4 1.3 %collective-permute-start.1 = (f32[112,256]{1,0:T(8,128)S(1)}, f32[112,256]{1,0:T(8,128)S(1)}, u32[]{:S(2)}, u32[]{:S(2)}) collective-permute-start(f32[112,256]{1,0:T(8,128)S(1)} %get-tuple-element.54), channel_id=1, source_target_pairs={{0,1},{1,0},{2,3},{3,2},{4,5},{5,4},{6,7},{7,6},{8,9},{9,8},{10,11... | collective-permute-start | bytes 344072 | tf_op jit(solution)/shard_map/exchange/ppermute | solution.py:46
  3.5 3.2 %collective-permute-start.2 = (f32[8,256]{1,0:T(8,128)S(1)}, f32[8,256]{1,0:T(8,128)S(1)}, u32[]{:S(2)}, u32[]{:S(2)}) collective-permute-start(f32[8,256]{1,0:T(8,128)S(1)} %get-tuple-element.56), channel_id=1, source_target_pairs={{0,3},{1,2},{2,1},{3,0},{4,7},{5,6},{6,5},{7,4},{8,11},{9,10},{10,... | collective-permute-start | bytes 24584 | tf_op jit(solution)/shard_map/exchange/ppermute | solution.py:51
  6.6 10.7 %collective-permute-start.3 = (f32[56,256]{1,0:T(8,128)S(1)}, f32[56,256]{1,0:T(8,128)S(1)}, u32[]{:S(2)}, u32[]{:S(2)}) collective-permute-start(f32[56,256]{1,0:T(8,128)S(1)} %pad_maximum_fusion.1), channel_id=1, source_target_pairs={{0,1},{1,0},{2,4},{3,5},{4,2},{5,3},{6,8},{7,9},{8,6},{9,7},{10,12... | collective-permute-start | bytes 172040 | tf_op jit(solution)/shard_map/exchange/ppermute | solution.py:63
  15.0 3.7 %collective-permute-start = (f32[40,256]{1,0:T(8,128)S(1)}, f32[40,256]{1,0:T(8,128)S(1)}, u32[]{:S(2)}, u32[]{:S(2)}) collective-permute-start(f32[40,256]{1,0:T(8,128)S(1)} %get-tuple-element.53), channel_id=1, source_target_pairs={{0,3},{1,2},{2,1},{3,0},{4,7},{5,6},{6,5},{7,4},{8,11},{9,10},{10,... | collective-permute-start | bytes 122888 | tf_op jit(solution)/shard_map/exchange/ppermute | solution.py:51
  17.3 3.1 %collective-permute-start.4 = (f32[8,256]{1,0:T(8,128)S(1)}, f32[8,256]{1,0:T(8,128)S(1)}, u32[]{:S(2)}, u32[]{:S(2)}) collective-permute-start(f32[8,256]{1,0:T(8,128)S(1)} %slice_add_fusion.9), channel_id=1, source_target_pairs={{0,3},{1,2},{2,1},{3,0},{4,7},{5,6},{6,5},{7,4},{8,11},{9,10},{10,... | collective-permute-start | bytes 24584 | tf_op jit(solution)/shard_map/exchange/ppermute | solution.py:51
  20.6 1.4 %collective-permute-start.6 = (f32[112,256]{1,0:T(8,128)S(1)}, f32[112,256]{1,0:T(8,128)S(1)}, u32[]{:S(2)}, u32[]{:S(2)}) collective-permute-start(f32[112,256]{1,0:T(8,128)S(1)} %get-tuple-element.65), channel_id=1, source_target_pairs={{0,1},{1,0},{2,3},{3,2},{4,5},{5,4},{6,7},{7,6},{8,9},{9,8},{10,11... | collective-permute-start | bytes 344072 | tf_op jit(solution)/shard_map/exchange/ppermute | solution.py:46
  21.0 3.1 %collective-permute-start.7 = (f32[8,256]{1,0:T(8,128)S(1)}, f32[8,256]{1,0:T(8,128)S(1)}, u32[]{:S(2)}, u32[]{:S(2)}) collective-permute-start(f32[8,256]{1,0:T(8,128)S(1)} %get-tuple-element.67), channel_id=1, source_target_pairs={{0,3},{1,2},{2,1},{3,0},{4,7},{5,6},{6,5},{7,4},{8,11},{9,10},{10,... | collective-permute-start | bytes 24584 | tf_op jit(solution)/shard_map/exchange/ppermute | solution.py:51
  24.1 8.5 %collective-permute-start.8 = (f32[56,256]{1,0:T(8,128)S(1)}, f32[56,256]{1,0:T(8,128)S(1)}, u32[]{:S(2)}, u32[]{:S(2)}) collective-permute-start(f32[56,256]{1,0:T(8,128)S(1)} %pad_maximum_fusion.2), channel_id=1, source_target_pairs={{0,1},{1,0},{2,4},{3,5},{4,2},{5,3},{6,8},{7,9},{8,6},{9,7},{10,12... | collective-permute-start | bytes 172040 | tf_op jit(solution)/shard_map/exchange/ppermute | solution.py:63
  30.1 3.5 %collective-permute-start.5 = (f32[40,256]{1,0:T(8,128)S(1)}, f32[40,256]{1,0:T(8,128)S(1)}, u32[]{:S(2)}, u32[]{:S(2)}) collective-permute-start(f32[40,256]{1,0:T(8,128)S(1)} %get-tuple-element.64), channel_id=1, source_target_pairs={{0,3},{1,2},{2,1},{3,0},{4,7},{5,6},{6,5},{7,4},{8,11},{9,10},{10,... | collective-permute-start | bytes 122888 | tf_op jit(solution)/shard_map/exchange/ppermute | solution.py:51
  32.6 3.1 %collective-permute-start.9 = (f32[8,256]{1,0:T(8,128)S(1)}, f32[8,256]{1,0:T(8,128)S(1)}, u32[]{:S(2)}, u32[]{:S(2)}) collective-permute-start(f32[8,256]{1,0:T(8,128)S(1)} %slice_add_fusion.6), channel_id=1, source_target_pairs={{0,3},{1,2},{2,1},{3,0},{4,7},{5,6},{6,5},{7,4},{8,11},{9,10},{10,... | collective-permute-start | bytes 24584 | tf_op jit(solution)/shard_map/exchange/ppermute | solution.py:51
  35.8 1.4 %collective-permute-start.11 = (f32[112,256]{1,0:T(8,128)S(1)}, f32[112,256]{1,0:T(8,128)S(1)}, u32[]{:S(2)}, u32[]{:S(2)}) collective-permute-start(f32[112,256]{1,0:T(8,128)S(1)} %get-tuple-element.75), channel_id=1, source_target_pairs={{0,1},{1,0},{2,3},{3,2},{4,5},{5,4},{6,7},{7,6},{8,9},{9,8},{10,11... | collective-permute-start | bytes 344072 | tf_op jit(solution)/shard_map/exchange/ppermute | solution.py:46
  36.0 3.3 %collective-permute-start.12 = (f32[8,256]{1,0:T(8,128)S(1)}, f32[8,256]{1,0:T(8,128)S(1)}, u32[]{:S(2)}, u32[]{:S(2)}) collective-permute-start(f32[8,256]{1,0:T(8,128)S(1)} %get-tuple-element.77), channel_id=1, source_target_pairs={{0,3},{1,2},{2,1},{3,0},{4,7},{5,6},{6,5},{7,4},{8,11},{9,10},{10,... | collective-permute-start | bytes 24584 | tf_op jit(solution)/shard_map/exchange/ppermute | solution.py:51
  39.3 8.5 %collective-permute-start.13 = (f32[56,256]{1,0:T(8,128)S(1)}, f32[56,256]{1,0:T(8,128)S(1)}, u32[]{:S(2)}, u32[]{:S(2)}) collective-permute-start(f32[56,256]{1,0:T(8,128)S(1)} %pad_maximum_fusion.3), channel_id=1, source_target_pairs={{0,1},{1,0},{2,4},{3,5},{4,2},{5,3},{6,8},{7,9},{8,6},{9,7},{10,12... | collective-permute-start | bytes 172040 | tf_op jit(solution)/shard_map/exchange/ppermute | solution.py:63
  45.4 3.7 %collective-permute-start.10 = (f32[40,256]{1,0:T(8,128)S(1)}, f32[40,256]{1,0:T(8,128)S(1)}, u32[]{:S(2)}, u32[]{:S(2)}) collective-permute-start(f32[40,256]{1,0:T(8,128)S(1)} %get-tuple-element.74), channel_id=1, source_target_pairs={{0,3},{1,2},{2,1},{3,0},{4,7},{5,6},{6,5},{7,4},{8,11},{9,10},{10,... | collective-permute-start | bytes 122888 | tf_op jit(solution)/shard_map/exchange/ppermute | solution.py:51
  47.7 3.1 %collective-permute-start.14 = (f32[8,256]{1,0:T(8,128)S(1)}, f32[8,256]{1,0:T(8,128)S(1)}, u32[]{:S(2)}, u32[]{:S(2)}) collective-permute-start(f32[8,256]{1,0:T(8,128)S(1)} %slice_add_fusion.3), channel_id=1, source_target_pairs={{0,3},{1,2},{2,1},{3,0},{4,7},{5,6},{6,5},{7,4},{8,11},{9,10},{10,... | collective-permute-start | bytes 24584 | tf_op jit(solution)/shard_map/exchange/ppermute | solution.py:51
  51.0 1.4 %collective-permute-start.16 = (f32[112,256]{1,0:T(8,128)S(1)}, f32[112,256]{1,0:T(8,128)S(1)}, u32[]{:S(2)}, u32[]{:S(2)}) collective-permute-start(f32[112,256]{1,0:T(8,128)S(1)} %get-tuple-element.85), channel_id=1, source_target_pairs={{0,1},{1,0},{2,3},{3,2},{4,5},{5,4},{6,7},{7,6},{8,9},{9,8},{10,11... | collective-permute-start | bytes 344072 | tf_op jit(solution)/shard_map/exchange/ppermute | solution.py:46
  51.5 3.1 %collective-permute-start.17 = (f32[8,256]{1,0:T(8,128)S(1)}, f32[8,256]{1,0:T(8,128)S(1)}, u32[]{:S(2)}, u32[]{:S(2)}) collective-permute-start(f32[8,256]{1,0:T(8,128)S(1)} %get-tuple-element.87), channel_id=1, source_target_pairs={{0,3},{1,2},{2,1},{3,0},{4,7},{5,6},{6,5},{7,4},{8,11},{9,10},{10,... | collective-permute-start | bytes 24584 | tf_op jit(solution)/shard_map/exchange/ppermute | solution.py:51
  54.6 8.5 %collective-permute-start.18 = (f32[56,256]{1,0:T(8,128)S(1)}, f32[56,256]{1,0:T(8,128)S(1)}, u32[]{:S(2)}, u32[]{:S(2)}) collective-permute-start(f32[56,256]{1,0:T(8,128)S(1)} %pad_maximum_fusion.4), channel_id=1, source_target_pairs={{0,1},{1,0},{2,4},{3,5},{4,2},{5,3},{6,8},{7,9},{8,6},{9,7},{10,12... | collective-permute-start | bytes 172040 | tf_op jit(solution)/shard_map/exchange/ppermute | solution.py:63
  60.5 3.5 %collective-permute-start.15 = (f32[40,256]{1,0:T(8,128)S(1)}, f32[40,256]{1,0:T(8,128)S(1)}, u32[]{:S(2)}, u32[]{:S(2)}) collective-permute-start(f32[40,256]{1,0:T(8,128)S(1)} %get-tuple-element.84), channel_id=1, source_target_pairs={{0,3},{1,2},{2,1},{3,0},{4,7},{5,6},{6,5},{7,4},{8,11},{9,10},{10,... | collective-permute-start | bytes 122888 | tf_op jit(solution)/shard_map/exchange/ppermute | solution.py:51
  63.1 3.1 %collective-permute-start.19 = (f32[8,256]{1,0:T(8,128)S(1)}, f32[8,256]{1,0:T(8,128)S(1)}, u32[]{:S(2)}, u32[]{:S(2)}) collective-permute-start(f32[8,256]{1,0:T(8,128)S(1)} %slice_add_fusion), channel_id=1, source_target_pairs={{0,3},{1,2},{2,1},{3,0},{4,7},{5,6},{6,5},{7,4},{8,11},{9,10},{10,... | collective-permute-start | bytes 24584 | tf_op jit(solution)/shard_map/exchange/ppermute | solution.py:51

commit v2 on v1

--- a/solution.py
+++ b/solution.py
@@ -35,9 +35,13 @@
 pops, edge, plane = 19, 16, 256
 f32, bf16 = jnp.float32, jnp.bfloat16
 
-item_row = (0, 0, 48)
-own_f, mate_f, far_d, loc_d, level_rows = 40, 88, 96, 104, 112
-loc_f, far_f, own_d, kept_rows = 0, 8, 16, 24
+item_row = (0, 0, 56)
+own_f, far_f, mate_f, far_d, loc_d, own_d, level_rows = 40, 48, 96, 104, 112, 120, 128
+kept_loc_f, kept_far_f, kept_own_d, kept_loc_d, kept_rows = 0, 8, 16, 24, 32
+rest_at, rest_rows = 56, 72
+rest_mate_f, rest_far_d, rest_loc_d, rest_own_d = 40, 48, 56, 64
+
+
 at_parent, at_octant, at_prev, at_next = 8, 9, 10, 11
 
 
@@ -90,6 +94,7 @@
 class Table:
     def __init__(self, row):
         codes = [row[0, j] for j in range(3)]
+        self.pair_codes = [row[0, j] for j in range(8, 11)]
         self.valid = [code >= 0 for code in codes]
         self.block = [(code >> 4) & 1 for code in codes]
         self.octant = [(code >> 1) & 7 for code in codes]
@@ -101,14 +106,20 @@
 def make_table(tables, slab, level):
     odd = slab & 1
     row, lane = iota(tables.shape, 0), iota(tables.shape, 1)
-    octant = jnp.where(level == 0, lane, pltpu.roll(tables, 127, 1))
-    here = jnp.where(level == 0, jnp.where(lane < at_parent, 1, 0), jnp.where(lane == at_parent, 1, 0))
-    code = row * 16 + octant * 2 + (tables & 1)
-    code = jnp.where((here == 1) & (row < 2) & (tables >= 0), code, -1)
-    offset = (tables >> 1) - slab
     towards = 1 - 2 * odd
-    values = [jnp.max(jnp.where(offset == d, code, -1)) for d in (towards, -towards, 0)]
+
+    def codes(of_level):
+        octant = jnp.where(of_level == 0, lane, pltpu.roll(tables, 127, 1))
+        coarse, fine = jnp.where(lane < at_parent, 1, 0), jnp.where(lane == at_parent, 1, 0)
+        here = jnp.where(of_level == 0, coarse, fine)
+        code = row * 16 + octant * 2 + (tables & 1)
+        code = jnp.where((here == 1) & (row < 2) & (tables >= 0), code, -1)
+        offset = (tables >> 1) - slab
+        return [jnp.max(jnp.where(offset == d, code, -1)) for d in (towards, -towards, 0)]
+
+    values = codes(level)
     values += [level, odd, tables[0, at_prev], tables[0, at_next], tables[1, at_next]]
+    values += codes(1 - level)
     out = jnp.zeros(tables.shape, jnp.int32)
     for n, value in enumerate(values):
         out = jnp.where(lane == n, value, out)
@@ -116,12 +127,26 @@
 
 
 def pick_matrices(t, j):
-    level, octant = t.level, t.octant[j]
-    source = cell_key(iota((plane, 128), 0), level, octant)
-    pick = ones_where(source == (iota((1, 128), 1) & 63))
-    target = cell_key(iota((1, plane), 1), 1 - level, octant)
+    return coupling_matrices(t.level, t.octant[j])
+
+
+def coupling_matrices(level, octant):
+    y0, z0 = ((octant >> 1) & 1) * 8, (octant & 1) * 8
+
+    def own_cell(y, z):
+        return jnp.where(level == 0, ((y0 + y) << 4) | (z0 + z), (y << 5) | (z << 1))
+
+    cell = iota((plane, 128), 0) & jnp.where(level == 0, 255, 238)
+    item = iota((1, 128), 1) & 63
+    pick = ones_where(cell == own_cell(item >> 3, item & 7))
+    there = iota((1, plane), 1)
+    y, z = there >> 4, there & 15
+    inside = ((y & 8) == y0) & ((z & 8) == z0)
+    to_fine = own_cell(y >> 1, z >> 1)
+    to_coarse = jnp.where(inside, own_cell(y & 7, z & 7), -1)
+    target = jnp.where(level == 0, to_fine, to_coarse)
     place = jnp.concatenate(
-        [ones_where(source == target[:, :128]), ones_where(source == target[:, 128:])], axis=1
+        [ones_where(cell == target[:, :128]), ones_where(cell == target[:, 128:])], axis=1
     )
     return pick, place
 
@@ -142,7 +167,7 @@
         low = alpha_ref[e, 0:1, :] * k_ref[0, 0:1, :]
         high = alpha_ref[pops + w, edge - 1 : edge, :] * k_ref[1, edge - 1 : edge, :]
         lvl_ref[loc_d + i : loc_d + i + 1, :] = jnp.where(odd == 1, low, high)
-        ends_ref[loc_f + i : loc_f + i + 1, :] = jnp.where(odd == 1, high, low)
+        ends_ref[kept_loc_f + i : kept_loc_f + i + 1, :] = jnp.where(odd == 1, high, low)
     for j in range(3):
         base = item_row[j]
         out_ref = item_ref if j == 0 else lvl_ref
@@ -184,20 +209,24 @@
                     )
                 spread = select(rim_scr[...], place) * plane_scale(t)
                 towards_d = other != odd
-                to_d = ((side_ref, 0), (lvl_ref, far_d), (ends_ref, own_d))[j]
-                to_f = ((lvl_ref, mate_f), (ends_ref, far_f), (lvl_ref, own_f))[j]
+                to_d = ((side_ref, 0), (lvl_ref, far_d), (lvl_ref, own_d))[j]
+                to_f = ((lvl_ref, mate_f), (lvl_ref, far_f), (lvl_ref, own_f))[j]
                 for wanted, (ref, row) in ((towards_d, to_d), (other == odd, to_f)):
 
                     @pl.when(wanted)
                     def _(ref=ref, row=row):
                         ref[row : row + 8, :] = spread
 
+    for row, kept in ((far_f, kept_far_f), (own_d, kept_own_d), (loc_d, kept_loc_d)):
+        ends_ref[kept : kept + 8, :] = lvl_ref[row : row + 8, :]
+
 
 def first_pack_kernel(*refs):
-    tables_ref, alpha_ref, d_ref, item_ref, side_ref, lvl_ref, ends_ref, k_ref = refs[:8]
-    scratch = refs[8:]
+    alpha_ref, d_ref, item_ref, side_ref, lvl_ref, ends_ref, k_ref = refs[:7]
+    scratch = refs[7:]
     w_ref = alpha_ref.at[blend_at : blend_at + 2]
-    row = make_table(tables_ref[...], lax.axis_index("slab"), lax.axis_index("lvl"))
+    tables = alpha_ref[tables_at, 0:8, 0:128].astype(jnp.int32)
+    row = make_table(tables, lax.axis_index("slab"), lax.axis_index("lvl"))
     d_ref[...] = row
     t = Table(row)
     level = t.level
@@ -234,11 +263,33 @@
 
 
 def fields_kernel(*refs):
-    d_ref, pop_ref, relax_ref, solid_ref = refs[:4]
-    u_ref, keep_ref, gain_ref, bits_ref, pick_ref, place_ref, pad_scr = refs[4:]
+    d_ref, pop_ref, relax_ref, solid_ref, w_ref, k_ref = refs[:6]
+    u_ref, keep_ref, gain_ref, bits_ref, pick_ref, place_ref = refs[6:12]
+    late_ref, fix_pick_ref, fix_place_ref, pad_scr = refs[12:]
     t = Table(d_ref[...])
     for j in range(3):
         pick_ref[j], place_ref[j] = pick_matrices(t, j)
+
+    def fixes(level, odd, valid, block, octant, other):
+        pick, place = coupling_matrices(level, octant)
+        ox, side = octant >> 2, 1 - odd
+        item = valid & (block == side) & ((level == 1) | (ox == side))
+        end = item & (other == side) & ((level == 0) | (ox == other))
+        scale = jnp.where(level == 0, 0.125, 1.0)
+        pick = (pick.astype(f32) * jnp.where(item, 1.0, 0.0)).astype(bf16)
+        place = (place.astype(f32) * jnp.where(end, scale, 0.0)).astype(bf16)
+        return pick, place
+
+    def of_code(code, level):
+        return fixes(level, t.odd, code >= 0, (code >> 4) & 1, (code >> 1) & 7, code & 1)
+
+    pair = 1 - t.level
+    fix_pick_ref[0], fix_place_ref[0] = of_code(t.pair_codes[1], pair)
+    fix_pick_ref[1], fix_place_ref[1] = of_code(t.pair_codes[2], pair)
+    fix_pick_ref[2], fix_place_ref[2] = fixes(
+        pair, 1 - t.odd, t.valid[0], t.other[0], t.octant[0], t.block[0]
+    )
+    fix_place_ref[3] = fixes(t.level, t.odd, t.valid[2], t.block[2], t.octant[2], t.other[2])[1]
     z = iota((edge, plane), 1) & 15
     for g in range(2):
         solid = solid_ref[g] > 0
@@ -255,12 +306,12 @@
             bits = bits | jnp.where(blocked, 1 << i, 0)
         bits_ref[g] = bits
     steps = pop_ref.shape[0]
-    for t in range(steps):
+    for n in range(steps):
         for g in range(2):
             total = jnp.zeros((edge, plane), f32)
             flow = [jnp.zeros((edge, plane), f32) for _ in range(3)]
             for i in range(pops):
-                f = pop_ref[t, g, i].astype(f32)
+                f = pop_ref[n, g, i].astype(f32)
                 total = total + f
                 for a in range(3):
                     if velocities[i][a] == 1:
@@ -268,7 +319,17 @@
                     elif velocities[i][a] == -1:
                         flow[a] = flow[a] - f
             for a in range(3):
-                u_ref[t, g, a] = flow[a] / total
+                u_ref[n, g, a] = flow[a] / total
+    for is_odd, (g, x) in enumerate(late_layer):
+
+        @pl.when(t.odd == is_odd)
+        def _(is_odd=is_odd, g=g, x=x):
+            link = jnp.where(t.prev if is_odd else t.next, 1.0, 0.0)
+            rows = [u_ref[n, g, a, x : x + 1, :] for n in range(steps) for a in range(3)]
+            rows += [keep_ref[g, x : x + 1, :] * link, gain_ref[g, x : x + 1, :] * link]
+            rows += [w_ref[g, x : x + 1, :], k_ref[g, x : x + 1, :]]
+            for n, row in enumerate(rows):
+                late_ref[n : n + 1, :] = row
 
 
 def collide(pulled, u, keep, gain):
@@ -304,12 +365,69 @@
     return out
 
 
-def step_kernel(*refs, first, last):
-    (d_ref, alpha_ref, k_ref, u_ref, keep_ref, gain_ref, bits_ref) = refs[:7]
-    (mate_ref, lvl_ref, far_ref) = refs[7:10]
-    refs = refs[10:]
+def add_item(t, j, item, half_scr, add):
+    level, g, octant = t.level, t.block[j], t.octant[j]
+    left = iota((40, 128), 1) < 64
+    a, b = item[:, 0:128], item[:, 128:256]
+    parts = [(a, left), (a, ~left), (b, left), (b, ~left)]
+    stacked = jnp.concatenate([jnp.where(m, v, 0.0) for v, m in parts], axis=0)
+    high = stacked.astype(bf16).astype(f32)
+    halves = jnp.concatenate([high, stacked - high], axis=1).astype(bf16)
+    target = cell_key(iota((1, plane), 1), level, octant)
+    matrix = ones_where((iota((plane, plane), 0) & 63) == target)
+    spread = jnp.dot(halves, matrix, preferred_element_type=f32)
+
+    @pl.when(level == 0)
+    def _():
+        first = pl.multiple_of((octant >> 2) * 8, 8)
+        add(g, first, 8, slice(0, plane), spread[0:152].reshape(pops, 8, plane))
+
+    @pl.when(level == 1)
+    def _():
+        for n in range(2):
+            lanes = slice(128 * n, 128 * n + 128)
+            half = spread[:, lanes] * 0.125
+            half_scr[n, pl.ds(0, 160, stride=2), :] = half
+            half_scr[n, pl.ds(1, 160, stride=2), :] = half
+            both = half_scr[n, 0:304, :].reshape(pops, edge, 128)
+            add(g, 0, edge, lanes, both)
+
+
+def before_kernel(*refs, first):
+    (d_ref, alpha_ref, k_ref, mate_ref, rest_ref) = refs[:5]
+    refs = refs[5:]
     if not first:
-        added_ref, refs = refs[0], refs[1:]
+        (added_ref, fix_ref), refs = refs[:2], refs[2:]
+    out_ref, half_scr = refs
+    t = Table(d_ref[...])
+    for g in range(2):
+        block = slice(g * pops, (g + 1) * pops)
+        out_ref[block] = alpha_ref[block] * k_ref[g][None]
+    if not first:
+        for is_odd, (g, x) in enumerate(late_layer):
+
+            @pl.when(t.odd == is_odd)
+            def _(g=g, x=x):
+                kept = k_ref[g, x : x + 1, :]
+                for i in range(pops):
+                    out_ref[g * pops + i, x : x + 1, :] += added_ref[i : i + 1, :] * kept
+
+    def add(g, start, layers, lanes, values):
+        out_ref[pl.ds(g * pops, pops), pl.ds(start, layers), lanes] += values
+
+    @pl.when(t.valid[0])
+    def _():
+        item = mate_ref[...] if first else mate_ref[...] + fix_ref[...]
+        add_item(t, 0, item, half_scr, add)
+
+    @pl.when(t.valid[2])
+    def _():
+        add_item(t, 2, rest_ref[0:40, :], half_scr, add)
+
+
+def step_kernel(*refs, last):
+    (d_ref, before_ref, k_ref, u_ref, keep_ref, gain_ref, bits_ref, lvl_ref, far_ref) = refs[:9]
+    refs = refs[9:]
     if not last:
         (w_ref, pick_ref, place_ref), refs = refs[:3], refs[3:]
         out_ref, *sent, beta_scr, item_scr, rim_scr, half_scr = refs
@@ -318,55 +436,17 @@
     t = Table(d_ref[...])
     level, odd = t.level, t.odd
     for g in range(2):
-        beta_scr[g, :, 8:24, :] = alpha_ref[g * pops : (g + 1) * pops] * k_ref[g][None]
-    if not first:
-        for is_odd, (g, x) in enumerate(late_layer):
-
-            @pl.when(odd == is_odd)
-            def _(g=g, x=x):
-                kept = k_ref[g, x : x + 1, :]
-                for i in range(pops):
-                    beta_scr[g, i, 8 + x : 9 + x, :] += added_ref[i : i + 1, :] * kept
-
-    sources = (mate_ref, far_ref, lvl_ref)
-    for j in range(3):
-        first = item_row[j]
-
-        @pl.when(t.valid[j])
-        def _(j=j, first=first):
-            g, octant = t.block[j], t.octant[j]
-            left = iota((40, 128), 1) < 64
-            a = sources[j][first : first + 40, 0:128]
-            b = sources[j][first : first + 40, 128:256]
-            stacked = jnp.concatenate(
-                [
-                    jnp.where(left, a, 0.0),
-                    jnp.where(left, 0.0, a),
-                    jnp.where(left, b, 0.0),
-                    jnp.where(left, 0.0, b),
-                ],
-                axis=0,
-            )
-            target = cell_key(iota((1, plane), 1), level, octant)
-            spread = select(stacked, ones_where((iota((128, plane), 0) & 63) == target))
-
-            @pl.when(level == 0)
-            def _():
-                rows = pl.ds(pl.multiple_of(8 + (octant >> 2) * 8, 8), 8)
-                beta_scr[g, :, rows, :] += spread[0:152].reshape(pops, 8, plane)
-
-            @pl.when(level == 1)
-            def _():
-                for n in range(2):
-                    lanes = slice(128 * n, 128 * n + 128)
-                    half = spread[:, lanes] * 0.125
-                    half_scr[n, pl.ds(0, 160, stride=2), :] = half
-                    half_scr[n, pl.ds(1, 160, stride=2), :] = half
-                    both = half_scr[n, 0:304, :].reshape(pops, edge, 128)
-                    beta_scr[g, :, 8:24, lanes] += both
-
-    from_d = lvl_ref[mate_f : mate_f + 8, :]
-    from_f = far_ref[40:48, :] + lvl_ref[far_d : far_d + 8, :]
+        beta_scr[g, :, 8:24, :] = before_ref[g * pops : (g + 1) * pops]
+
+    def add(g, start, layers, lanes, values):
+        beta_scr[g, :, pl.ds(8 + start, layers), lanes] += values
+
+    @pl.when(t.valid[1])
+    def _():
+        add_item(t, 1, far_ref[0:40, :], half_scr, add)
+
+    from_d = lvl_ref[rest_mate_f : rest_mate_f + 8, :]
+    from_f = far_ref[40:48, :] + lvl_ref[rest_far_d : rest_far_d + 8, :]
     above = jnp.where(odd == 1, from_f, from_d)
     below = jnp.where(odd == 1, from_d, from_f)
     above = jnp.where(t.next, above, 0.0)
@@ -416,57 +496,90 @@
     return collide(pulled, u, keep_ref[g, rows, :], gain_ref[g, rows, :])
 
 
-def finish_kernel(*refs):
-    (d_ref, late_ref, u_ref, keep_ref, gain_ref, w_ref, k_ref, pick_ref, place_ref) = refs[:9]
-    given, added_ref, sent, rim_scr = refs[9:13], refs[13], refs[14:18], refs[18]
-    item_ref, side_ref, lvl_ref, ends_ref = sent
-    t = Table(d_ref[...])
-    for source, ref in zip(given, sent):
-        ref[...] = source[...]
-    added_ref[...] = jnp.zeros_like(added_ref)
-    rim_scr[...] = jnp.zeros_like(rim_scr)
-
-    def side(is_odd):
-        g, x = late_layer[is_odd]
-        leaving = (west_pops, east_pops)[is_odd]
-        values = late_values(is_odd, late_ref, u_ref, keep_ref, gain_ref)
-        for i in range(pops):
-            added_ref[i : i + 1, :] = values[i]
-        kept, weight = k_ref[g, x : x + 1, :], w_ref[g, x : x + 1, :]
-        for n, i in enumerate(leaving):
-            lvl_ref[loc_d + n : loc_d + n + 1, :] += values[i] * kept
-            rim_scr[n : n + 1, :] = values[i] * weight
-        weighted = added_ref[...] * weight
-        left = iota((1, 128), 1) < 64
-        at_row = iota((8, plane), 0) == (0 if is_odd else 7)
-        for j in range(3):
-            base = item_row[j]
-            out_ref = item_ref if j == 0 else lvl_ref
-            other, ox = t.other[j], t.octant[j] >> 2
-            inside = (t.level == 1) | (ox == 1 - is_odd)
-
-            @pl.when(t.valid[j] & (t.block[j] == g) & inside)
-            def _(j=j, base=base, out_ref=out_ref, ox=ox, other=other):
-                picked = select(weighted, pick_ref[j])
-                for n in range(5):
-                    a, b, c, d = (picked[m : m + 1] for m in (n, 5 + n, 10 + n, 15 + n))
-                    row = jnp.concatenate([jnp.where(left, a, b), jnp.where(left, c, d)], axis=1)
-                    tile = slice(base + 8 * n, base + 8 * n + 8)
-                    out_ref[tile, :] += jnp.where(at_row, row, 0.0)
-
-                @pl.when((other == 1 - is_odd) & ((t.level == 0) | (ox == other)))
-                def _():
-                    spread = select(rim_scr[...], place_ref[j]) * plane_scale(t)
-                    ref, row = ((side_ref, 0), (lvl_ref, far_d), (ends_ref, own_d))[j]
-                    ref[row : row + 8, :] += spread
-
-    @pl.when((t.odd == 0) & t.next)
-    def _():
-        side(0)
-
-    @pl.when((t.odd == 1) & t.prev)
-    def _():
-        side(1)
+def late_share(late, fields, step, odd):
+    z = iota((8, plane), 1) & 15
+    pulled = [0.0] * pops
+    for n in range(5):
+        e, w = east_pops[n], west_pops[n]
+        pulled[e] = jnp.where(odd == 0, moved_cells(late, velocities[e], z)[n : n + 1], 0.0)
+        pulled[w] = jnp.where(odd == 0, 0.0, moved_cells(late, velocities[w], z)[n : n + 1])
+    u = [fields[3 * step + a : 3 * step + a + 1] for a in range(3)]
+    return collide(pulled, u, fields[12:13], fields[13:14])
+
+
+def leaving(values, odd, scr):
+    for n in range(5):
+        e, w = east_pops[n], west_pops[n]
+        scr[n : n + 1, :] = jnp.where(odd == 0, values[w], values[e])
+    return scr[...]
+
+
+def item_share(weighted, pick, odd, ref, base):
+    picked = select(weighted, pick)
+    left = iota((1, 128), 1) < 64
+    at_row = iota((8, plane), 0) == jnp.where(odd == 0, 7, 0)
+    for n in range(5):
+        a, b, c, d = (picked[m : m + 1] for m in (n, 5 + n, 10 + n, 15 + n))
+        row = jnp.concatenate([jnp.where(left, a, b), jnp.where(left, c, d)], axis=1)
+        tile = slice(base + 8 * n, base + 8 * n + 8)
+        ref[tile, :] += jnp.where(at_row, row, 0.0)
+
+
+def clear(*refs):
+    for ref in refs:
+        ref[...] = jnp.zeros_like(ref)
+
+
+def far_message_kernel(*refs, step):
+    (got_ref, planes_ref, lvl_ref, ends_ref, pair_ref, mate_ref, pick_ref, place_ref) = refs[:8]
+    out_ref, all_scr, rim_scr = refs[8:]
+    odd = lax.axis_index("slab") & 1
+    clear(all_scr, rim_scr)
+    out_ref[0:40, :] = lvl_ref[0:40, :]
+    fields = pair_ref[...]
+    values = late_share(got_ref[8:16, :], fields, step, odd)
+    for i in range(pops):
+        all_scr[i : i + 1, :] = values[i]
+    item_share(all_scr[...] * fields[14:15], pick_ref[0], odd, out_ref, 0)
+    fields = mate_ref[...]
+    values = late_share(planes_ref[0:8, :], fields, step, 1 - odd)
+    share = select(leaving(values, 1 - odd, rim_scr) * fields[14:15], place_ref[2])
+    end = lvl_ref[own_f : own_f + 8, :] + ends_ref[kept_loc_f : kept_loc_f + 8, :]
+    out_ref[40:48, :] = end + got_ref[16:24, :] + share
+    out_ref[48:56, :] = lvl_ref[far_f : far_f + 8, :]
+    out_ref[56:64, :] = ends_ref[kept_far_f : kept_far_f + 8, :]
+
+
+def shares_kernel(*refs, step):
+    (got_ref, planes_ref, lvl_ref, ends_ref, own_ref, pair_ref, mate_ref) = refs[:7]
+    (pick_ref, place_ref) = refs[7:9]
+    rest_ref, kept_ref, added_ref, fix_ref, all_scr, rim_scr = refs[9:]
+    odd = lax.axis_index("slab") & 1
+    clear(all_scr, rim_scr, added_ref, fix_ref)
+    rest_ref[...] = lvl_ref[rest_at:level_rows, :]
+    kept_ref[...] = ends_ref[kept_own_d:kept_rows, :]
+    fields = pair_ref[...]
+    values = late_share(got_ref[8:16, :], fields, step, odd)
+    for i in range(pops):
+        all_scr[i : i + 1, :] = values[i]
+    item_share(all_scr[...] * fields[14:15], pick_ref[1], odd, rest_ref, 0)
+    rim = leaving(values, odd, rim_scr)
+    rest_ref[rest_loc_d : rest_loc_d + 8, :] += rim * fields[15:16]
+    rim = rim * fields[14:15]
+    rest_ref[rest_far_d : rest_far_d + 8, :] += select(rim, place_ref[0])
+    rest_ref[rest_own_d : rest_own_d + 8, :] += select(rim, place_ref[1])
+    fields = own_ref[...]
+    values = late_share(got_ref[0:8, :], fields, step, odd)
+    for i in range(pops):
+        added_ref[i : i + 1, :] = values[i]
+    rim = leaving(values, odd, rim_scr)
+    kept_ref[8:16, :] += rim * fields[15:16]
+    kept_ref[0:8, :] += select(rim * fields[14:15], place_ref[3])
+    fields = mate_ref[...]
+    values = late_share(planes_ref[0:8, :], fields, step, 1 - odd)
+    for i in range(pops):
+        all_scr[i : i + 1, :] = values[i]
+    item_share(all_scr[...] * fields[14:15], pick_ref[2], 1 - odd, fix_ref, 0)
 
 
 def last_kernel(d_ref, alpha_ref, late_ref, u_ref, keep_ref, gain_ref, out_ref, tile_scr, sems):
@@ -517,9 +630,11 @@
 half_scratch = [pltpu.VMEM((2, 320, 128), f32)]
 pack_scratch = [pltpu.VMEM((160, plane), f32), pltpu.VMEM((8, plane), f32)] + half_scratch
 messages = [shape(rows, plane) for rows in (40, 8, level_rows, kept_rows)]
+share_scratch = [pltpu.VMEM((24, plane), f32), pltpu.VMEM((8, plane), f32)]
 field = shape(2, edge, plane)
 state = shape(2 * pops, edge, plane)
 blend_at = 2 * pops
+tables_at = blend_at + 2
 
 
 def hbm():
@@ -547,18 +662,28 @@
     adjoint_final, populations, relaxation, blend, solid, chain, parent, children, *, slabs
 ):
     steps = populations.shape[0]
-    alpha = jnp.concatenate([adjoint_final.reshape(2 * pops, edge, plane), blend[0]], axis=0)
-    tables = jnp.concatenate([children, parent, chain[0]], axis=1)
-    tables = jnp.pad(tables, ((0, 6), (0, 116)), constant_values=-1)
+    tables = jnp.concatenate([children, parent, chain[0]], axis=1).astype(f32)
+    tables = jnp.pad(tables, ((0, edge - 2), (0, plane - 12)), constant_values=-1.0)
+    alpha = jnp.concatenate(
+        [adjoint_final.reshape(2 * pops, edge, plane), blend[0], tables[None]], axis=0
+    )
     table, *sent, kept = call(
         first_pack_kernel,
         [shape(8, 128, dtype=jnp.int32)] + messages + [field],
-        (tables, alpha),
+        (alpha,),
         pack_scratch,
         "pack_first",
     )
-    weights = alpha[blend_at:]
-    flows, keep, gain, bits, pick, place = call(
+    weights = alpha[blend_at:tables_at]
+    with jax.named_scope("exchange"):
+        item, side, lvl, ends = sent
+        lvl = level_swap(lvl, slabs)
+        side = mate_swap(side, slabs, 1)
+        end = lvl[own_f : own_f + 8] + ends[kept_loc_f : kept_loc_f + 8] + side
+        parts = [lvl[0:40], end, lvl[far_f : far_f + 8], ends[kept_far_f : kept_far_f + 8]]
+        message = jnp.concatenate(parts, axis=0)
+        rest, kept_d = lvl[rest_at:], ends[kept_own_d:]
+    flows, keep, gain, bits, pick, place, own_late, fix_pick, fix_place = call(
         fields_kernel,
         [
             shape(steps, 2, 3, edge, plane),
@@ -567,33 +692,39 @@
             shape(2, edge, plane, dtype=jnp.int32),
             shape(3, plane, 128, dtype=bf16),
             shape(3, plane, plane, dtype=bf16),
+            shape(16, plane),
+            shape(3, plane, 128, dtype=bf16),
+            shape(4, plane, plane, dtype=bf16),
         ],
-        (table, populations[:, 0], relaxation[0], solid[0]),
+        (table, populations[:, 0], relaxation[0], solid[0], weights, kept),
         [pltpu.VMEM((32, plane), f32)],
         "flow_fields",
         estimate=cost(4_000_000, 2_000_000),
     )
-    added = None
+    shares = []
     for t in range(steps - 1, -1, -1):
         first, last = t == steps - 1, t == 0
         u = flows[t]
-        near, side, lvl, ends = sent
         with jax.named_scope("exchange"):
-            lvl = level_swap(lvl, slabs)
-            side = mate_swap(side, slabs, 1)
-            end = lvl[own_f : own_f + 8] + ends[loc_f : loc_f + 8] + side
-            far = jnp.concatenate([lvl[0:40], end, ends[far_f : far_f + 8]], axis=0)
-            far = far_swap(far, slabs)
-            mate = mate_swap(near, slabs, 1)
-            end = lvl[loc_d : loc_d + 8] + ends[own_d : own_d + 8] + far[48:56]
-            late = mate_swap(end, slabs, 1)
-        ins = [table, alpha, kept, u, keep, gain, bits, mate, lvl, far]
-        if not first:
-            ins += [added]
+            far = far_swap(message, slabs)
+            mate = mate_swap(item, slabs, 1)
+            pair_end = rest[rest_loc_d : rest_loc_d + 8] + kept_d[0:8] + far[56:64]
+            own_end = kept_d[8:16] + rest[rest_own_d : rest_own_d + 8] + far[48:56]
+            if last:
+                late = mate_swap(pair_end, slabs, 1)
+        before = call(
+            functools.partial(before_kernel, first=first),
+            [state],
+            (table, alpha, kept, mate, rest, *shares),
+            half_scratch,
+            "before",
+            estimate=cost(4_000_000, 2_000_000),
+        )[0]
+        ins = [table, before, kept, u, keep, gain, bits, rest, far]
         if not last:
             ins += [weights, pick, place]
         got = call(
-            functools.partial(step_kernel, first=first, last=last),
+            functools.partial(step_kernel, last=last),
             [state] + ([] if last else messages),
             ins,
             [pltpu.VMEM((2, pops, 32, plane), f32)] + (half_scratch if last else pack_scratch),
@@ -610,14 +741,33 @@
                 "finish",
                 out_specs=[hbm()],
             )[0]
-        else:
-            added, *sent = call(
-                finish_kernel,
-                [shape(24, plane)] + messages,
-                (table, late, u, keep, gain, weights, kept, pick, place, *got[1:]),
-                [pltpu.VMEM((8, plane), f32)],
-                "finish",
-            )
+            continue
+        item, side, lvl, ends = got[1:]
+        with jax.named_scope("exchange"):
+            planes = jnp.concatenate([pair_end, own_end], axis=0)
+            parts = [planes, side]
+            if first:
+                lvl = jnp.concatenate([lvl, own_late], axis=0)
+                parts += [own_late]
+            lvl = level_swap(lvl, slabs)
+            late = mate_swap(jnp.concatenate(parts, axis=0), slabs, 1)
+            if first:
+                pair_late, mate_late = lvl[level_rows:], late[24:40]
+        message = call(
+            functools.partial(far_message_kernel, step=t),
+            [shape(64, plane)],
+            (late, planes, lvl, ends, pair_late, mate_late, fix_pick, fix_place),
+            share_scratch,
+            "far_message",
+        )[0]
+        rest, kept_d, *shares = call(
+            functools.partial(shares_kernel, step=t),
+            [shape(rest_rows, plane), shape(16, plane), shape(24, plane), shape(40, plane)],
+            (late, planes, lvl, ends, own_late, pair_late, mate_late, fix_pick, fix_place),
+            share_scratch,
+            "shares",
+            estimate=cost(2_000_000, 500_000),
+        )
     return alpha.reshape(1, 2, pops, edge, plane)
 
 

time: 68.5 us -> 65.7 us (0.959); the launches traced: 67.2 us -> 66.4 us
  waiting for transfers between devices: 25.7 us -> 23.8 us
  starting transfers between devices: 29.6 us -> 30.4 us
    ppermute x12 -> x9, waiting for transfers between devices: 14.1 us -> 18.7 us  [mate_swap(): return lax.ppermute(value, axes, pairs)]
    ppermute x4, waiting for transfers between devices: 8.97 us -> 5.14 us  [far_swap(): return lax.ppermute(value, axes, pairs)]
    ppermute x4, waiting for transfers between devices: 2.6 us -> 0.01 us  [level_swap(): return lax.ppermute(value, axes, pairs)]
    ppermute x4, starting transfers between devices: 26.4 us -> 27.8 us  [far_swap(): return lax.ppermute(value, axes, pairs)]
    convert_element_type x0 -> x1, other arithmetic: none -> 0.89 us  [local(): tables = jnp.concatenate([children, parent, chain[0]], axis=1).astype(f32)]
    concatenate x6 -> x9, other arithmetic: 2.06 us -> 1.2 us  [the longest x1 1.14 us: local(): jnp.concatenate([adjoint_final.reshape(2 * pops, edge, plane), blend[0],...]
    pallas_call x10 -> x17, Pallas kernels: 9.44 us -> 9.54 us  [call(): pl.pallas_call(kernel, out_shape=outs, in_specs=[vmem()] * len(ins), out_...]
    ppermute x12 -> x9, starting transfers between devices: 2.19 us -> 2.12 us  [mate_swap(): return lax.ppermute(value, axes, pairs)]
  transfers between devices with their start and end apart: 20 -> 17, of which waited for: 19 -> 10; matrix products, arithmetic and copies ran while one was open for 0% -> 0% of each run, Pallas kernels for 10% -> 5%
where the time goes in v2:
time: 65.7 us; the launch traced here: 66.4 us
  starting transfers between devices  30.4 us (46%)
  waiting for transfers between devices  23.8 us (36%)
  Pallas kernels  9.54 us (15%)
  other arithmetic  2.12 us (3%)
    ppermute x4, starting transfers between devices, far_swap(): return lax.ppermute(value, axes, pairs)  27.8 us
    ppermute x9, waiting for transfers between devices, mate_swap(): return lax.ppermute(value, axes, pairs)  18.7 us
    pallas_call x17, Pallas kernels, call(): pl.pallas_call(kernel, out_shape=outs, in_specs=[vmem()] * len(ins), out_...  9.54 us
    ppermute x4, waiting for transfers between devices, far_swap(): return lax.ppermute(value, axes, pairs)  5.14 us
    ppermute x9, starting transfers between devices, mate_swap(): return lax.ppermute(value, axes, pairs)  2.12 us
  transfers between devices with their start and end apart: 17, of which 10 were waited for; matrix products, arithmetic and copies ran while one was open for 0% of the time, Pallas kernels for 5%

profile of v2, /device:TPU:6, one launch (start us, length us, event | category | flops | bytes accessed | tf_op | source)
XLA Modules:
  0.0 66.4 jit_solution(6969212738473534965)
XLA Ops:
  0.0 0.9 %add_convert_fusion = f32[2,12]{1,0:T(2,128)S(1)} fusion(s32[2,2]{1,0:T(2,128)} %bitcast.26, s32[2,2]{1,0:T(2,128)} %param.14, s32[2,8]{1,0:T(2,128)} %param.15), kind=kLoop, calls=%fused_computation.25 | loop fusion | flops 72 | bytes 192 | tf_op jit(solution)/shard_map/convert_element_type | solution.py:665
  0.9 1.1 %pad_maximum_fusion.refs_0_.refs_1_ = f32[41,16,256]{2,1,0:T(8,128)S(1)} fusion(f32[1,16,256]{2,1,0:T(8,128)S(1)} %pad_bitcast_fusion, f32[2,16,256]{2,1,0:T(8,128)} %bitcast.18, f32[38,16,256]{2,1,0:T(8,128)} %bitcast.25), kind=kLoop, calls=%fused_computation | loop fusion | flops 335872 | bytes 1343488 | tf_op jit(solution)/shard_map/concatenate | solution.py:667
  2.1 0.9 %pack_first.1 = (s32[8,128]{1,0:T(8,128)S(1)}, f32[40,256]{1,0:T(8,128)S(1)}, f32[8,256]{1,0:T(8,128)S(1)}, f32[128,256]{1,0:T(8,128)S(1)}, f32[32,256]{1,0:T(8,128)S(1)}, /*index=5*/f32[2,16,256]{2,1,0:T(8,128)S(1)}) custom-call(f32[41,16,256]{2,1,0:T(8,128)S(1)} %pad_maximum_fusion.refs_0_.refs_1_), custom_call_target="tpu_custom_call" | custom-call | tf_op jit(solution)/shard_map/pack_first/pallas_call | solution.py:650
  2.9 1.4 %collective-permute-start.2 = (f32[8,256]{1,0:T(8,128)S(1)}, f32[8,256]{1,0:T(8,128)S(1)}, u32[]{:S(2)}, u32[]{:S(2)}) collective-permute-start(f32[8,256]{1,0:T(8,128)S(1)} %get-tuple-element.56), channel_id=1, source_target_pairs={{0,3},{1,2},{2,1},{3,0},{4,7},{5,6},{6,5},{7,4},{8,11},{9,10},{10,... | collective-permute-start | bytes 24584 | tf_op jit(solution)/shard_map/exchange/ppermute | solution.py:55
  4.8 0.9 %flow_fields.1 = (f32[4,2,3,16,256]{4,3,2,1,0:T(8,128)S(1)}, f32[2,16,256]{2,1,0:T(8,128)S(1)}, f32[2,16,256]{2,1,0:T(8,128)S(1)}, s32[2,16,256]{2,1,0:T(8,128)S...) custom-call(s32[8,128]{1,0:T(8,128)S(1)} %get-tuple-element.47.refs_, ...), custom_call_target="tpu_custom_call" | custom-call | flops 4000000 | bytes 2000000 | tf_op jit(solution)/shard_map/flow_fields/pallas_call | solution.py:650
  6.1 9.4 %collective-permute-start.3 = (f32[64,256]{1,0:T(8,128)S(1)}, f32[64,256]{1,0:T(8,128)S(1)}, u32[]{:S(2)}, u32[]{:S(2)}) collective-permute-start(f32[64,256]{1,0:T(8,128)S(1)} %pad_maximum_fusion.2), channel_id=1, source_target_pairs={{0,1},{1,0},{2,4},{3,5},{4,2},{5,3},{6,8},{7,9},{8,6},{9,7},{10,12... | collective-permute-start | bytes 196616 | tf_op jit(solution)/shard_map/exchange/ppermute | solution.py:67
  15.7 2.6 %collective-permute-done.3.refs_8_ = f32[64,256]{1,0:T(8,128)S(1)} collective-permute-done((f32[64,256]{1,0:T(8,128)S(1)}, f32[64,256]{1,0:T(8,128)S(1)}, u32[]{:S(2)}, u32[]{:S(2)}) %collective-permute-start.3) | collective-permute-done | bytes 65568 | tf_op jit(solution)/shard_map/exchange/ppermute | solution.py:67
  18.4 1.1 %step.4 = (f32[38,16,256]{2,1,0:T(8,128)S(1)}, f32[40,256]{1,0:T(8,128)S(1)}, f32[8,256]{1,0:T(8,128)S(1)}, f32[128,256]{1,0:T(8,128)S(1)}, f32[32,256]{1,0:T(8,128)S(1)}) custom-call(s32[8,128]{1,0:T(8,128)S(1)} %get-tuple-element.47.refs_0_.d_ref, f32[38,16,256]{2,1,0:T(8,128)S(1)} %before.4.refs_1_, f32[2,16,256]{2,1,0:T(8,128)S(1)} %get-tuple-element.48.refs_2_.refs_5_, ...), custom_call_target="tpu_custom_call" | custom-call | flops 8000000 | bytes 2000000 | tf_op jit(solution)/shard_map/step/pallas_call | solution.py:650
  19.8 3.4 %collective-permute-done.5.refs_0_ = f32[40,256]{1,0:T(8,128)S(1)} collective-permute-done((f32[40,256]{1,0:T(8,128)S(1)}, f32[40,256]{1,0:T(8,128)S(1)}, u32[]{:S(2)}, u32[]{:S(2)}) %collective-permute-start.5) | collective-permute-done | bytes 40992 | tf_op jit(solution)/shard_map/exchange/ppermute | solution.py:55
  23.5 7.0 %collective-permute-start.7 = (f32[64,256]{1,0:T(8,128)S(1)}, f32[64,256]{1,0:T(8,128)S(1)}, u32[]{:S(2)}, u32[]{:S(2)}) collective-permute-start(f32[64,256]{1,0:T(8,128)S(1)} %far_message.3), channel_id=1, source_target_pairs={{0,1},{1,0},{2,4},{3,5},{4,2},{5,3},{6,8},{7,9},{8,6},{9,7},{10,12... | collective-permute-start | bytes 196616 | tf_op jit(solution)/shard_map/exchange/ppermute | solution.py:67
  31.0 3.1 %collective-permute-done.4.refs_3_ = f32[40,256]{1,0:T(8,128)S(1)} collective-permute-done((f32[40,256]{1,0:T(8,128)S(1)}, f32[40,256]{1,0:T(8,128)S(1)}, u32[]{:S(2)}, u32[]{:S(2)}) %collective-permute-start.4) | collective-permute-done | bytes 40992 | tf_op jit(solution)/shard_map/exchange/ppermute | solution.py:55
  34.3 1.1 %step.5 = (f32[38,16,256]{2,1,0:T(8,128)S(1)}, f32[40,256]{1,0:T(8,128)S(1)}, f32[8,256]{1,0:T(8,128)S(1)}, f32[128,256]{1,0:T(8,128)S(1)}, f32[32,256]{1,0:T(8,128)S(1)}) custom-call(s32[8,128]{1,0:T(8,128)S(1)} %get-tuple-element.47.refs_0_.d_ref, f32[38,16,256]{2,1,0:T(8,128)S(1)} %before.5.refs_1_, f32[2,16,256]{2,1,0:T(8,128)S(1)} %get-tuple-element.48.refs_2_.refs_5_, ...), custom_call_target="tpu_custom_call" | custom-call | flops 8000000 | bytes 2000000 | tf_op jit(solution)/shard_map/step/pallas_call | solution.py:650
  35.7 3.2 %collective-permute-done.9.refs_0_ = f32[24,256]{1,0:T(8,128)S(1)} collective-permute-done((f32[24,256]{1,0:T(8,128)S(1)}, f32[24,256]{1,0:T(8,128)S(1)}, u32[]{:S(2)}, u32[]{:S(2)}) %collective-permute-start.9) | collective-permute-done | bytes 24608 | tf_op jit(solution)/shard_map/exchange/ppermute | solution.py:55
  39.2 5.7 %collective-permute-start.11 = (f32[64,256]{1,0:T(8,128)S(1)}, f32[64,256]{1,0:T(8,128)S(1)}, u32[]{:S(2)}, u32[]{:S(2)}) collective-permute-start(f32[64,256]{1,0:T(8,128)S(1)} %far_message.4), channel_id=1, source_target_pairs={{0,1},{1,0},{2,4},{3,5},{4,2},{5,3},{6,8},{7,9},{8,6},{9,7},{10,12... | collective-permute-start | bytes 196616 | tf_op jit(solution)/shard_map/exchange/ppermute | solution.py:67
  44.9 0.5 shares.4
  45.4 3.1 %collective-permute-done.8.refs_3_ = f32[40,256]{1,0:T(8,128)S(1)} collective-permute-done((f32[40,256]{1,0:T(8,128)S(1)}, f32[40,256]{1,0:T(8,128)S(1)}, u32[]{:S(2)}, u32[]{:S(2)}) %collective-permute-start.8) | collective-permute-done | bytes 40992 | tf_op jit(solution)/shard_map/exchange/ppermute | solution.py:55
  48.6 1.1 %step.6 = (f32[38,16,256]{2,1,0:T(8,128)S(1)}, f32[40,256]{1,0:T(8,128)S(1)}, f32[8,256]{1,0:T(8,128)S(1)}, f32[128,256]{1,0:T(8,128)S(1)}, f32[32,256]{1,0:T(8,128)S(1)}) custom-call(s32[8,128]{1,0:T(8,128)S(1)} %get-tuple-element.47.refs_0_.d_ref, f32[38,16,256]{2,1,0:T(8,128)S(1)} %before.6.refs_1_, f32[2,16,256]{2,1,0:T(8,128)S(1)} %get-tuple-element.48.refs_2_.refs_5_, ...), custom_call_target="tpu_custom_call" | custom-call | flops 8000000 | bytes 2000000 | tf_op jit(solution)/shard_map/step/pallas_call | solution.py:650
  50.0 3.2 %collective-permute-done.13.refs_0_ = f32[24,256]{1,0:T(8,128)S(1)} collective-permute-done((f32[24,256]{1,0:T(8,128)S(1)}, f32[24,256]{1,0:T(8,128)S(1)}, u32[]{:S(2)}, u32[]{:S(2)}) %collective-permute-start.13) | collective-permute-done | bytes 24608 | tf_op jit(solution)/shard_map/exchange/ppermute | solution.py:55
  53.6 5.7 %collective-permute-start.15 = (f32[64,256]{1,0:T(8,128)S(1)}, f32[64,256]{1,0:T(8,128)S(1)}, u32[]{:S(2)}, u32[]{:S(2)}) collective-permute-start(f32[64,256]{1,0:T(8,128)S(1)} %far_message.5), channel_id=1, source_target_pairs={{0,1},{1,0},{2,4},{3,5},{4,2},{5,3},{6,8},{7,9},{8,6},{9,7},{10,12... | collective-permute-start | bytes 196616 | tf_op jit(solution)/shard_map/exchange/ppermute | solution.py:67
  59.7 2.5 %collective-permute-done.15.refs_8_ = f32[64,256]{1,0:T(8,128)S(1)} collective-permute-done((f32[64,256]{1,0:T(8,128)S(1)}, f32[64,256]{1,0:T(8,128)S(1)}, u32[]{:S(2)}, u32[]{:S(2)}) %collective-permute-start.15) | collective-permute-done | bytes 65568 | tf_op jit(solution)/shard_map/exchange/ppermute | solution.py:67
  62.2 0.6 collective-permute-done.12.refs_3_
  63.0 0.7 %step.7.alpha_ref = f32[38,16,256]{2,1,0:T(8,128)S(1)} custom-call(s32[8,128]{1,0:T(8,128)S(1)} %get-tuple-element.47.refs_0_.d_ref, f32[38,16,256]{2,1,0:T(8,128)S(1)} %before.7.refs_1_, f32[2,16,256]{2,1,0:T(8,128)S(1)} %get-tuple-element.48.refs_2_.refs_5_, f32[2,3,16,256]{3,2,1,0:T(8,128)S(1)} %get-tuple-element.89.refs_3_.u_ref, ...), custom_call_target="tpu_custom_call" | custom-call | flops 8000000 | bytes 2000000 | tf_op jit(solution)/shard_map/step/pallas_call | solution.py:650
  63.7 1.6 %collective-permute-done.16.late_ref = f32[8,256]{1,0:T(8,128)S(1)} collective-permute-done((f32[8,256]{1,0:T(8,128)S(1)}, f32[8,256]{1,0:T(8,128)S(1)}, u32[]{:S(2)}, u32[]{:S(2)}) %collective-permute-start.16) | collective-permute-done | bytes 8224 | tf_op jit(solution)/shard_map/exchange/ppermute | solution.py:55
  65.3 0.9 %finish.1 = f32[38,16,256]{2,1,0:T(8,128)} custom-call(s32[8,128]{1,0:T(8,128)S(1)} %get-tuple-element.47.refs_0_.d_ref, f32[38,16,256]{2,1,0:T(8,128)S(1)} %step.7.alpha_ref, f32[8,256]{1,0:T(8,128)S(1)} %collective-permute-done.16.late_ref, f32[2,3,16,256]{3,2,1,0:T(8,128)S(1)} %get-tuple-element.89.refs_3_.u_ref, ...), custom_call_target="tpu_custom_call" | custom-call | tf_op jit(solution)/shard_map/finish/pallas_call | solution.py:650
  (56 shorter events, 4.2 us)
Async XLA Ops:
  0.0 4.8 %copy-start.1 = (f32[1,2,16,256]{3,2,1,0:T(8,128)S(1)}, f32[1,2,16,256]{3,2,1,0:T(8,128)}, u32[]{:S(2)}) copy-start(f32[1,2,16,256]{3,2,1,0:T(8,128)} %param.11) | copy-start | bytes 98308
  0.0 4.8 %copy-start.3 = (s32[1,2,16,256]{3,2,1,0:T(8,128)S(1)}, s32[1,2,16,256]{3,2,1,0:T(8,128)}, u32[]{:S(2)}) copy-start(s32[1,2,16,256]{3,2,1,0:T(8,128)} %param.12) | copy-start | bytes 98308
  0.0 4.8 %copy-start.2 = (f32[1,2,16,256]{3,2,1,0:T(8,128)S(1)}, f32[1,2,16,256]{3,2,1,0:T(8,128)}, u32[]{:S(2)}) copy-start(f32[1,2,16,256]{3,2,1,0:T(8,128)} %param.10) | copy-start | bytes 98308
  0.0 4.8 %copy-start = (bf16[4,1,2,19,16,256]{5,4,3,2,1,0:T(8,128)(2,1)S(1)}, bf16[4,1,2,19,16,256]{5,4,3,2,1,0:T(8,128)(2,1)}, u32[]{:S(2)}) copy-start(bf16[4,1,2,19,16,256]{5,4,3,2,1,0:T(8,128)(2,1)} %param.9) | copy-start | bytes 3735556
  2.9 2.8 %collective-permute-start.1 = (f32[128,256]{1,0:T(8,128)S(1)}, f32[128,256]{1,0:T(8,128)S(1)}, u32[]{:S(2)}, u32[]{:S(2)}) collective-permute-start(f32[128,256]{1,0:T(8,128)S(1)} %get-tuple-element.50), channel_id=1, source_target_pairs={{0,1},{1,0},{2,3},{3,2},{4,5},{5,4},{6,7},{7,6},{8,9},{9,8},{10,11... | collective-permute-start | bytes 393224 | tf_op jit(solution)/shard_map/exchange/ppermute | solution.py:50
  2.9 3.2 %collective-permute-start.2 = (f32[8,256]{1,0:T(8,128)S(1)}, f32[8,256]{1,0:T(8,128)S(1)}, u32[]{:S(2)}, u32[]{:S(2)}) collective-permute-start(f32[8,256]{1,0:T(8,128)S(1)} %get-tuple-element.56), channel_id=1, source_target_pairs={{0,3},{1,2},{2,1},{3,0},{4,7},{5,6},{6,5},{7,4},{8,11},{9,10},{10,... | collective-permute-start | bytes 24584 | tf_op jit(solution)/shard_map/exchange/ppermute | solution.py:55
  4.3 11.2 %collective-permute-start = (f32[40,256]{1,0:T(8,128)S(1)}, f32[40,256]{1,0:T(8,128)S(1)}, u32[]{:S(2)}, u32[]{:S(2)}) collective-permute-start(f32[40,256]{1,0:T(8,128)S(1)} %get-tuple-element.49), channel_id=1, source_target_pairs={{0,3},{1,2},{2,1},{3,0},{4,7},{5,6},{6,5},{7,4},{8,11},{9,10},{10,... | collective-permute-start | bytes 122888 | tf_op jit(solution)/shard_map/exchange/ppermute | solution.py:55
  6.1 12.3 %collective-permute-start.3 = (f32[64,256]{1,0:T(8,128)S(1)}, f32[64,256]{1,0:T(8,128)S(1)}, u32[]{:S(2)}, u32[]{:S(2)}) collective-permute-start(f32[64,256]{1,0:T(8,128)S(1)} %pad_maximum_fusion.2), channel_id=1, source_target_pairs={{0,1},{1,0},{2,4},{3,5},{4,2},{5,3},{6,8},{7,9},{8,6},{9,7},{10,12... | collective-permute-start | bytes 196616 | tf_op jit(solution)/shard_map/exchange/ppermute | solution.py:67
  19.5 3.7 %collective-permute-start.6 = (f32[144,256]{1,0:T(8,128)S(1)}, f32[144,256]{1,0:T(8,128)S(1)}, u32[]{:S(2)}, u32[]{:S(2)}) collective-permute-start(f32[144,256]{1,0:T(8,128)S(1)} %pad_maximum_fusion.1), channel_id=1, source_target_pairs={{0,1},{1,0},{2,3},{3,2},{4,5},{5,4},{6,7},{7,6},{8,9},{9,8},{10,11... | collective-permute-start | bytes 442376 | tf_op jit(solution)/shard_map/exchange/ppermute | solution.py:50
  19.7 3.5 %collective-permute-start.5 = (f32[40,256]{1,0:T(8,128)S(1)}, f32[40,256]{1,0:T(8,128)S(1)}, u32[]{:S(2)}, u32[]{:S(2)}) collective-permute-start(f32[40,256]{1,0:T(8,128)S(1)} %pad_maximum_fusion.3), channel_id=1, source_target_pairs={{0,3},{1,2},{2,1},{3,0},{4,7},{5,6},{6,5},{7,4},{8,11},{9,10},{10,... | collective-permute-start | bytes 122888 | tf_op jit(solution)/shard_map/exchange/ppermute | solution.py:55
  23.5 10.7 %collective-permute-start.7 = (f32[64,256]{1,0:T(8,128)S(1)}, f32[64,256]{1,0:T(8,128)S(1)}, u32[]{:S(2)}, u32[]{:S(2)}) collective-permute-start(f32[64,256]{1,0:T(8,128)S(1)} %far_message.3), channel_id=1, source_target_pairs={{0,1},{1,0},{2,4},{3,5},{4,2},{5,3},{6,8},{7,9},{8,6},{9,7},{10,12... | collective-permute-start | bytes 196616 | tf_op jit(solution)/shard_map/exchange/ppermute | solution.py:67
  30.5 3.6 %collective-permute-start.4 = (f32[40,256]{1,0:T(8,128)S(1)}, f32[40,256]{1,0:T(8,128)S(1)}, u32[]{:S(2)}, u32[]{:S(2)}) collective-permute-start(f32[40,256]{1,0:T(8,128)S(1)} %get-tuple-element.60), channel_id=1, source_target_pairs={{0,3},{1,2},{2,1},{3,0},{4,7},{5,6},{6,5},{7,4},{8,11},{9,10},{10,... | collective-permute-start | bytes 122888 | tf_op jit(solution)/shard_map/exchange/ppermute | solution.py:55
  35.4 3.5 %collective-permute-start.10 = (f32[128,256]{1,0:T(8,128)S(1)}, f32[128,256]{1,0:T(8,128)S(1)}, u32[]{:S(2)}, u32[]{:S(2)}) collective-permute-start(f32[128,256]{1,0:T(8,128)S(1)} %get-tuple-element.74), channel_id=1, source_target_pairs={{0,1},{1,0},{2,3},{3,2},{4,5},{5,4},{6,7},{7,6},{8,9},{9,8},{10,11... | collective-permute-start | bytes 393224 | tf_op jit(solution)/shard_map/exchange/ppermute | solution.py:50
  35.5 3.4 %collective-permute-start.9 = (f32[24,256]{1,0:T(8,128)S(1)}, f32[24,256]{1,0:T(8,128)S(1)}, u32[]{:S(2)}, u32[]{:S(2)}) collective-permute-start(f32[24,256]{1,0:T(8,128)S(1)} %pad_maximum_fusion.4), channel_id=1, source_target_pairs={{0,3},{1,2},{2,1},{3,0},{4,7},{5,6},{6,5},{7,4},{8,11},{9,10},{10,... | collective-permute-start | bytes 73736 | tf_op jit(solution)/shard_map/exchange/ppermute | solution.py:55
  39.2 9.4 %collective-permute-start.11 = (f32[64,256]{1,0:T(8,128)S(1)}, f32[64,256]{1,0:T(8,128)S(1)}, u32[]{:S(2)}, u32[]{:S(2)}) collective-permute-start(f32[64,256]{1,0:T(8,128)S(1)} %far_message.4), channel_id=1, source_target_pairs={{0,1},{1,0},{2,4},{3,5},{4,2},{5,3},{6,8},{7,9},{8,6},{9,7},{10,12... | collective-permute-start | bytes 196616 | tf_op jit(solution)/shard_map/exchange/ppermute | solution.py:67
  44.9 3.6 %collective-permute-start.8 = (f32[40,256]{1,0:T(8,128)S(1)}, f32[40,256]{1,0:T(8,128)S(1)}, u32[]{:S(2)}, u32[]{:S(2)}) collective-permute-start(f32[40,256]{1,0:T(8,128)S(1)} %get-tuple-element.71), channel_id=1, source_target_pairs={{0,3},{1,2},{2,1},{3,0},{4,7},{5,6},{6,5},{7,4},{8,11},{9,10},{10,... | collective-permute-start | bytes 122888 | tf_op jit(solution)/shard_map/exchange/ppermute | solution.py:55
  49.7 3.5 %collective-permute-start.14 = (f32[128,256]{1,0:T(8,128)S(1)}, f32[128,256]{1,0:T(8,128)S(1)}, u32[]{:S(2)}, u32[]{:S(2)}) collective-permute-start(f32[128,256]{1,0:T(8,128)S(1)} %get-tuple-element.83), channel_id=1, source_target_pairs={{0,1},{1,0},{2,3},{3,2},{4,5},{5,4},{6,7},{7,6},{8,9},{9,8},{10,11... | collective-permute-start | bytes 393224 | tf_op jit(solution)/shard_map/exchange/ppermute | solution.py:50
  49.9 3.3 %collective-permute-start.13 = (f32[24,256]{1,0:T(8,128)S(1)}, f32[24,256]{1,0:T(8,128)S(1)}, u32[]{:S(2)}, u32[]{:S(2)}) collective-permute-start(f32[24,256]{1,0:T(8,128)S(1)} %pad_maximum_fusion.5), channel_id=1, source_target_pairs={{0,3},{1,2},{2,1},{3,0},{4,7},{5,6},{6,5},{7,4},{8,11},{9,10},{10,... | collective-permute-start | bytes 73736 | tf_op jit(solution)/shard_map/exchange/ppermute | solution.py:55
  53.6 8.7 %collective-permute-start.15 = (f32[64,256]{1,0:T(8,128)S(1)}, f32[64,256]{1,0:T(8,128)S(1)}, u32[]{:S(2)}, u32[]{:S(2)}) collective-permute-start(f32[64,256]{1,0:T(8,128)S(1)} %far_message.5), channel_id=1, source_target_pairs={{0,1},{1,0},{2,4},{3,5},{4,2},{5,3},{6,8},{7,9},{8,6},{9,7},{10,12... | collective-permute-start | bytes 196616 | tf_op jit(solution)/shard_map/exchange/ppermute | solution.py:67
  59.3 3.6 %collective-permute-start.12 = (f32[40,256]{1,0:T(8,128)S(1)}, f32[40,256]{1,0:T(8,128)S(1)}, u32[]{:S(2)}, u32[]{:S(2)}) collective-permute-start(f32[40,256]{1,0:T(8,128)S(1)} %get-tuple-element.80), channel_id=1, source_target_pairs={{0,3},{1,2},{2,1},{3,0},{4,7},{5,6},{6,5},{7,4},{8,11},{9,10},{10,... | collective-permute-start | bytes 122888 | tf_op jit(solution)/shard_map/exchange/ppermute | solution.py:55
  62.2 3.1 %collective-permute-start.16 = (f32[8,256]{1,0:T(8,128)S(1)}, f32[8,256]{1,0:T(8,128)S(1)}, u32[]{:S(2)}, u32[]{:S(2)}) collective-permute-start(f32[8,256]{1,0:T(8,128)S(1)} %slice_add_fusion), channel_id=1, source_target_pairs={{0,3},{1,2},{2,1},{3,0},{4,7},{5,6},{6,5},{7,4},{8,11},{9,10},{10,... | collective-permute-start | bytes 24584 | tf_op jit(solution)/shard_map/exchange/ppermute | solution.py:55

commit v3 on v2

--- a/solution.py
+++ b/solution.py
@@ -159,7 +159,8 @@
     item_scr, rim_scr, half_scr = scratch
     level, odd = t.level, t.odd
     for ref in (item_ref, side_ref, lvl_ref, ends_ref):
-        ref[...] = jnp.zeros_like(ref)
+        if ref is not None:
+            ref[...] = jnp.zeros_like(ref)
     item_scr[152:160, :] = jnp.zeros((8, plane), f32)
     rim_scr[...] = jnp.zeros_like(rim_scr)
     for i in range(5):
@@ -212,6 +213,8 @@
                 to_d = ((side_ref, 0), (lvl_ref, far_d), (lvl_ref, own_d))[j]
                 to_f = ((lvl_ref, mate_f), (lvl_ref, far_f), (lvl_ref, own_f))[j]
                 for wanted, (ref, row) in ((towards_d, to_d), (other == odd, to_f)):
+                    if ref is None:
+                        continue
 
                     @pl.when(wanted)
                     def _(ref=ref, row=row):
@@ -429,8 +432,8 @@
     (d_ref, before_ref, k_ref, u_ref, keep_ref, gain_ref, bits_ref, lvl_ref, far_ref) = refs[:9]
     refs = refs[9:]
     if not last:
-        (w_ref, pick_ref, place_ref), refs = refs[:3], refs[3:]
-        out_ref, *sent, beta_scr, item_scr, rim_scr, half_scr = refs
+        (w_ref, place_ref), refs = refs[:2], refs[2:]
+        out_ref, side_ref, beta_scr, rim_scr, half_scr = refs
     else:
         out_ref, beta_scr, half_scr = refs
     t = Table(d_ref[...])
@@ -476,9 +479,40 @@
             for i in range(pops):
                 out_ref[g * pops + i, rows, :] = done[i]
     if not last:
-        scratch = (item_scr, rim_scr, half_scr)
-        matrices = lambda j: (pick_ref[j], place_ref[j])
-        pack(t, out_ref, w_ref, k_ref, *sent, scratch, matrices)
+        side_plane(t, out_ref, w_ref, place_ref[0], side_ref, rim_scr)
+
+
+def side_plane(t, alpha_ref, w_ref, place, side_ref, rim_scr):
+    clear(side_ref, rim_scr)
+    level, odd = t.level, t.odd
+    g, other, ox = t.block[0], t.other[0], t.octant[0] >> 2
+    x = jnp.where(other == 1, 7, 0)
+
+    def rows(layer):
+        weight = w_ref[g, pl.ds(layer, 1), :]
+        for i in range(5):
+            pop = jnp.where(other == 1, west_pops[i], east_pops[i])
+            rim_scr[i : i + 1, :] += alpha_ref[g * pops + pop, pl.ds(layer, 1), :] * weight
+
+    @pl.when(t.valid[0] & (other != odd) & ((level == 0) | (ox == other)))
+    def _():
+        @pl.when(level == 0)
+        def _():
+            rows(ox * 8 + x)
+
+        @pl.when(level == 1)
+        def _():
+            rows(2 * x)
+            rows(2 * x + 1)
+
+        side_ref[...] = select(rim_scr[...], place) * plane_scale(t)
+
+
+def pack_kernel(*refs):
+    d_ref, alpha_ref, w_ref, k_ref, pick_ref, place_ref, item_ref, lvl_ref, ends_ref = refs[:9]
+    matrices = lambda j: (pick_ref[j], place_ref[j])
+    t = Table(d_ref[...])
+    pack(t, alpha_ref, w_ref, k_ref, item_ref, None, lvl_ref, ends_ref, refs[9:], matrices)
 
 
 late_layer = ((1, edge - 1), (0, 0))
@@ -530,24 +564,20 @@
         ref[...] = jnp.zeros_like(ref)
 
 
-def far_message_kernel(*refs, step):
-    (got_ref, planes_ref, lvl_ref, ends_ref, pair_ref, mate_ref, pick_ref, place_ref) = refs[:8]
-    out_ref, all_scr, rim_scr = refs[8:]
+def far_shares_kernel(*refs, step):
+    (got_ref, planes_ref, pair_ref, mate_ref, pick_ref, place_ref) = refs[:6]
+    out_ref, all_scr, rim_scr = refs[6:]
     odd = lax.axis_index("slab") & 1
-    clear(all_scr, rim_scr)
-    out_ref[0:40, :] = lvl_ref[0:40, :]
+    clear(out_ref, all_scr, rim_scr)
     fields = pair_ref[...]
-    values = late_share(got_ref[8:16, :], fields, step, odd)
+    values = late_share(got_ref[5:13, :], fields, step, odd)
     for i in range(pops):
         all_scr[i : i + 1, :] = values[i]
     item_share(all_scr[...] * fields[14:15], pick_ref[0], odd, out_ref, 0)
     fields = mate_ref[...]
     values = late_share(planes_ref[0:8, :], fields, step, 1 - odd)
     share = select(leaving(values, 1 - odd, rim_scr) * fields[14:15], place_ref[2])
-    end = lvl_ref[own_f : own_f + 8, :] + ends_ref[kept_loc_f : kept_loc_f + 8, :]
-    out_ref[40:48, :] = end + got_ref[16:24, :] + share
-    out_ref[48:56, :] = lvl_ref[far_f : far_f + 8, :]
-    out_ref[56:64, :] = ends_ref[kept_far_f : kept_far_f + 8, :]
+    out_ref[40:45, :] = got_ref[10:15, :] + share[0:5]
 
 
 def shares_kernel(*refs, step):
@@ -559,7 +589,7 @@
     rest_ref[...] = lvl_ref[rest_at:level_rows, :]
     kept_ref[...] = ends_ref[kept_own_d:kept_rows, :]
     fields = pair_ref[...]
-    values = late_share(got_ref[8:16, :], fields, step, odd)
+    values = late_share(got_ref[5:13, :], fields, step, odd)
     for i in range(pops):
         all_scr[i : i + 1, :] = values[i]
     item_share(all_scr[...] * fields[14:15], pick_ref[1], odd, rest_ref, 0)
@@ -656,6 +686,12 @@
             compiler_params=params,
             cost_estimate=estimate,
         )(*ins)
+
+
+def far_message(lvl, ends, side, share=0.0):
+    end = lvl[own_f : own_f + 5] + ends[kept_loc_f : kept_loc_f + 5] + side
+    parts = [lvl[0:40] + share, end, lvl[far_f : far_f + 5], ends[kept_far_f : kept_far_f + 5]]
+    return jnp.pad(jnp.concatenate(parts, axis=0), ((0, 1), (0, 0)))
 
 
 def local(
@@ -679,9 +715,7 @@
         item, side, lvl, ends = sent
         lvl = level_swap(lvl, slabs)
         side = mate_swap(side, slabs, 1)
-        end = lvl[own_f : own_f + 8] + ends[kept_loc_f : kept_loc_f + 8] + side
-        parts = [lvl[0:40], end, lvl[far_f : far_f + 8], ends[kept_far_f : kept_far_f + 8]]
-        message = jnp.concatenate(parts, axis=0)
+        message = far_message(lvl, ends, side[0:5])
         rest, kept_d = lvl[rest_at:], ends[kept_own_d:]
     flows, keep, gain, bits, pick, place, own_late, fix_pick, fix_place = call(
         fields_kernel,
@@ -708,10 +742,10 @@
         with jax.named_scope("exchange"):
             far = far_swap(message, slabs)
             mate = mate_swap(item, slabs, 1)
-            pair_end = rest[rest_loc_d : rest_loc_d + 8] + kept_d[0:8] + far[56:64]
-            own_end = kept_d[8:16] + rest[rest_own_d : rest_own_d + 8] + far[48:56]
+            pair_end = rest[rest_loc_d : rest_loc_d + 5] + kept_d[0:5] + far[50:55]
+            own_end = kept_d[8:13] + rest[rest_own_d : rest_own_d + 5] + far[45:50]
             if last:
-                late = mate_swap(pair_end, slabs, 1)
+                late = mate_swap(jnp.pad(pair_end, ((0, 3), (0, 0))), slabs, 1)
         before = call(
             functools.partial(before_kernel, first=first),
             [state],
@@ -722,12 +756,14 @@
         )[0]
         ins = [table, before, kept, u, keep, gain, bits, rest, far]
         if not last:
-            ins += [weights, pick, place]
+            ins += [weights, place]
         got = call(
             functools.partial(step_kernel, last=last),
-            [state] + ([] if last else messages),
+            [state] + ([] if last else [shape(8, plane)]),
             ins,
-            [pltpu.VMEM((2, pops, 32, plane), f32)] + (half_scratch if last else pack_scratch),
+            [pltpu.VMEM((2, pops, 32, plane), f32)]
+            + ([] if last else [pltpu.VMEM((8, plane), f32)])
+            + half_scratch,
             "step",
             estimate=cost(8_000_000, 2_000_000),
         )
@@ -742,24 +778,33 @@
                 out_specs=[hbm()],
             )[0]
             continue
-        item, side, lvl, ends = got[1:]
         with jax.named_scope("exchange"):
-            planes = jnp.concatenate([pair_end, own_end], axis=0)
-            parts = [planes, side]
+            planes = jnp.concatenate([pair_end, own_end, got[1][0:5]], axis=0)
+            planes = jnp.pad(planes, ((0, 1), (0, 0)))
             if first:
-                lvl = jnp.concatenate([lvl, own_late], axis=0)
-                parts += [own_late]
+                planes = jnp.concatenate([planes, own_late], axis=0)
+            late = mate_swap(planes, slabs, 1)
+        item, lvl, ends = call(
+            pack_kernel,
+            [messages[0], messages[2], messages[3]],
+            (table, alpha, weights, kept, pick, place),
+            pack_scratch,
+            "pack",
+            estimate=cost(8_000_000, 2_000_000),
+        )
+        with jax.named_scope("exchange"):
             lvl = level_swap(lvl, slabs)
-            late = mate_swap(jnp.concatenate(parts, axis=0), slabs, 1)
             if first:
-                pair_late, mate_late = lvl[level_rows:], late[24:40]
-        message = call(
-            functools.partial(far_message_kernel, step=t),
-            [shape(64, plane)],
-            (late, planes, lvl, ends, pair_late, mate_late, fix_pick, fix_place),
+                pair_late, mate_late = level_swap(own_late, slabs), late[16:32]
+        more = call(
+            functools.partial(far_shares_kernel, step=t),
+            [shape(48, plane)],
+            (late, planes, pair_late, mate_late, fix_pick, fix_place),
             share_scratch,
-            "far_message",
+            "far_shares",
+            estimate=cost(40_000_000_000, 4_000_000),
         )[0]
+        message = far_message(lvl, ends, more[40:45], more[0:40])
         rest, kept_d, *shares = call(
             functools.partial(shares_kernel, step=t),
             [shape(rest_rows, plane), shape(16, plane), shape(24, plane), shape(40, plane)],

time: 65.7 us -> 63.5 us (0.967)
  starting transfers between devices: 30.4 us -> 27 us
  Pallas kernels: 9.54 us -> 12 us
  waiting for transfers between devices: 23.8 us -> 21.8 us
    ppermute x4, starting transfers between devices: 27.8 us -> 24.5 us  [far_swap(): return lax.ppermute(value, axes, pairs)]
    ppermute x9, waiting for transfers between devices: 18.7 us -> 15.7 us  [mate_swap(): return lax.ppermute(value, axes, pairs)]
    pallas_call x17 -> x20, Pallas kernels: 9.54 us -> 12 us  [call(): pl.pallas_call(kernel, out_shape=outs, in_specs=[vmem()] * len(ins), out_...]
    ppermute x4, waiting for transfers between devices: 5.14 us -> 6.04 us  [far_swap(): return lax.ppermute(value, axes, pairs)]
  transfers between devices with their start and end apart: 17 -> 18, of which waited for: 10 -> 10; matrix products, arithmetic and copies ran while one was open for 0% -> 0% of each run, Pallas kernels for 5% -> 12%
where the time goes in v3:
time: 63.5 us; the launch traced here: 63.6 us
  starting transfers between devices  27 us (43%)
  waiting for transfers between devices  21.8 us (34%)
  Pallas kernels  12 us (19%)
  other arithmetic  2.21 us (3%)
    ppermute x4, starting transfers between devices, far_swap(): return lax.ppermute(value, axes, pairs)  24.5 us
    ppermute x9, waiting for transfers between devices, mate_swap(): return lax.ppermute(value, axes, pairs)  15.7 us
    pallas_call x20, Pallas kernels, call(): pl.pallas_call(kernel, out_shape=outs, in_specs=[vmem()] * len(ins), out_...  12 us
    ppermute x4, waiting for transfers between devices, far_swap(): return lax.ppermute(value, axes, pairs)  6.04 us
    ppermute x9, starting transfers between devices, mate_swap(): return lax.ppermute(value, axes, pairs)  2.21 us
  transfers between devices with their start and end apart: 18, of which 10 were waited for; matrix products, arithmetic and copies ran while one was open for 0% of the time, Pallas kernels for 12%

profile of v3, /device:TPU:6, one launch (start us, length us, event | category | flops | bytes accessed | tf_op | source)
XLA Modules:
  0.0 63.6 jit_solution(414685742270066226)
XLA Ops:
  0.0 0.9 %add_convert_fusion = f32[2,12]{1,0:T(2,128)S(1)} fusion(s32[2,2]{1,0:T(2,128)} %bitcast.35, s32[2,2]{1,0:T(2,128)} %param.14, s32[2,8]{1,0:T(2,128)} %param.15), kind=kLoop, calls=%fused_computation.47 | loop fusion | flops 72 | bytes 192 | tf_op jit(solution)/shard_map/convert_element_type | solution.py:701
  0.9 1.1 %pad_maximum_fusion.refs_0_.refs_1_ = f32[41,16,256]{2,1,0:T(8,128)S(1)} fusion(f32[1,16,256]{2,1,0:T(8,128)S(1)} %pad_bitcast_fusion, f32[2,16,256]{2,1,0:T(8,128)} %bitcast.20, f32[38,16,256]{2,1,0:T(8,128)} %bitcast.34), kind=kLoop, calls=%fused_computation | loop fusion | flops 335872 | bytes 1343488 | tf_op jit(solution)/shard_map/concatenate | solution.py:703
  2.1 1.2 %pack_first.1 = (s32[8,128]{1,0:T(8,128)S(1)}, f32[40,256]{1,0:T(8,128)S(1)}, f32[8,256]{1,0:T(8,128)S(1)}, f32[128,256]{1,0:T(8,128)S(1)}, f32[32,256]{1,0:T(8,128)S(1)}, /*index=5*/f32[2,16,256]{2,1,0:T(8,128)S(1)}) custom-call(f32[41,16,256]{2,1,0:T(8,128)S(1)} %pad_maximum_fusion.refs_0_.refs_1_), custom_call_target="tpu_custom_call" | custom-call | tf_op jit(solution)/shard_map/pack_first/pallas_call | solution.py:680
  3.3 1.0 %collective-permute-start.2 = (f32[8,256]{1,0:T(8,128)S(1)}, f32[8,256]{1,0:T(8,128)S(1)}, u32[]{:S(2)}, u32[]{:S(2)}) collective-permute-start(f32[8,256]{1,0:T(8,128)S(1)} %get-tuple-element.56), channel_id=1, source_target_pairs={{0,3},{1,2},{2,1},{3,0},{4,7},{5,6},{6,5},{7,4},{8,11},{9,10},{10,... | collective-permute-start | bytes 24584 | tf_op jit(solution)/shard_map/exchange/ppermute | solution.py:55
  4.3 0.8 %collective-permute-start = (f32[40,256]{1,0:T(8,128)S(1)}, f32[40,256]{1,0:T(8,128)S(1)}, u32[]{:S(2)}, u32[]{:S(2)}) collective-permute-start(f32[40,256]{1,0:T(8,128)S(1)} %get-tuple-element.49), channel_id=1, source_target_pairs={{0,3},{1,2},{2,1},{3,0},{4,7},{5,6},{6,5},{7,4},{8,11},{9,10},{10,... | collective-permute-start | bytes 122888 | tf_op jit(solution)/shard_map/exchange/ppermute | solution.py:55
  5.2 0.9 %flow_fields.1 = (f32[4,2,3,16,256]{4,3,2,1,0:T(8,128)S(1)}, f32[2,16,256]{2,1,0:T(8,128)S(1)}, f32[2,16,256]{2,1,0:T(8,128)S(1)}, s32[2,16,256]{2,1,0:T(8,128)S...) custom-call(s32[8,128]{1,0:T(8,128)S(1)} %get-tuple-element.47.refs_, ...), custom_call_target="tpu_custom_call" | custom-call | flops 4000000 | bytes 2000000 | tf_op jit(solution)/shard_map/flow_fields/pallas_call | solution.py:680
  6.5 9.0 %collective-permute-start.3 = (f32[56,256]{1,0:T(8,128)S(1)}, f32[56,256]{1,0:T(8,128)S(1)}, u32[]{:S(2)}, u32[]{:S(2)}) collective-permute-start(f32[56,256]{1,0:T(8,128)S(1)} %select_maximum_fusion.9), channel_id=1, source_target_pairs={{0,1},{1,0},{2,4},{3,5},{4,2},{5,3},{6,8},{7,9},{8,6},{9,7},{10,12... | collective-permute-start | bytes 172040 | tf_op jit(solution)/shard_map/exchange/ppermute | solution.py:67
  15.9 2.3 %collective-permute-done.3.refs_8_ = f32[56,256]{1,0:T(8,128)S(1)} collective-permute-done((f32[56,256]{1,0:T(8,128)S(1)}, f32[56,256]{1,0:T(8,128)S(1)}, u32[]{:S(2)}, u32[]{:S(2)}) %collective-permute-start.3) | collective-permute-done | bytes 57376 | tf_op jit(solution)/shard_map/exchange/ppermute | solution.py:67
  19.2 0.9 %pack.3 = (f32[40,256]{1,0:T(8,128)S(1)}, f32[128,256]{1,0:T(8,128)S(1)}, f32[32,256]{1,0:T(8,128)S(1)}) custom-call(s32[8,128]{1,0:T(8,128)S(1)} %get-tuple-element.47.refs_0_.d_ref, f32[38,16,256]{2,1,0:T(8,128)S(1)} %get-tuple-element.58.refs_1_, f32[2,16,256]{2,1,0:T(8,128)S(1)} %bitcast.23, f32[2,16,256]{2,1,0:T(8,128)S(1)} %get-tuple-element.48.refs_2_.refs_5_.refs_3_, ...), custom_call_target="tpu_custom_call" | custom-call | flops 8000000 | bytes 2000000 | tf_op jit(solution)/shard_map/pack/pallas_call | solution.py:680
  20.1 2.4 %collective-permute-done.5.refs_0_ = f32[32,256]{1,0:T(8,128)S(1)} collective-permute-done((f32[32,256]{1,0:T(8,128)S(1)}, f32[32,256]{1,0:T(8,128)S(1)}, u32[]{:S(2)}, u32[]{:S(2)}) %collective-permute-start.5) | collective-permute-done | bytes 32800 | tf_op jit(solution)/shard_map/exchange/ppermute | solution.py:55
  22.9 6.3 %collective-permute-start.8 = (f32[56,256]{1,0:T(8,128)S(1)}, f32[56,256]{1,0:T(8,128)S(1)}, u32[]{:S(2)}, u32[]{:S(2)}) collective-permute-start(f32[56,256]{1,0:T(8,128)S(1)} %select_maximum_fusion.6), channel_id=1, source_target_pairs={{0,1},{1,0},{2,4},{3,5},{4,2},{5,3},{6,8},{7,9},{8,6},{9,7},{10,12... | collective-permute-start | bytes 172040 | tf_op jit(solution)/shard_map/exchange/ppermute | solution.py:67
  29.7 3.3 %collective-permute-done.4.refs_3_ = f32[40,256]{1,0:T(8,128)S(1)} collective-permute-done((f32[40,256]{1,0:T(8,128)S(1)}, f32[40,256]{1,0:T(8,128)S(1)}, u32[]{:S(2)}, u32[]{:S(2)}) %collective-permute-start.4) | collective-permute-done | bytes 40992 | tf_op jit(solution)/shard_map/exchange/ppermute | solution.py:55
  33.3 0.7 %step.5 = (f32[38,16,256]{2,1,0:T(8,128)S(1)}, f32[8,256]{1,0:T(8,128)S(1)}) custom-call(s32[8,128]{1,0:T(8,128)S(1)} %get-tuple-element.47.refs_0_.d_ref, f32[38,16,256]{2,1,0:T(8,128)S(1)} %before.5.refs_1_, f32[2,16,256]{2,1,0:T(8,128)S(1)} %get-tuple-element.48.refs_2_.refs_5_.refs_3_, f32[2,3,16,256]{3,2,1,0:T(8,128)S(1)} %get-tuple-element.91.refs_3_, ...), custom_call_target="tpu_custom_call" | custom-call | flops 8000000 | bytes 2000000 | tf_op jit(solution)/shard_map/step/pallas_call | solution.py:680
  34.1 0.9 %pack.4 = (f32[40,256]{1,0:T(8,128)S(1)}, f32[128,256]{1,0:T(8,128)S(1)}, f32[32,256]{1,0:T(8,128)S(1)}) custom-call(s32[8,128]{1,0:T(8,128)S(1)} %get-tuple-element.47.refs_0_.d_ref, f32[38,16,256]{2,1,0:T(8,128)S(1)} %get-tuple-element.70.refs_1_, f32[2,16,256]{2,1,0:T(8,128)S(1)} %bitcast.25, f32[2,16,256]{2,1,0:T(8,128)S(1)} %get-tuple-element.48.refs_2_.refs_5_.refs_3_, ...), custom_call_target="tpu_custom_call" | custom-call | flops 8000000 | bytes 2000000 | tf_op jit(solution)/shard_map/pack/pallas_call | solution.py:680
  35.0 2.4 %collective-permute-done.10.refs_0_ = f32[16,256]{1,0:T(8,128)S(1)} collective-permute-done((f32[16,256]{1,0:T(8,128)S(1)}, f32[16,256]{1,0:T(8,128)S(1)}, u32[]{:S(2)}, u32[]{:S(2)}) %collective-permute-start.10) | collective-permute-done | bytes 16416 | tf_op jit(solution)/shard_map/exchange/ppermute | solution.py:55
  37.8 4.6 %collective-permute-start.12 = (f32[56,256]{1,0:T(8,128)S(1)}, f32[56,256]{1,0:T(8,128)S(1)}, u32[]{:S(2)}, u32[]{:S(2)}) collective-permute-start(f32[56,256]{1,0:T(8,128)S(1)} %select_maximum_fusion.3), channel_id=1, source_target_pairs={{0,1},{1,0},{2,4},{3,5},{4,2},{5,3},{6,8},{7,9},{8,6},{9,7},{10,12... | collective-permute-start | bytes 172040 | tf_op jit(solution)/shard_map/exchange/ppermute | solution.py:67
  42.9 3.0 %collective-permute-done.9.refs_3_ = f32[40,256]{1,0:T(8,128)S(1)} collective-permute-done((f32[40,256]{1,0:T(8,128)S(1)}, f32[40,256]{1,0:T(8,128)S(1)}, u32[]{:S(2)}, u32[]{:S(2)}) %collective-permute-start.9) | collective-permute-done | bytes 40992 | tf_op jit(solution)/shard_map/exchange/ppermute | solution.py:55
  47.3 0.9 %pack.5 = (f32[40,256]{1,0:T(8,128)S(1)}, f32[128,256]{1,0:T(8,128)S(1)}, f32[32,256]{1,0:T(8,128)S(1)}) custom-call(s32[8,128]{1,0:T(8,128)S(1)} %get-tuple-element.47.refs_0_.d_ref, f32[38,16,256]{2,1,0:T(8,128)S(1)} %get-tuple-element.79.refs_1_, f32[2,16,256]{2,1,0:T(8,128)S(1)} %bitcast.27, f32[2,16,256]{2,1,0:T(8,128)S(1)} %get-tuple-element.48.refs_2_.refs_5_.refs_3_, ...), custom_call_target="tpu_custom_call" | custom-call | flops 8000000 | bytes 2000000 | tf_op jit(solution)/shard_map/pack/pallas_call | solution.py:680
  48.2 2.3 %collective-permute-done.14.refs_0_ = f32[16,256]{1,0:T(8,128)S(1)} collective-permute-done((f32[16,256]{1,0:T(8,128)S(1)}, f32[16,256]{1,0:T(8,128)S(1)}, u32[]{:S(2)}, u32[]{:S(2)}) %collective-permute-start.14) | collective-permute-done | bytes 16416 | tf_op jit(solution)/shard_map/exchange/ppermute | solution.py:55
  50.8 4.6 %collective-permute-start.16 = (f32[56,256]{1,0:T(8,128)S(1)}, f32[56,256]{1,0:T(8,128)S(1)}, u32[]{:S(2)}, u32[]{:S(2)}) collective-permute-start(f32[56,256]{1,0:T(8,128)S(1)} %select_maximum_fusion), channel_id=1, source_target_pairs={{0,1},{1,0},{2,4},{3,5},{4,2},{5,3},{6,8},{7,9},{8,6},{9,7},{10,12... | collective-permute-start | bytes 172040 | tf_op jit(solution)/shard_map/exchange/ppermute | solution.py:67
  55.9 3.4 %collective-permute-done.16.refs_8_ = f32[56,256]{1,0:T(8,128)S(1)} collective-permute-done((f32[56,256]{1,0:T(8,128)S(1)}, f32[56,256]{1,0:T(8,128)S(1)}, u32[]{:S(2)}, u32[]{:S(2)}) %collective-permute-start.16) | collective-permute-done | bytes 57376 | tf_op jit(solution)/shard_map/exchange/ppermute | solution.py:67
  59.8 0.7 %step.7.alpha_ref = f32[38,16,256]{2,1,0:T(8,128)S(1)} custom-call(s32[8,128]{1,0:T(8,128)S(1)} %get-tuple-element.47.refs_0_.d_ref, f32[38,16,256]{2,1,0:T(8,128)S(1)} %before.7.refs_1_, f32[2,16,256]{2,1,0:T(8,128)S(1)} %get-tuple-element.48.refs_2_.refs_5_.refs_3_, f32[2,3,16,256]{3,2,1,0:T(8,128)S(1)} %get-tuple-element.89.refs_3_.u_ref, ...), custom_call_target="tpu_custom_call" | custom-call | flops 8000000 | bytes 2000000 | tf_op jit(solution)/shard_map/step/pallas_call | solution.py:680
  60.5 2.0 %collective-permute-done.17.late_ref = f32[8,256]{1,0:T(8,128)S(1)} collective-permute-done((f32[8,256]{1,0:T(8,128)S(1)}, f32[8,256]{1,0:T(8,128)S(1)}, u32[]{:S(2)}, u32[]{:S(2)}) %collective-permute-start.17) | collective-permute-done | bytes 8224 | tf_op jit(solution)/shard_map/exchange/ppermute | solution.py:55
  62.5 0.9 %finish.1 = f32[38,16,256]{2,1,0:T(8,128)} custom-call(s32[8,128]{1,0:T(8,128)S(1)} %get-tuple-element.47.refs_0_.d_ref, f32[38,16,256]{2,1,0:T(8,128)S(1)} %step.7.alpha_ref, f32[8,256]{1,0:T(8,128)S(1)} %collective-permute-done.17.late_ref, f32[2,3,16,256]{3,2,1,0:T(8,128)S(1)} %get-tuple-element.89.refs_3_.u_ref, ...), custom_call_target="tpu_custom_call" | custom-call | tf_op jit(solution)/shard_map/finish/pallas_call | solution.py:680
  (67 shorter events, 6.6 us)
Async XLA Ops:
  0.0 5.2 %copy-start = (f32[1,2,16,256]{3,2,1,0:T(8,128)S(1)}, f32[1,2,16,256]{3,2,1,0:T(8,128)}, u32[]{:S(2)}) copy-start(f32[1,2,16,256]{3,2,1,0:T(8,128)} %param.11) | copy-start | bytes 98308
  0.0 5.2 %copy-start.1 = (bf16[4,1,2,19,16,256]{5,4,3,2,1,0:T(8,128)(2,1)S(1)}, bf16[4,1,2,19,16,256]{5,4,3,2,1,0:T(8,128)(2,1)}, u32[]{:S(2)}) copy-start(bf16[4,1,2,19,16,256]{5,4,3,2,1,0:T(8,128)(2,1)} %param.9) | copy-start | bytes 3735556
  0.0 5.2 %copy-start.2 = (f32[1,2,16,256]{3,2,1,0:T(8,128)S(1)}, f32[1,2,16,256]{3,2,1,0:T(8,128)}, u32[]{:S(2)}) copy-start(f32[1,2,16,256]{3,2,1,0:T(8,128)} %param.10) | copy-start | bytes 98308
  0.0 5.2 %copy-start.3 = (s32[1,2,16,256]{3,2,1,0:T(8,128)S(1)}, s32[1,2,16,256]{3,2,1,0:T(8,128)}, u32[]{:S(2)}) copy-start(s32[1,2,16,256]{3,2,1,0:T(8,128)} %param.12) | copy-start | bytes 98308
  3.3 2.8 %collective-permute-start.1 = (f32[128,256]{1,0:T(8,128)S(1)}, f32[128,256]{1,0:T(8,128)S(1)}, u32[]{:S(2)}, u32[]{:S(2)}) collective-permute-start(f32[128,256]{1,0:T(8,128)S(1)} %get-tuple-element.50), channel_id=1, source_target_pairs={{0,1},{1,0},{2,3},{3,2},{4,5},{5,4},{6,7},{7,6},{8,9},{9,8},{10,11... | collective-permute-start | bytes 393224 | tf_op jit(solution)/shard_map/exchange/ppermute | solution.py:50
  3.3 3.2 %collective-permute-start.2 = (f32[8,256]{1,0:T(8,128)S(1)}, f32[8,256]{1,0:T(8,128)S(1)}, u32[]{:S(2)}, u32[]{:S(2)}) collective-permute-start(f32[8,256]{1,0:T(8,128)S(1)} %get-tuple-element.56), channel_id=1, source_target_pairs={{0,3},{1,2},{2,1},{3,0},{4,7},{5,6},{6,5},{7,4},{8,11},{9,10},{10,... | collective-permute-start | bytes 24584 | tf_op jit(solution)/shard_map/exchange/ppermute | solution.py:55
  4.3 11.3 %collective-permute-start = (f32[40,256]{1,0:T(8,128)S(1)}, f32[40,256]{1,0:T(8,128)S(1)}, u32[]{:S(2)}, u32[]{:S(2)}) collective-permute-start(f32[40,256]{1,0:T(8,128)S(1)} %get-tuple-element.49), channel_id=1, source_target_pairs={{0,3},{1,2},{2,1},{3,0},{4,7},{5,6},{6,5},{7,4},{8,11},{9,10},{10,... | collective-permute-start | bytes 122888 | tf_op jit(solution)/shard_map/exchange/ppermute | solution.py:55
  6.5 11.7 %collective-permute-start.3 = (f32[56,256]{1,0:T(8,128)S(1)}, f32[56,256]{1,0:T(8,128)S(1)}, u32[]{:S(2)}, u32[]{:S(2)}) collective-permute-start(f32[56,256]{1,0:T(8,128)S(1)} %select_maximum_fusion.9), channel_id=1, source_target_pairs={{0,1},{1,0},{2,4},{3,5},{4,2},{5,3},{6,8},{7,9},{8,6},{9,7},{10,12... | collective-permute-start | bytes 172040 | tf_op jit(solution)/shard_map/exchange/ppermute | solution.py:67
  18.9 3.6 %collective-permute-start.5 = (f32[32,256]{1,0:T(8,128)S(1)}, f32[32,256]{1,0:T(8,128)S(1)}, u32[]{:S(2)}, u32[]{:S(2)}) collective-permute-start(f32[32,256]{1,0:T(8,128)S(1)} %pad_maximum_fusion.1.refs_1_), channel_id=1, source_target_pairs={{0,3},{1,2},{2,1},{3,0},{4,7},{5,6},{6,5},{7,4},{8,11},{9,10},{10,... | collective-permute-start | bytes 98312 | tf_op jit(solution)/shard_map/exchange/ppermute | solution.py:55
  19.0 3.5 %collective-permute-start.7 = (f32[16,256]{1,0:T(8,128)S(1)}, f32[16,256]{1,0:T(8,128)S(1)}, u32[]{:S(2)}, u32[]{:S(2)}) collective-permute-start(f32[16,256]{1,0:T(8,128)S(1)} %get-tuple-element.62.refs_4_), channel_id=1, source_target_pairs={{0,1},{1,0},{2,3},{3,2},{4,5},{5,4},{6,7},{7,6},{8,9},{9,8},{10,11... | collective-permute-start | bytes 49160 | tf_op jit(solution)/shard_map/exchange/ppermute | solution.py:50
  20.0 2.8 %collective-permute-start.6 = (f32[128,256]{1,0:T(8,128)S(1)}, f32[128,256]{1,0:T(8,128)S(1)}, u32[]{:S(2)}, u32[]{:S(2)}) collective-permute-start(f32[128,256]{1,0:T(8,128)S(1)} %get-tuple-element.63), channel_id=1, source_target_pairs={{0,1},{1,0},{2,3},{3,2},{4,5},{5,4},{6,7},{7,6},{8,9},{9,8},{10,11... | collective-permute-start | bytes 393224 | tf_op jit(solution)/shard_map/exchange/ppermute | solution.py:50
  22.9 10.4 %collective-permute-start.8 = (f32[56,256]{1,0:T(8,128)S(1)}, f32[56,256]{1,0:T(8,128)S(1)}, u32[]{:S(2)}, u32[]{:S(2)}) collective-permute-start(f32[56,256]{1,0:T(8,128)S(1)} %select_maximum_fusion.6), channel_id=1, source_target_pairs={{0,1},{1,0},{2,4},{3,5},{4,2},{5,3},{6,8},{7,9},{8,6},{9,7},{10,12... | collective-permute-start | bytes 172040 | tf_op jit(solution)/shard_map/exchange/ppermute | solution.py:67
  29.2 3.7 %collective-permute-start.4 = (f32[40,256]{1,0:T(8,128)S(1)}, f32[40,256]{1,0:T(8,128)S(1)}, u32[]{:S(2)}, u32[]{:S(2)}) collective-permute-start(f32[40,256]{1,0:T(8,128)S(1)} %get-tuple-element.60), channel_id=1, source_target_pairs={{0,3},{1,2},{2,1},{3,0},{4,7},{5,6},{6,5},{7,4},{8,11},{9,10},{10,... | collective-permute-start | bytes 122888 | tf_op jit(solution)/shard_map/exchange/ppermute | solution.py:55
  34.0 3.4 %collective-permute-start.10 = (f32[16,256]{1,0:T(8,128)S(1)}, f32[16,256]{1,0:T(8,128)S(1)}, u32[]{:S(2)}, u32[]{:S(2)}) collective-permute-start(f32[16,256]{1,0:T(8,128)S(1)} %select_maximum_fusion.14.refs_1_), channel_id=1, source_target_pairs={{0,3},{1,2},{2,1},{3,0},{4,7},{5,6},{6,5},{7,4},{8,11},{9,10},{10,... | collective-permute-start | bytes 49160 | tf_op jit(solution)/shard_map/exchange/ppermute | solution.py:55
  35.0 2.8 %collective-permute-start.11 = (f32[128,256]{1,0:T(8,128)S(1)}, f32[128,256]{1,0:T(8,128)S(1)}, u32[]{:S(2)}, u32[]{:S(2)}) collective-permute-start(f32[128,256]{1,0:T(8,128)S(1)} %get-tuple-element.74), channel_id=1, source_target_pairs={{0,1},{1,0},{2,3},{3,2},{4,5},{5,4},{6,7},{7,6},{8,9},{9,8},{10,11... | collective-permute-start | bytes 393224 | tf_op jit(solution)/shard_map/exchange/ppermute | solution.py:50
  37.8 8.7 %collective-permute-start.12 = (f32[56,256]{1,0:T(8,128)S(1)}, f32[56,256]{1,0:T(8,128)S(1)}, u32[]{:S(2)}, u32[]{:S(2)}) collective-permute-start(f32[56,256]{1,0:T(8,128)S(1)} %select_maximum_fusion.3), channel_id=1, source_target_pairs={{0,1},{1,0},{2,4},{3,5},{4,2},{5,3},{6,8},{7,9},{8,6},{9,7},{10,12... | collective-permute-start | bytes 172040 | tf_op jit(solution)/shard_map/exchange/ppermute | solution.py:67
  42.4 3.4 %collective-permute-start.9 = (f32[40,256]{1,0:T(8,128)S(1)}, f32[40,256]{1,0:T(8,128)S(1)}, u32[]{:S(2)}, u32[]{:S(2)}) collective-permute-start(f32[40,256]{1,0:T(8,128)S(1)} %get-tuple-element.71), channel_id=1, source_target_pairs={{0,3},{1,2},{2,1},{3,0},{4,7},{5,6},{6,5},{7,4},{8,11},{9,10},{10,... | collective-permute-start | bytes 122888 | tf_op jit(solution)/shard_map/exchange/ppermute | solution.py:55
  47.2 3.3 %collective-permute-start.14 = (f32[16,256]{1,0:T(8,128)S(1)}, f32[16,256]{1,0:T(8,128)S(1)}, u32[]{:S(2)}, u32[]{:S(2)}) collective-permute-start(f32[16,256]{1,0:T(8,128)S(1)} %select_maximum_fusion.12.refs_1_), channel_id=1, source_target_pairs={{0,3},{1,2},{2,1},{3,0},{4,7},{5,6},{6,5},{7,4},{8,11},{9,10},{10,... | collective-permute-start | bytes 49160 | tf_op jit(solution)/shard_map/exchange/ppermute | solution.py:55
  48.1 2.6 %collective-permute-start.15 = (f32[128,256]{1,0:T(8,128)S(1)}, f32[128,256]{1,0:T(8,128)S(1)}, u32[]{:S(2)}, u32[]{:S(2)}) collective-permute-start(f32[128,256]{1,0:T(8,128)S(1)} %get-tuple-element.83), channel_id=1, source_target_pairs={{0,1},{1,0},{2,3},{3,2},{4,5},{5,4},{6,7},{7,6},{8,9},{9,8},{10,11... | collective-permute-start | bytes 393224 | tf_op jit(solution)/shard_map/exchange/ppermute | solution.py:50
  50.8 8.5 %collective-permute-start.16 = (f32[56,256]{1,0:T(8,128)S(1)}, f32[56,256]{1,0:T(8,128)S(1)}, u32[]{:S(2)}, u32[]{:S(2)}) collective-permute-start(f32[56,256]{1,0:T(8,128)S(1)} %select_maximum_fusion), channel_id=1, source_target_pairs={{0,1},{1,0},{2,4},{3,5},{4,2},{5,3},{6,8},{7,9},{8,6},{9,7},{10,12... | collective-permute-start | bytes 172040 | tf_op jit(solution)/shard_map/exchange/ppermute | solution.py:67
  55.4 4.0 %collective-permute-start.13 = (f32[40,256]{1,0:T(8,128)S(1)}, f32[40,256]{1,0:T(8,128)S(1)}, u32[]{:S(2)}, u32[]{:S(2)}) collective-permute-start(f32[40,256]{1,0:T(8,128)S(1)} %get-tuple-element.80), channel_id=1, source_target_pairs={{0,3},{1,2},{2,1},{3,0},{4,7},{5,6},{6,5},{7,4},{8,11},{9,10},{10,... | collective-permute-start | bytes 122888 | tf_op jit(solution)/shard_map/exchange/ppermute | solution.py:55
  59.3 3.2 %collective-permute-start.17 = (f32[8,256]{1,0:T(8,128)S(1)}, f32[8,256]{1,0:T(8,128)S(1)}, u32[]{:S(2)}, u32[]{:S(2)}) collective-permute-start(f32[8,256]{1,0:T(8,128)S(1)} %pad.39), channel_id=1, source_target_pairs={{0,3},{1,2},{2,1},{3,0},{4,7},{5,6},{6,5},{7,4},{8,11},{9,10},{10,... | collective-permute-start | bytes 24584 | tf_op jit(solution)/shard_map/exchange/ppermute | solution.py:55

commit v4 on v3

--- a/solution.py
+++ b/solution.py
@@ -752,7 +752,7 @@
             (table, alpha, kept, mate, rest, *shares),
             half_scratch,
             "before",
-            estimate=cost(4_000_000, 2_000_000),
+            estimate=cost(40_000_000_000, 2_000_000),
         )[0]
         ins = [table, before, kept, u, keep, gain, bits, rest, far]
         if not last:

time: 63.5 us -> 61.5 us (0.969); the launches traced: 63.6 us -> 60.4 us
  waiting for transfers between devices: 21.8 us -> 13 us
  starting transfers between devices: 27 us -> 32.6 us
    ppermute x9, waiting for transfers between devices: 15.7 us -> 5.4 us  [mate_swap(): return lax.ppermute(value, axes, pairs)]
    ppermute x9, starting transfers between devices: 2.21 us -> 6.13 us  [mate_swap(): return lax.ppermute(value, axes, pairs)]
    ppermute x4, starting transfers between devices: 24.5 us -> 26.2 us  [far_swap(): return lax.ppermute(value, axes, pairs)]
    ppermute x4, waiting for transfers between devices: 6.04 us -> 7.58 us  [far_swap(): return lax.ppermute(value, axes, pairs)]
  transfers between devices with their start and end apart: 18 -> 18, of which waited for: 10 -> 10; matrix products, arithmetic and copies ran while one was open for 0% -> 0% of each run, Pallas kernels for 12% -> 13%
where the time goes in v4:
time: 61.5 us; the launch traced here: 60.4 us
  starting transfers between devices  32.6 us (53%)
  waiting for transfers between devices  13 us (21%)
  Pallas kernels  12 us (20%)
  other arithmetic  2.21 us (4%)
    ppermute x4, starting transfers between devices, far_swap(): return lax.ppermute(value, axes, pairs)  26.2 us
    pallas_call x20, Pallas kernels, call(): pl.pallas_call(kernel, out_shape=outs, in_specs=[vmem()] * len(ins), out_...  12 us
    ppermute x4, waiting for transfers between devices, far_swap(): return lax.ppermute(value, axes, pairs)  7.58 us
    ppermute x9, starting transfers between devices, mate_swap(): return lax.ppermute(value, axes, pairs)  6.13 us
    ppermute x9, waiting for transfers between devices, mate_swap(): return lax.ppermute(value, axes, pairs)  5.4 us
  transfers between devices with their start and end apart: 18, of which 10 were waited for; matrix products, arithmetic and copies ran while one was open for 0% of the time, Pallas kernels for 13%

profile of v4, /device:TPU:6, one launch (start us, length us, event | category | flops | bytes accessed | tf_op | source)
XLA Modules:
  0.0 60.4 jit_solution(297958978236396844)
XLA Ops:
  0.0 0.9 %add_convert_fusion = f32[2,12]{1,0:T(2,128)S(1)} fusion(s32[2,2]{1,0:T(2,128)} %bitcast.35, s32[2,2]{1,0:T(2,128)} %param.14, s32[2,8]{1,0:T(2,128)} %param.15), kind=kLoop, calls=%fused_computation.47 | loop fusion | flops 72 | bytes 192 | tf_op jit(solution)/shard_map/convert_element_type | solution.py:701
  0.9 1.1 %pad_maximum_fusion.refs_0_.refs_1_ = f32[41,16,256]{2,1,0:T(8,128)S(1)} fusion(f32[1,16,256]{2,1,0:T(8,128)S(1)} %pad_bitcast_fusion, f32[2,16,256]{2,1,0:T(8,128)} %bitcast.20, f32[38,16,256]{2,1,0:T(8,128)} %bitcast.34), kind=kLoop, calls=%fused_computation | loop fusion | flops 335872 | bytes 1343488 | tf_op jit(solution)/shard_map/concatenate | solution.py:703
  2.1 1.2 %pack_first.1 = (s32[8,128]{1,0:T(8,128)S(1)}, f32[40,256]{1,0:T(8,128)S(1)}, f32[8,256]{1,0:T(8,128)S(1)}, f32[128,256]{1,0:T(8,128)S(1)}, f32[32,256]{1,0:T(8,128)S(1)}, /*index=5*/f32[2,16,256]{2,1,0:T(8,128)S(1)}) custom-call(f32[41,16,256]{2,1,0:T(8,128)S(1)} %pad_maximum_fusion.refs_0_.refs_1_), custom_call_target="tpu_custom_call" | custom-call | tf_op jit(solution)/shard_map/pack_first/pallas_call | solution.py:680
  3.3 1.7 %collective-permute-start.2 = (f32[8,256]{1,0:T(8,128)S(1)}, f32[8,256]{1,0:T(8,128)S(1)}, u32[]{:S(2)}, u32[]{:S(2)}) collective-permute-start(f32[8,256]{1,0:T(8,128)S(1)} %get-tuple-element.56), channel_id=1, source_target_pairs={{0,3},{1,2},{2,1},{3,0},{4,7},{5,6},{6,5},{7,4},{8,11},{9,10},{10,... | collective-permute-start | bytes 24584 | tf_op jit(solution)/shard_map/exchange/ppermute | solution.py:55
  5.2 0.9 %flow_fields.1 = (f32[4,2,3,16,256]{4,3,2,1,0:T(8,128)S(1)}, f32[2,16,256]{2,1,0:T(8,128)S(1)}, f32[2,16,256]{2,1,0:T(8,128)S(1)}, s32[2,16,256]{2,1,0:T(8,128)S...) custom-call(s32[8,128]{1,0:T(8,128)S(1)} %get-tuple-element.47.refs_, ...), custom_call_target="tpu_custom_call" | custom-call | flops 4000000 | bytes 2000000 | tf_op jit(solution)/shard_map/flow_fields/pallas_call | solution.py:680
  6.5 8.4 %collective-permute-start.3 = (f32[56,256]{1,0:T(8,128)S(1)}, f32[56,256]{1,0:T(8,128)S(1)}, u32[]{:S(2)}, u32[]{:S(2)}) collective-permute-start(f32[56,256]{1,0:T(8,128)S(1)} %select_maximum_fusion.9), channel_id=1, source_target_pairs={{0,1},{1,0},{2,4},{3,5},{4,2},{5,3},{6,8},{7,9},{8,6},{9,7},{10,12... | collective-permute-start | bytes 172040 | tf_op jit(solution)/shard_map/exchange/ppermute | solution.py:67
  15.2 2.0 %collective-permute-done.3.refs_8_ = f32[56,256]{1,0:T(8,128)S(1)} collective-permute-done((f32[56,256]{1,0:T(8,128)S(1)}, f32[56,256]{1,0:T(8,128)S(1)}, u32[]{:S(2)}, u32[]{:S(2)}) %collective-permute-start.3) | collective-permute-done | bytes 57376 | tf_op jit(solution)/shard_map/exchange/ppermute | solution.py:67
  17.3 0.7 %step.4 = (f32[38,16,256]{2,1,0:T(8,128)S(1)}, f32[8,256]{1,0:T(8,128)S(1)}) custom-call(s32[8,128]{1,0:T(8,128)S(1)} %get-tuple-element.47.refs_0_.d_ref, f32[38,16,256]{2,1,0:T(8,128)S(1)} %before.4.refs_1_, f32[2,16,256]{2,1,0:T(8,128)S(1)} %get-tuple-element.48.refs_2_.refs_5_.refs_3_, f32[2,3,16,256]{3,2,1,0:T(8,128)S(1)} %get-tuple-element.92.refs_3_, ...), custom_call_target="tpu_custom_call" | custom-call | flops 8000000 | bytes 2000000 | tf_op jit(solution)/shard_map/step/pallas_call | solution.py:680
  18.2 0.9 %pack.3 = (f32[40,256]{1,0:T(8,128)S(1)}, f32[128,256]{1,0:T(8,128)S(1)}, f32[32,256]{1,0:T(8,128)S(1)}) custom-call(s32[8,128]{1,0:T(8,128)S(1)} %get-tuple-element.47.refs_0_.d_ref, f32[38,16,256]{2,1,0:T(8,128)S(1)} %get-tuple-element.58.refs_1_, f32[2,16,256]{2,1,0:T(8,128)S(1)} %bitcast.23, f32[2,16,256]{2,1,0:T(8,128)S(1)} %get-tuple-element.48.refs_2_.refs_5_.refs_3_, ...), custom_call_target="tpu_custom_call" | custom-call | flops 8000000 | bytes 2000000 | tf_op jit(solution)/shard_map/pack/pallas_call | solution.py:680
  19.2 2.1 %collective-permute-start.4 = (f32[40,256]{1,0:T(8,128)S(1)}, f32[40,256]{1,0:T(8,128)S(1)}, u32[]{:S(2)}, u32[]{:S(2)}) collective-permute-start(f32[40,256]{1,0:T(8,128)S(1)} %get-tuple-element.60), channel_id=1, source_target_pairs={{0,3},{1,2},{2,1},{3,0},{4,7},{5,6},{6,5},{7,4},{8,11},{9,10},{10,... | collective-permute-start | bytes 122888 | tf_op jit(solution)/shard_map/exchange/ppermute | solution.py:55
  22.0 6.0 %collective-permute-start.8 = (f32[56,256]{1,0:T(8,128)S(1)}, f32[56,256]{1,0:T(8,128)S(1)}, u32[]{:S(2)}, u32[]{:S(2)}) collective-permute-start(f32[56,256]{1,0:T(8,128)S(1)} %select_maximum_fusion.6), channel_id=1, source_target_pairs={{0,1},{1,0},{2,4},{3,5},{4,2},{5,3},{6,8},{7,9},{8,6},{9,7},{10,12... | collective-permute-start | bytes 172040 | tf_op jit(solution)/shard_map/exchange/ppermute | solution.py:67
  28.7 1.7 %collective-permute-done.8.refs_8_ = f32[56,256]{1,0:T(8,128)S(1)} collective-permute-done((f32[56,256]{1,0:T(8,128)S(1)}, f32[56,256]{1,0:T(8,128)S(1)}, u32[]{:S(2)}, u32[]{:S(2)}) %collective-permute-start.8) | collective-permute-done | bytes 57376 | tf_op jit(solution)/shard_map/exchange/ppermute | solution.py:67
  31.3 0.9 %pack.4 = (f32[40,256]{1,0:T(8,128)S(1)}, f32[128,256]{1,0:T(8,128)S(1)}, f32[32,256]{1,0:T(8,128)S(1)}) custom-call(s32[8,128]{1,0:T(8,128)S(1)} %get-tuple-element.47.refs_0_.d_ref, f32[38,16,256]{2,1,0:T(8,128)S(1)} %get-tuple-element.70.refs_1_, f32[2,16,256]{2,1,0:T(8,128)S(1)} %bitcast.25, f32[2,16,256]{2,1,0:T(8,128)S(1)} %get-tuple-element.48.refs_2_.refs_5_.refs_3_, ...), custom_call_target="tpu_custom_call" | custom-call | flops 8000000 | bytes 2000000 | tf_op jit(solution)/shard_map/pack/pallas_call | solution.py:680
  32.2 1.9 %collective-permute-start.9 = (f32[40,256]{1,0:T(8,128)S(1)}, f32[40,256]{1,0:T(8,128)S(1)}, u32[]{:S(2)}, u32[]{:S(2)}) collective-permute-start(f32[40,256]{1,0:T(8,128)S(1)} %get-tuple-element.71), channel_id=1, source_target_pairs={{0,3},{1,2},{2,1},{3,0},{4,7},{5,6},{6,5},{7,4},{8,11},{9,10},{10,... | collective-permute-start | bytes 122888 | tf_op jit(solution)/shard_map/exchange/ppermute | solution.py:55
  34.8 5.9 %collective-permute-start.12 = (f32[56,256]{1,0:T(8,128)S(1)}, f32[56,256]{1,0:T(8,128)S(1)}, u32[]{:S(2)}, u32[]{:S(2)}) collective-permute-start(f32[56,256]{1,0:T(8,128)S(1)} %select_maximum_fusion.3), channel_id=1, source_target_pairs={{0,1},{1,0},{2,4},{3,5},{4,2},{5,3},{6,8},{7,9},{8,6},{9,7},{10,12... | collective-permute-start | bytes 172040 | tf_op jit(solution)/shard_map/exchange/ppermute | solution.py:67
  41.6 1.7 %collective-permute-done.12.refs_8_ = f32[56,256]{1,0:T(8,128)S(1)} collective-permute-done((f32[56,256]{1,0:T(8,128)S(1)}, f32[56,256]{1,0:T(8,128)S(1)}, u32[]{:S(2)}, u32[]{:S(2)}) %collective-permute-start.12) | collective-permute-done | bytes 57376 | tf_op jit(solution)/shard_map/exchange/ppermute | solution.py:67
  43.3 0.7 %step.6 = (f32[38,16,256]{2,1,0:T(8,128)S(1)}, f32[8,256]{1,0:T(8,128)S(1)}) custom-call(s32[8,128]{1,0:T(8,128)S(1)} %get-tuple-element.47.refs_0_.d_ref, f32[38,16,256]{2,1,0:T(8,128)S(1)} %before.6.refs_1_, f32[2,16,256]{2,1,0:T(8,128)S(1)} %get-tuple-element.48.refs_2_.refs_5_.refs_3_, f32[2,3,16,256]{3,2,1,0:T(8,128)S(1)} %get-tuple-element.90.refs_3_, ...), custom_call_target="tpu_custom_call" | custom-call | flops 8000000 | bytes 2000000 | tf_op jit(solution)/shard_map/step/pallas_call | solution.py:680
  44.1 0.9 %pack.5 = (f32[40,256]{1,0:T(8,128)S(1)}, f32[128,256]{1,0:T(8,128)S(1)}, f32[32,256]{1,0:T(8,128)S(1)}) custom-call(s32[8,128]{1,0:T(8,128)S(1)} %get-tuple-element.47.refs_0_.d_ref, f32[38,16,256]{2,1,0:T(8,128)S(1)} %get-tuple-element.79.refs_1_, f32[2,16,256]{2,1,0:T(8,128)S(1)} %bitcast.27, f32[2,16,256]{2,1,0:T(8,128)S(1)} %get-tuple-element.48.refs_2_.refs_5_.refs_3_, ...), custom_call_target="tpu_custom_call" | custom-call | flops 8000000 | bytes 2000000 | tf_op jit(solution)/shard_map/pack/pallas_call | solution.py:680
  45.0 2.3 %collective-permute-done.14.refs_0_ = f32[16,256]{1,0:T(8,128)S(1)} collective-permute-done((f32[16,256]{1,0:T(8,128)S(1)}, f32[16,256]{1,0:T(8,128)S(1)}, u32[]{:S(2)}, u32[]{:S(2)}) %collective-permute-start.14) | collective-permute-done | bytes 16416 | tf_op jit(solution)/shard_map/exchange/ppermute | solution.py:55
  47.7 5.9 %collective-permute-start.16 = (f32[56,256]{1,0:T(8,128)S(1)}, f32[56,256]{1,0:T(8,128)S(1)}, u32[]{:S(2)}, u32[]{:S(2)}) collective-permute-start(f32[56,256]{1,0:T(8,128)S(1)} %select_maximum_fusion), channel_id=1, source_target_pairs={{0,1},{1,0},{2,4},{3,5},{4,2},{5,3},{6,8},{7,9},{8,6},{9,7},{10,12... | collective-permute-start | bytes 172040 | tf_op jit(solution)/shard_map/exchange/ppermute | solution.py:67
  54.1 2.1 %collective-permute-done.16.refs_8_ = f32[56,256]{1,0:T(8,128)S(1)} collective-permute-done((f32[56,256]{1,0:T(8,128)S(1)}, f32[56,256]{1,0:T(8,128)S(1)}, u32[]{:S(2)}, u32[]{:S(2)}) %collective-permute-start.16) | collective-permute-done | bytes 57376 | tf_op jit(solution)/shard_map/exchange/ppermute | solution.py:67
  56.3 0.8 %collective-permute-done.13.refs_3_ = f32[40,256]{1,0:T(8,128)S(1)} collective-permute-done((f32[40,256]{1,0:T(8,128)S(1)}, f32[40,256]{1,0:T(8,128)S(1)}, u32[]{:S(2)}, u32[]{:S(2)}) %collective-permute-start.13) | collective-permute-done | bytes 40992 | tf_op jit(solution)/shard_map/exchange/ppermute | solution.py:55
  58.1 1.3 %collective-permute-done.17.late_ref = f32[8,256]{1,0:T(8,128)S(1)} collective-permute-done((f32[8,256]{1,0:T(8,128)S(1)}, f32[8,256]{1,0:T(8,128)S(1)}, u32[]{:S(2)}, u32[]{:S(2)}) %collective-permute-start.17) | collective-permute-done | bytes 8224 | tf_op jit(solution)/shard_map/exchange/ppermute | solution.py:55
  59.3 0.9 %finish.1 = f32[38,16,256]{2,1,0:T(8,128)} custom-call(s32[8,128]{1,0:T(8,128)S(1)} %get-tuple-element.47.refs_0_.d_ref, f32[38,16,256]{2,1,0:T(8,128)S(1)} %step.7.alpha_ref, f32[8,256]{1,0:T(8,128)S(1)} %collective-permute-done.17.late_ref, f32[2,3,16,256]{3,2,1,0:T(8,128)S(1)} %get-tuple-element.89.refs_3_.u_ref, ...), custom_call_target="tpu_custom_call" | custom-call | tf_op jit(solution)/shard_map/finish/pallas_call | solution.py:680
  (67 shorter events, 7.1 us)
Async XLA Ops:
  0.0 5.2 %copy-start = (f32[1,2,16,256]{3,2,1,0:T(8,128)S(1)}, f32[1,2,16,256]{3,2,1,0:T(8,128)}, u32[]{:S(2)}) copy-start(f32[1,2,16,256]{3,2,1,0:T(8,128)} %param.11) | copy-start | bytes 98308
  0.0 5.2 %copy-start.1 = (bf16[4,1,2,19,16,256]{5,4,3,2,1,0:T(8,128)(2,1)S(1)}, bf16[4,1,2,19,16,256]{5,4,3,2,1,0:T(8,128)(2,1)}, u32[]{:S(2)}) copy-start(bf16[4,1,2,19,16,256]{5,4,3,2,1,0:T(8,128)(2,1)} %param.9) | copy-start | bytes 3735556
  0.0 5.2 %copy-start.2 = (f32[1,2,16,256]{3,2,1,0:T(8,128)S(1)}, f32[1,2,16,256]{3,2,1,0:T(8,128)}, u32[]{:S(2)}) copy-start(f32[1,2,16,256]{3,2,1,0:T(8,128)} %param.10) | copy-start | bytes 98308
  0.0 5.2 %copy-start.3 = (s32[1,2,16,256]{3,2,1,0:T(8,128)S(1)}, s32[1,2,16,256]{3,2,1,0:T(8,128)}, u32[]{:S(2)}) copy-start(s32[1,2,16,256]{3,2,1,0:T(8,128)} %param.12) | copy-start | bytes 98308
  3.3 2.8 %collective-permute-start.1 = (f32[128,256]{1,0:T(8,128)S(1)}, f32[128,256]{1,0:T(8,128)S(1)}, u32[]{:S(2)}, u32[]{:S(2)}) collective-permute-start(f32[128,256]{1,0:T(8,128)S(1)} %get-tuple-element.50), channel_id=1, source_target_pairs={{0,1},{1,0},{2,3},{3,2},{4,5},{5,4},{6,7},{7,6},{8,9},{9,8},{10,11... | collective-permute-start | bytes 393224 | tf_op jit(solution)/shard_map/exchange/ppermute | solution.py:50
  3.3 3.2 %collective-permute-start.2 = (f32[8,256]{1,0:T(8,128)S(1)}, f32[8,256]{1,0:T(8,128)S(1)}, u32[]{:S(2)}, u32[]{:S(2)}) collective-permute-start(f32[8,256]{1,0:T(8,128)S(1)} %get-tuple-element.56), channel_id=1, source_target_pairs={{0,3},{1,2},{2,1},{3,0},{4,7},{5,6},{6,5},{7,4},{8,11},{9,10},{10,... | collective-permute-start | bytes 24584 | tf_op jit(solution)/shard_map/exchange/ppermute | solution.py:55
  5.0 9.9 %collective-permute-start = (f32[40,256]{1,0:T(8,128)S(1)}, f32[40,256]{1,0:T(8,128)S(1)}, u32[]{:S(2)}, u32[]{:S(2)}) collective-permute-start(f32[40,256]{1,0:T(8,128)S(1)} %get-tuple-element.49), channel_id=1, source_target_pairs={{0,3},{1,2},{2,1},{3,0},{4,7},{5,6},{6,5},{7,4},{8,11},{9,10},{10,... | collective-permute-start | bytes 122888 | tf_op jit(solution)/shard_map/exchange/ppermute | solution.py:55
  6.5 10.8 %collective-permute-start.3 = (f32[56,256]{1,0:T(8,128)S(1)}, f32[56,256]{1,0:T(8,128)S(1)}, u32[]{:S(2)}, u32[]{:S(2)}) collective-permute-start(f32[56,256]{1,0:T(8,128)S(1)} %select_maximum_fusion.9), channel_id=1, source_target_pairs={{0,1},{1,0},{2,4},{3,5},{4,2},{5,3},{6,8},{7,9},{8,6},{9,7},{10,12... | collective-permute-start | bytes 172040 | tf_op jit(solution)/shard_map/exchange/ppermute | solution.py:67
  18.0 3.6 %collective-permute-start.5 = (f32[32,256]{1,0:T(8,128)S(1)}, f32[32,256]{1,0:T(8,128)S(1)}, u32[]{:S(2)}, u32[]{:S(2)}) collective-permute-start(f32[32,256]{1,0:T(8,128)S(1)} %pad_maximum_fusion.1.refs_1_), channel_id=1, source_target_pairs={{0,3},{1,2},{2,1},{3,0},{4,7},{5,6},{6,5},{7,4},{8,11},{9,10},{10,... | collective-permute-start | bytes 98312 | tf_op jit(solution)/shard_map/exchange/ppermute | solution.py:55
  18.1 3.5 %collective-permute-start.7 = (f32[16,256]{1,0:T(8,128)S(1)}, f32[16,256]{1,0:T(8,128)S(1)}, u32[]{:S(2)}, u32[]{:S(2)}) collective-permute-start(f32[16,256]{1,0:T(8,128)S(1)} %get-tuple-element.62.refs_4_), channel_id=1, source_target_pairs={{0,1},{1,0},{2,3},{3,2},{4,5},{5,4},{6,7},{7,6},{8,9},{9,8},{10,11... | collective-permute-start | bytes 49160 | tf_op jit(solution)/shard_map/exchange/ppermute | solution.py:50
  19.1 2.8 %collective-permute-start.6 = (f32[128,256]{1,0:T(8,128)S(1)}, f32[128,256]{1,0:T(8,128)S(1)}, u32[]{:S(2)}, u32[]{:S(2)}) collective-permute-start(f32[128,256]{1,0:T(8,128)S(1)} %get-tuple-element.63), channel_id=1, source_target_pairs={{0,1},{1,0},{2,3},{3,2},{4,5},{5,4},{6,7},{7,6},{8,9},{9,8},{10,11... | collective-permute-start | bytes 393224 | tf_op jit(solution)/shard_map/exchange/ppermute | solution.py:50
  19.2 9.2 %collective-permute-start.4 = (f32[40,256]{1,0:T(8,128)S(1)}, f32[40,256]{1,0:T(8,128)S(1)}, u32[]{:S(2)}, u32[]{:S(2)}) collective-permute-start(f32[40,256]{1,0:T(8,128)S(1)} %get-tuple-element.60), channel_id=1, source_target_pairs={{0,3},{1,2},{2,1},{3,0},{4,7},{5,6},{6,5},{7,4},{8,11},{9,10},{10,... | collective-permute-start | bytes 122888 | tf_op jit(solution)/shard_map/exchange/ppermute | solution.py:55
  22.0 8.5 %collective-permute-start.8 = (f32[56,256]{1,0:T(8,128)S(1)}, f32[56,256]{1,0:T(8,128)S(1)}, u32[]{:S(2)}, u32[]{:S(2)}) collective-permute-start(f32[56,256]{1,0:T(8,128)S(1)} %select_maximum_fusion.6), channel_id=1, source_target_pairs={{0,1},{1,0},{2,4},{3,5},{4,2},{5,3},{6,8},{7,9},{8,6},{9,7},{10,12... | collective-permute-start | bytes 172040 | tf_op jit(solution)/shard_map/exchange/ppermute | solution.py:67
  31.2 3.3 %collective-permute-start.10 = (f32[16,256]{1,0:T(8,128)S(1)}, f32[16,256]{1,0:T(8,128)S(1)}, u32[]{:S(2)}, u32[]{:S(2)}) collective-permute-start(f32[16,256]{1,0:T(8,128)S(1)} %select_maximum_fusion.14.refs_1_), channel_id=1, source_target_pairs={{0,3},{1,2},{2,1},{3,0},{4,7},{5,6},{6,5},{7,4},{8,11},{9,10},{10,... | collective-permute-start | bytes 49160 | tf_op jit(solution)/shard_map/exchange/ppermute | solution.py:55
  32.1 2.6 %collective-permute-start.11 = (f32[128,256]{1,0:T(8,128)S(1)}, f32[128,256]{1,0:T(8,128)S(1)}, u32[]{:S(2)}, u32[]{:S(2)}) collective-permute-start(f32[128,256]{1,0:T(8,128)S(1)} %get-tuple-element.74), channel_id=1, source_target_pairs={{0,1},{1,0},{2,3},{3,2},{4,5},{5,4},{6,7},{7,6},{8,9},{9,8},{10,11... | collective-permute-start | bytes 393224 | tf_op jit(solution)/shard_map/exchange/ppermute | solution.py:50
  32.2 9.1 %collective-permute-start.9 = (f32[40,256]{1,0:T(8,128)S(1)}, f32[40,256]{1,0:T(8,128)S(1)}, u32[]{:S(2)}, u32[]{:S(2)}) collective-permute-start(f32[40,256]{1,0:T(8,128)S(1)} %get-tuple-element.71), channel_id=1, source_target_pairs={{0,3},{1,2},{2,1},{3,0},{4,7},{5,6},{6,5},{7,4},{8,11},{9,10},{10,... | collective-permute-start | bytes 122888 | tf_op jit(solution)/shard_map/exchange/ppermute | solution.py:55
  34.8 8.5 %collective-permute-start.12 = (f32[56,256]{1,0:T(8,128)S(1)}, f32[56,256]{1,0:T(8,128)S(1)}, u32[]{:S(2)}, u32[]{:S(2)}) collective-permute-start(f32[56,256]{1,0:T(8,128)S(1)} %select_maximum_fusion.3), channel_id=1, source_target_pairs={{0,1},{1,0},{2,4},{3,5},{4,2},{5,3},{6,8},{7,9},{8,6},{9,7},{10,12... | collective-permute-start | bytes 172040 | tf_op jit(solution)/shard_map/exchange/ppermute | solution.py:67
  44.0 3.3 %collective-permute-start.14 = (f32[16,256]{1,0:T(8,128)S(1)}, f32[16,256]{1,0:T(8,128)S(1)}, u32[]{:S(2)}, u32[]{:S(2)}) collective-permute-start(f32[16,256]{1,0:T(8,128)S(1)} %select_maximum_fusion.12.refs_1_), channel_id=1, source_target_pairs={{0,3},{1,2},{2,1},{3,0},{4,7},{5,6},{6,5},{7,4},{8,11},{9,10},{10,... | collective-permute-start | bytes 49160 | tf_op jit(solution)/shard_map/exchange/ppermute | solution.py:55
  45.0 2.6 %collective-permute-start.15 = (f32[128,256]{1,0:T(8,128)S(1)}, f32[128,256]{1,0:T(8,128)S(1)}, u32[]{:S(2)}, u32[]{:S(2)}) collective-permute-start(f32[128,256]{1,0:T(8,128)S(1)} %get-tuple-element.83), channel_id=1, source_target_pairs={{0,1},{1,0},{2,3},{3,2},{4,5},{5,4},{6,7},{7,6},{8,9},{9,8},{10,11... | collective-permute-start | bytes 393224 | tf_op jit(solution)/shard_map/exchange/ppermute | solution.py:50
  47.7 8.5 %collective-permute-start.16 = (f32[56,256]{1,0:T(8,128)S(1)}, f32[56,256]{1,0:T(8,128)S(1)}, u32[]{:S(2)}, u32[]{:S(2)}) collective-permute-start(f32[56,256]{1,0:T(8,128)S(1)} %select_maximum_fusion), channel_id=1, source_target_pairs={{0,1},{1,0},{2,4},{3,5},{4,2},{5,3},{6,8},{7,9},{8,6},{9,7},{10,12... | collective-permute-start | bytes 172040 | tf_op jit(solution)/shard_map/exchange/ppermute | solution.py:67
  53.6 3.5 %collective-permute-start.13 = (f32[40,256]{1,0:T(8,128)S(1)}, f32[40,256]{1,0:T(8,128)S(1)}, u32[]{:S(2)}, u32[]{:S(2)}) collective-permute-start(f32[40,256]{1,0:T(8,128)S(1)} %get-tuple-element.80), channel_id=1, source_target_pairs={{0,3},{1,2},{2,1},{3,0},{4,7},{5,6},{6,5},{7,4},{8,11},{9,10},{10,... | collective-permute-start | bytes 122888 | tf_op jit(solution)/shard_map/exchange/ppermute | solution.py:55
  56.2 3.2 %collective-permute-start.17 = (f32[8,256]{1,0:T(8,128)S(1)}, f32[8,256]{1,0:T(8,128)S(1)}, u32[]{:S(2)}, u32[]{:S(2)}) collective-permute-start(f32[8,256]{1,0:T(8,128)S(1)} %pad.39), channel_id=1, source_target_pairs={{0,3},{1,2},{2,1},{3,0},{4,7},{5,6},{6,5},{7,4},{8,11},{9,10},{10,... | collective-permute-start | bytes 24584 | tf_op jit(solution)/shard_map/exchange/ppermute | solution.py:55

commit v5 on v4

--- a/solution.py
+++ b/solution.py
@@ -811,7 +811,7 @@
             (late, planes, lvl, ends, own_late, pair_late, mate_late, fix_pick, fix_place),
             share_scratch,
             "shares",
-            estimate=cost(2_000_000, 500_000),
+            estimate=cost(40_000_000_000, 2_000_000),
         )
     return alpha.reshape(1, 2, pops, edge, plane)
 

time: 61.5 us -> 61.1 us (level)
  the two profiles are of different devices: /device:TPU:6 before, /device:TPU:2 now
where the time goes in v5:
time: 61.1 us; the launch traced here: 60.7 us
  starting transfers between devices  36.1 us (59%)
  Pallas kernels  12 us (20%)
  waiting for transfers between devices  9.76 us (16%)
  other arithmetic  2.21 us (4%)
    ppermute x4, starting transfers between devices, far_swap(): return lax.ppermute(value, axes, pairs)  28.1 us
    pallas_call x20, Pallas kernels, call(): pl.pallas_call(kernel, out_shape=outs, in_specs=[vmem()] * len(ins), out_...  12 us
    ppermute x9, starting transfers between devices, mate_swap(): return lax.ppermute(value, axes, pairs)  7.31 us
    ppermute x4, waiting for transfers between devices, far_swap(): return lax.ppermute(value, axes, pairs)  6.05 us
    ppermute x9, waiting for transfers between devices, mate_swap(): return lax.ppermute(value, axes, pairs)  3.69 us
  transfers between devices with their start and end apart: 18, of which 9 were waited for; matrix products, arithmetic and copies ran while one was open for 0% of the time, Pallas kernels for 14%

profile of v5, /device:TPU:2, one launch (start us, length us, event | category | flops | bytes accessed | tf_op | source)
XLA Modules:
  0.0 60.7 jit_solution(16720027286195316360)
XLA Ops:
  0.0 0.9 %add_convert_fusion = f32[2,12]{1,0:T(2,128)S(1)} fusion(s32[2,2]{1,0:T(2,128)} %bitcast.35, s32[2,2]{1,0:T(2,128)} %param.14, s32[2,8]{1,0:T(2,128)} %param.15), kind=kLoop, calls=%fused_computation.47 | loop fusion | flops 72 | bytes 192 | tf_op jit(solution)/shard_map/convert_element_type | solution.py:701
  0.9 1.1 %pad_maximum_fusion.refs_0_.refs_1_ = f32[41,16,256]{2,1,0:T(8,128)S(1)} fusion(f32[1,16,256]{2,1,0:T(8,128)S(1)} %pad_bitcast_fusion, f32[2,16,256]{2,1,0:T(8,128)} %bitcast.20, f32[38,16,256]{2,1,0:T(8,128)} %bitcast.34), kind=kLoop, calls=%fused_computation | loop fusion | flops 335872 | bytes 1343488 | tf_op jit(solution)/shard_map/concatenate | solution.py:703
  2.1 1.2 %pack_first.1 = (s32[8,128]{1,0:T(8,128)S(1)}, f32[40,256]{1,0:T(8,128)S(1)}, f32[8,256]{1,0:T(8,128)S(1)}, f32[128,256]{1,0:T(8,128)S(1)}, f32[32,256]{1,0:T(8,128)S(1)}, /*index=5*/f32[2,16,256]{2,1,0:T(8,128)S(1)}) custom-call(f32[41,16,256]{2,1,0:T(8,128)S(1)} %pad_maximum_fusion.refs_0_.refs_1_), custom_call_target="tpu_custom_call" | custom-call | tf_op jit(solution)/shard_map/pack_first/pallas_call | solution.py:680
  3.3 1.3 %collective-permute-start.2 = (f32[8,256]{1,0:T(8,128)S(1)}, f32[8,256]{1,0:T(8,128)S(1)}, u32[]{:S(2)}, u32[]{:S(2)}) collective-permute-start(f32[8,256]{1,0:T(8,128)S(1)} %get-tuple-element.56), channel_id=1, source_target_pairs={{0,3},{1,2},{2,1},{3,0},{4,7},{5,6},{6,5},{7,4},{8,11},{9,10},{10,... | collective-permute-start | bytes 24584 | tf_op jit(solution)/shard_map/exchange/ppermute | solution.py:55
  4.6 0.5 collective-permute-start
  5.2 0.9 %flow_fields.1 = (f32[4,2,3,16,256]{4,3,2,1,0:T(8,128)S(1)}, f32[2,16,256]{2,1,0:T(8,128)S(1)}, f32[2,16,256]{2,1,0:T(8,128)S(1)}, s32[2,16,256]{2,1,0:T(8,128)S...) custom-call(s32[8,128]{1,0:T(8,128)S(1)} %get-tuple-element.47.refs_, ...), custom_call_target="tpu_custom_call" | custom-call | flops 4000000 | bytes 2000000 | tf_op jit(solution)/shard_map/flow_fields/pallas_call | solution.py:680
  6.5 8.8 %collective-permute-start.3 = (f32[56,256]{1,0:T(8,128)S(1)}, f32[56,256]{1,0:T(8,128)S(1)}, u32[]{:S(2)}, u32[]{:S(2)}) collective-permute-start(f32[56,256]{1,0:T(8,128)S(1)} %select_maximum_fusion.9), channel_id=1, source_target_pairs={{0,1},{1,0},{2,4},{3,5},{4,2},{5,3},{6,8},{7,9},{8,6},{9,7},{10,12... | collective-permute-start | bytes 172040 | tf_op jit(solution)/shard_map/exchange/ppermute | solution.py:67
  15.8 2.0 %collective-permute-done.3.refs_8_ = f32[56,256]{1,0:T(8,128)S(1)} collective-permute-done((f32[56,256]{1,0:T(8,128)S(1)}, f32[56,256]{1,0:T(8,128)S(1)}, u32[]{:S(2)}, u32[]{:S(2)}) %collective-permute-start.3) | collective-permute-done | bytes 57376 | tf_op jit(solution)/shard_map/exchange/ppermute | solution.py:67
  17.8 0.5 step.4
  18.6 0.9 %pack.3 = (f32[40,256]{1,0:T(8,128)S(1)}, f32[128,256]{1,0:T(8,128)S(1)}, f32[32,256]{1,0:T(8,128)S(1)}) custom-call(s32[8,128]{1,0:T(8,128)S(1)} %get-tuple-element.47.refs_0_.d_ref, f32[38,16,256]{2,1,0:T(8,128)S(1)} %get-tuple-element.58.refs_1_, f32[2,16,256]{2,1,0:T(8,128)S(1)} %bitcast.23, f32[2,16,256]{2,1,0:T(8,128)S(1)} %get-tuple-element.48.refs_2_.refs_5_.refs_3_, ...), custom_call_target="tpu_custom_call" | custom-call | flops 8000000 | bytes 2000000 | tf_op jit(solution)/shard_map/pack/pallas_call | solution.py:680
  20.0 1.3 %collective-permute-start.4 = (f32[40,256]{1,0:T(8,128)S(1)}, f32[40,256]{1,0:T(8,128)S(1)}, u32[]{:S(2)}, u32[]{:S(2)}) collective-permute-start(f32[40,256]{1,0:T(8,128)S(1)} %get-tuple-element.60), channel_id=1, source_target_pairs={{0,3},{1,2},{2,1},{3,0},{4,7},{5,6},{6,5},{7,4},{8,11},{9,10},{10,... | collective-permute-start | bytes 122888 | tf_op jit(solution)/shard_map/exchange/ppermute | solution.py:55
  21.2 0.6 collective-permute-done.5.refs_0_
  22.2 6.3 %collective-permute-start.8 = (f32[56,256]{1,0:T(8,128)S(1)}, f32[56,256]{1,0:T(8,128)S(1)}, u32[]{:S(2)}, u32[]{:S(2)}) collective-permute-start(f32[56,256]{1,0:T(8,128)S(1)} %select_maximum_fusion.6), channel_id=1, source_target_pairs={{0,1},{1,0},{2,4},{3,5},{4,2},{5,3},{6,8},{7,9},{8,6},{9,7},{10,12... | collective-permute-start | bytes 172040 | tf_op jit(solution)/shard_map/exchange/ppermute | solution.py:67
  29.6 1.2 %collective-permute-done.8.refs_8_ = f32[56,256]{1,0:T(8,128)S(1)} collective-permute-done((f32[56,256]{1,0:T(8,128)S(1)}, f32[56,256]{1,0:T(8,128)S(1)}, u32[]{:S(2)}, u32[]{:S(2)}) %collective-permute-start.8) | collective-permute-done | bytes 57376 | tf_op jit(solution)/shard_map/exchange/ppermute | solution.py:67
  31.4 0.9 %pack.4 = (f32[40,256]{1,0:T(8,128)S(1)}, f32[128,256]{1,0:T(8,128)S(1)}, f32[32,256]{1,0:T(8,128)S(1)}) custom-call(s32[8,128]{1,0:T(8,128)S(1)} %get-tuple-element.47.refs_0_.d_ref, f32[38,16,256]{2,1,0:T(8,128)S(1)} %get-tuple-element.70.refs_1_, f32[2,16,256]{2,1,0:T(8,128)S(1)} %bitcast.25, f32[2,16,256]{2,1,0:T(8,128)S(1)} %get-tuple-element.48.refs_2_.refs_5_.refs_3_, ...), custom_call_target="tpu_custom_call" | custom-call | flops 8000000 | bytes 2000000 | tf_op jit(solution)/shard_map/pack/pallas_call | solution.py:680
  32.3 2.0 %collective-permute-start.9 = (f32[40,256]{1,0:T(8,128)S(1)}, f32[40,256]{1,0:T(8,128)S(1)}, u32[]{:S(2)}, u32[]{:S(2)}) collective-permute-start(f32[40,256]{1,0:T(8,128)S(1)} %get-tuple-element.71), channel_id=1, source_target_pairs={{0,3},{1,2},{2,1},{3,0},{4,7},{5,6},{6,5},{7,4},{8,11},{9,10},{10,... | collective-permute-start | bytes 122888 | tf_op jit(solution)/shard_map/exchange/ppermute | solution.py:55
  34.9 6.5 %collective-permute-start.12 = (f32[56,256]{1,0:T(8,128)S(1)}, f32[56,256]{1,0:T(8,128)S(1)}, u32[]{:S(2)}, u32[]{:S(2)}) collective-permute-start(f32[56,256]{1,0:T(8,128)S(1)} %select_maximum_fusion.3), channel_id=1, source_target_pairs={{0,1},{1,0},{2,4},{3,5},{4,2},{5,3},{6,8},{7,9},{8,6},{9,7},{10,12... | collective-permute-start | bytes 172040 | tf_op jit(solution)/shard_map/exchange/ppermute | solution.py:67
  42.4 1.2 %collective-permute-done.12.refs_8_ = f32[56,256]{1,0:T(8,128)S(1)} collective-permute-done((f32[56,256]{1,0:T(8,128)S(1)}, f32[56,256]{1,0:T(8,128)S(1)}, u32[]{:S(2)}, u32[]{:S(2)}) %collective-permute-start.12) | collective-permute-done | bytes 57376 | tf_op jit(solution)/shard_map/exchange/ppermute | solution.py:67
  44.2 0.9 %pack.5 = (f32[40,256]{1,0:T(8,128)S(1)}, f32[128,256]{1,0:T(8,128)S(1)}, f32[32,256]{1,0:T(8,128)S(1)}) custom-call(s32[8,128]{1,0:T(8,128)S(1)} %get-tuple-element.47.refs_0_.d_ref, f32[38,16,256]{2,1,0:T(8,128)S(1)} %get-tuple-element.79.refs_1_, f32[2,16,256]{2,1,0:T(8,128)S(1)} %bitcast.27, f32[2,16,256]{2,1,0:T(8,128)S(1)} %get-tuple-element.48.refs_2_.refs_5_.refs_3_, ...), custom_call_target="tpu_custom_call" | custom-call | flops 8000000 | bytes 2000000 | tf_op jit(solution)/shard_map/pack/pallas_call | solution.py:680
  45.1 1.8 %collective-permute-start.13 = (f32[40,256]{1,0:T(8,128)S(1)}, f32[40,256]{1,0:T(8,128)S(1)}, u32[]{:S(2)}, u32[]{:S(2)}) collective-permute-start(f32[40,256]{1,0:T(8,128)S(1)} %get-tuple-element.80), channel_id=1, source_target_pairs={{0,3},{1,2},{2,1},{3,0},{4,7},{5,6},{6,5},{7,4},{8,11},{9,10},{10,... | collective-permute-start | bytes 122888 | tf_op jit(solution)/shard_map/exchange/ppermute | solution.py:55
  47.8 6.5 %collective-permute-start.16 = (f32[56,256]{1,0:T(8,128)S(1)}, f32[56,256]{1,0:T(8,128)S(1)}, u32[]{:S(2)}, u32[]{:S(2)}) collective-permute-start(f32[56,256]{1,0:T(8,128)S(1)} %select_maximum_fusion), channel_id=1, source_target_pairs={{0,1},{1,0},{2,4},{3,5},{4,2},{5,3},{6,8},{7,9},{8,6},{9,7},{10,12... | collective-permute-start | bytes 172040 | tf_op jit(solution)/shard_map/exchange/ppermute | solution.py:67
  54.7 1.7 %collective-permute-done.16.refs_8_ = f32[56,256]{1,0:T(8,128)S(1)} collective-permute-done((f32[56,256]{1,0:T(8,128)S(1)}, f32[56,256]{1,0:T(8,128)S(1)}, u32[]{:S(2)}, u32[]{:S(2)}) %collective-permute-start.16) | collective-permute-done | bytes 57376 | tf_op jit(solution)/shard_map/exchange/ppermute | solution.py:67
  57.6 2.0 %collective-permute-done.17.late_ref = f32[8,256]{1,0:T(8,128)S(1)} collective-permute-done((f32[8,256]{1,0:T(8,128)S(1)}, f32[8,256]{1,0:T(8,128)S(1)}, u32[]{:S(2)}, u32[]{:S(2)}) %collective-permute-start.17) | collective-permute-done | bytes 8224 | tf_op jit(solution)/shard_map/exchange/ppermute | solution.py:55
  59.6 0.9 %finish.1 = f32[38,16,256]{2,1,0:T(8,128)} custom-call(s32[8,128]{1,0:T(8,128)S(1)} %get-tuple-element.47.refs_0_.d_ref, f32[38,16,256]{2,1,0:T(8,128)S(1)} %step.7.alpha_ref, f32[8,256]{1,0:T(8,128)S(1)} %collective-permute-done.17.late_ref, f32[2,3,16,256]{3,2,1,0:T(8,128)S(1)} %get-tuple-element.89.refs_3_.u_ref, ...), custom_call_target="tpu_custom_call" | custom-call | tf_op jit(solution)/shard_map/finish/pallas_call | solution.py:680
  (67 shorter events, 8.3 us)
Async XLA Ops:
  0.0 5.1 %copy-start = (f32[1,2,16,256]{3,2,1,0:T(8,128)S(1)}, f32[1,2,16,256]{3,2,1,0:T(8,128)}, u32[]{:S(2)}) copy-start(f32[1,2,16,256]{3,2,1,0:T(8,128)} %param.11) | copy-start | bytes 98308
  0.0 5.1 %copy-start.1 = (bf16[4,1,2,19,16,256]{5,4,3,2,1,0:T(8,128)(2,1)S(1)}, bf16[4,1,2,19,16,256]{5,4,3,2,1,0:T(8,128)(2,1)}, u32[]{:S(2)}) copy-start(bf16[4,1,2,19,16,256]{5,4,3,2,1,0:T(8,128)(2,1)} %param.9) | copy-start | bytes 3735556
  0.0 5.1 %copy-start.2 = (f32[1,2,16,256]{3,2,1,0:T(8,128)S(1)}, f32[1,2,16,256]{3,2,1,0:T(8,128)}, u32[]{:S(2)}) copy-start(f32[1,2,16,256]{3,2,1,0:T(8,128)} %param.10) | copy-start | bytes 98308
  0.0 5.1 %copy-start.3 = (s32[1,2,16,256]{3,2,1,0:T(8,128)S(1)}, s32[1,2,16,256]{3,2,1,0:T(8,128)}, u32[]{:S(2)}) copy-start(s32[1,2,16,256]{3,2,1,0:T(8,128)} %param.12) | copy-start | bytes 98308
  3.3 2.8 %collective-permute-start.1 = (f32[128,256]{1,0:T(8,128)S(1)}, f32[128,256]{1,0:T(8,128)S(1)}, u32[]{:S(2)}, u32[]{:S(2)}) collective-permute-start(f32[128,256]{1,0:T(8,128)S(1)} %get-tuple-element.50), channel_id=1, source_target_pairs={{0,1},{1,0},{2,3},{3,2},{4,5},{5,4},{6,7},{7,6},{8,9},{9,8},{10,11... | collective-permute-start | bytes 393224 | tf_op jit(solution)/shard_map/exchange/ppermute | solution.py:50
  3.3 3.2 %collective-permute-start.2 = (f32[8,256]{1,0:T(8,128)S(1)}, f32[8,256]{1,0:T(8,128)S(1)}, u32[]{:S(2)}, u32[]{:S(2)}) collective-permute-start(f32[8,256]{1,0:T(8,128)S(1)} %get-tuple-element.56), channel_id=1, source_target_pairs={{0,3},{1,2},{2,1},{3,0},{4,7},{5,6},{6,5},{7,4},{8,11},{9,10},{10,... | collective-permute-start | bytes 24584 | tf_op jit(solution)/shard_map/exchange/ppermute | solution.py:55
  4.6 10.6 %collective-permute-start = (f32[40,256]{1,0:T(8,128)S(1)}, f32[40,256]{1,0:T(8,128)S(1)}, u32[]{:S(2)}, u32[]{:S(2)}) collective-permute-start(f32[40,256]{1,0:T(8,128)S(1)} %get-tuple-element.49), channel_id=1, source_target_pairs={{0,3},{1,2},{2,1},{3,0},{4,7},{5,6},{6,5},{7,4},{8,11},{9,10},{10,... | collective-permute-start | bytes 122888 | tf_op jit(solution)/shard_map/exchange/ppermute | solution.py:55
  6.5 11.3 %collective-permute-start.3 = (f32[56,256]{1,0:T(8,128)S(1)}, f32[56,256]{1,0:T(8,128)S(1)}, u32[]{:S(2)}, u32[]{:S(2)}) collective-permute-start(f32[56,256]{1,0:T(8,128)S(1)} %select_maximum_fusion.9), channel_id=1, source_target_pairs={{0,1},{1,0},{2,4},{3,5},{4,2},{5,3},{6,8},{7,9},{8,6},{9,7},{10,12... | collective-permute-start | bytes 172040 | tf_op jit(solution)/shard_map/exchange/ppermute | solution.py:67
  18.3 3.5 %collective-permute-start.5 = (f32[32,256]{1,0:T(8,128)S(1)}, f32[32,256]{1,0:T(8,128)S(1)}, u32[]{:S(2)}, u32[]{:S(2)}) collective-permute-start(f32[32,256]{1,0:T(8,128)S(1)} %pad_maximum_fusion.1.refs_1_), channel_id=1, source_target_pairs={{0,3},{1,2},{2,1},{3,0},{4,7},{5,6},{6,5},{7,4},{8,11},{9,10},{10,... | collective-permute-start | bytes 98312 | tf_op jit(solution)/shard_map/exchange/ppermute | solution.py:55
  18.4 3.4 %collective-permute-start.7 = (f32[16,256]{1,0:T(8,128)S(1)}, f32[16,256]{1,0:T(8,128)S(1)}, u32[]{:S(2)}, u32[]{:S(2)}) collective-permute-start(f32[16,256]{1,0:T(8,128)S(1)} %get-tuple-element.62.refs_4_), channel_id=1, source_target_pairs={{0,1},{1,0},{2,3},{3,2},{4,5},{5,4},{6,7},{7,6},{8,9},{9,8},{10,11... | collective-permute-start | bytes 49160 | tf_op jit(solution)/shard_map/exchange/ppermute | solution.py:50
  19.5 2.7 %collective-permute-start.6 = (f32[128,256]{1,0:T(8,128)S(1)}, f32[128,256]{1,0:T(8,128)S(1)}, u32[]{:S(2)}, u32[]{:S(2)}) collective-permute-start(f32[128,256]{1,0:T(8,128)S(1)} %get-tuple-element.63), channel_id=1, source_target_pairs={{0,1},{1,0},{2,3},{3,2},{4,5},{5,4},{6,7},{7,6},{8,9},{9,8},{10,11... | collective-permute-start | bytes 393224 | tf_op jit(solution)/shard_map/exchange/ppermute | solution.py:50
  20.0 9.1 %collective-permute-start.4 = (f32[40,256]{1,0:T(8,128)S(1)}, f32[40,256]{1,0:T(8,128)S(1)}, u32[]{:S(2)}, u32[]{:S(2)}) collective-permute-start(f32[40,256]{1,0:T(8,128)S(1)} %get-tuple-element.60), channel_id=1, source_target_pairs={{0,3},{1,2},{2,1},{3,0},{4,7},{5,6},{6,5},{7,4},{8,11},{9,10},{10,... | collective-permute-start | bytes 122888 | tf_op jit(solution)/shard_map/exchange/ppermute | solution.py:55
  22.2 8.5 %collective-permute-start.8 = (f32[56,256]{1,0:T(8,128)S(1)}, f32[56,256]{1,0:T(8,128)S(1)}, u32[]{:S(2)}, u32[]{:S(2)}) collective-permute-start(f32[56,256]{1,0:T(8,128)S(1)} %select_maximum_fusion.6), channel_id=1, source_target_pairs={{0,1},{1,0},{2,4},{3,5},{4,2},{5,3},{6,8},{7,9},{8,6},{9,7},{10,12... | collective-permute-start | bytes 172040 | tf_op jit(solution)/shard_map/exchange/ppermute | solution.py:67
  31.3 3.3 %collective-permute-start.10 = (f32[16,256]{1,0:T(8,128)S(1)}, f32[16,256]{1,0:T(8,128)S(1)}, u32[]{:S(2)}, u32[]{:S(2)}) collective-permute-start(f32[16,256]{1,0:T(8,128)S(1)} %select_maximum_fusion.14.refs_1_), channel_id=1, source_target_pairs={{0,3},{1,2},{2,1},{3,0},{4,7},{5,6},{6,5},{7,4},{8,11},{9,10},{10,... | collective-permute-start | bytes 49160 | tf_op jit(solution)/shard_map/exchange/ppermute | solution.py:55
  32.2 2.6 %collective-permute-start.11 = (f32[128,256]{1,0:T(8,128)S(1)}, f32[128,256]{1,0:T(8,128)S(1)}, u32[]{:S(2)}, u32[]{:S(2)}) collective-permute-start(f32[128,256]{1,0:T(8,128)S(1)} %get-tuple-element.74), channel_id=1, source_target_pairs={{0,1},{1,0},{2,3},{3,2},{4,5},{5,4},{6,7},{7,6},{8,9},{9,8},{10,11... | collective-permute-start | bytes 393224 | tf_op jit(solution)/shard_map/exchange/ppermute | solution.py:50
  32.3 9.6 %collective-permute-start.9 = (f32[40,256]{1,0:T(8,128)S(1)}, f32[40,256]{1,0:T(8,128)S(1)}, u32[]{:S(2)}, u32[]{:S(2)}) collective-permute-start(f32[40,256]{1,0:T(8,128)S(1)} %get-tuple-element.71), channel_id=1, source_target_pairs={{0,3},{1,2},{2,1},{3,0},{4,7},{5,6},{6,5},{7,4},{8,11},{9,10},{10,... | collective-permute-start | bytes 122888 | tf_op jit(solution)/shard_map/exchange/ppermute | solution.py:55
  34.9 8.7 %collective-permute-start.12 = (f32[56,256]{1,0:T(8,128)S(1)}, f32[56,256]{1,0:T(8,128)S(1)}, u32[]{:S(2)}, u32[]{:S(2)}) collective-permute-start(f32[56,256]{1,0:T(8,128)S(1)} %select_maximum_fusion.3), channel_id=1, source_target_pairs={{0,1},{1,0},{2,4},{3,5},{4,2},{5,3},{6,8},{7,9},{8,6},{9,7},{10,12... | collective-permute-start | bytes 172040 | tf_op jit(solution)/shard_map/exchange/ppermute | solution.py:67
  44.1 3.3 %collective-permute-start.14 = (f32[16,256]{1,0:T(8,128)S(1)}, f32[16,256]{1,0:T(8,128)S(1)}, u32[]{:S(2)}, u32[]{:S(2)}) collective-permute-start(f32[16,256]{1,0:T(8,128)S(1)} %select_maximum_fusion.12.refs_1_), channel_id=1, source_target_pairs={{0,3},{1,2},{2,1},{3,0},{4,7},{5,6},{6,5},{7,4},{8,11},{9,10},{10,... | collective-permute-start | bytes 49160 | tf_op jit(solution)/shard_map/exchange/ppermute | solution.py:55
  45.1 2.6 %collective-permute-start.15 = (f32[128,256]{1,0:T(8,128)S(1)}, f32[128,256]{1,0:T(8,128)S(1)}, u32[]{:S(2)}, u32[]{:S(2)}) collective-permute-start(f32[128,256]{1,0:T(8,128)S(1)} %get-tuple-element.83), channel_id=1, source_target_pairs={{0,1},{1,0},{2,3},{3,2},{4,5},{5,4},{6,7},{7,6},{8,9},{9,8},{10,11... | collective-permute-start | bytes 393224 | tf_op jit(solution)/shard_map/exchange/ppermute | solution.py:50
  45.1 11.4 %collective-permute-start.13 = (f32[40,256]{1,0:T(8,128)S(1)}, f32[40,256]{1,0:T(8,128)S(1)}, u32[]{:S(2)}, u32[]{:S(2)}) collective-permute-start(f32[40,256]{1,0:T(8,128)S(1)} %get-tuple-element.80), channel_id=1, source_target_pairs={{0,3},{1,2},{2,1},{3,0},{4,7},{5,6},{6,5},{7,4},{8,11},{9,10},{10,... | collective-permute-start | bytes 122888 | tf_op jit(solution)/shard_map/exchange/ppermute | solution.py:55
  47.8 8.7 %collective-permute-start.16 = (f32[56,256]{1,0:T(8,128)S(1)}, f32[56,256]{1,0:T(8,128)S(1)}, u32[]{:S(2)}, u32[]{:S(2)}) collective-permute-start(f32[56,256]{1,0:T(8,128)S(1)} %select_maximum_fusion), channel_id=1, source_target_pairs={{0,1},{1,0},{2,4},{3,5},{4,2},{5,3},{6,8},{7,9},{8,6},{9,7},{10,12... | collective-permute-start | bytes 172040 | tf_op jit(solution)/shard_map/exchange/ppermute | solution.py:67
  56.5 3.2 %collective-permute-start.17 = (f32[8,256]{1,0:T(8,128)S(1)}, f32[8,256]{1,0:T(8,128)S(1)}, u32[]{:S(2)}, u32[]{:S(2)}) collective-permute-start(f32[8,256]{1,0:T(8,128)S(1)} %pad.39), channel_id=1, source_target_pairs={{0,3},{1,2},{2,1},{3,0},{4,7},{5,6},{6,5},{7,4},{8,11},{9,10},{10,... | collective-permute-start | bytes 24584 | tf_op jit(solution)/shard_map/exchange/ppermute | solution.py:55
